TPU v7x, 32 devices: a whole 2x2x4 slice. The times are simulated.
32 devices in a mesh: dp: 4 (over z), row: 2 (over x), col: 4 (over y, core).
Axes of the slice: x: 2, y: 2, z: 4, core: 2. Of those that a mesh axis runs over, the one named last changes fastest.
Arguments:
- tokens: bfloat16 [16, 1024, 1024], P(('dp', 'row'), None, 'col'), may hold values from -6 to 6
- segments: int32 [16, 1024], P(('dp', 'row')), may hold values from 0 to 2, as said below
- w_qkv: bfloat16 [1024, 3072], P('row', 'col'), may hold values from -0.1875 to 0.1875
- qv_bias: float32 [2048], P('col'), may hold values from -1.2 to 1.2
- w_out: bfloat16 [1024, 1024], P('col', 'row'), may hold values from -0.75 to 0.75
- out_bias: float32 [1024], P('col'), may hold values from -3 to 3
- gain_one: float32 [1024], P('col'), may hold values from 0.1 to 1.9
- shift_one: float32 [1024], P('col'), may hold values from -3 to 3
- w_in: bfloat16 [1024, 4096], P('row', 'col'), may hold values from -0.1875 to 0.1875
- in_bias: float32 [4096], P('col'), may hold values from -3 to 3
- w_down: bfloat16 [4096, 1024], P('col', 'row'), may hold values from -0.09375 to 0.09375
- down_bias: float32 [1024], P('col'), may hold values from -3 to 3
- gain_two: float32 [1024], P('col'), may hold values from 0.1 to 1.9
- shift_two: float32 [1024], P('col'), may hold values from -3 to 3
- cotangent: bfloat16 [16, 1024, 1024], P(('dp', 'row'), None, 'col'), may hold values from -6 to 6
Outputs:
- output: bfloat16 [16, 1024, 1024], P(('dp', 'row'), None, 'col')
- grad_tokens: bfloat16 [16, 1024, 1024], P(('dp', 'row'), None, 'col')
- grad_w_qkv: float32 [1024, 3072], P('row', 'col')
- grad_qv_bias: float32 [2048], P('col')
- grad_w_out: float32 [1024, 1024], P('col', 'row')
- grad_out_bias: float32 [1024], P('col')
- grad_gain_one: float32 [1024], P('col')
- grad_shift_one: float32 [1024], P('col')
- grad_w_in: float32 [1024, 4096], P('row', 'col')
- grad_in_bias: float32 [4096], P('col')
- grad_w_down: float32 [4096, 1024], P('col', 'row')
- grad_down_bias: float32 [1024], P('col')
- grad_gain_two: float32 [1024], P('col')
- grad_shift_two: float32 [1024], P('col')
Inputs may be any that keep to these rules, and one draw needn't show every extreme that they name: `segments`: each row is one packed sequence: 0 at its first position, never falling, rising by at most one from a position to the next; no document begins within 128 positions of position 512. Positions 1022 and 1023 each raise the number unless it is already 2; the number never exceeds 2, so all positions numbered 2 attend to one another as one block.
All inputs are finite; a program needn't handle non-finite values.
Results may differ from a plain program's by a relative error of at most 0.019.
Values may be sent and summed in bfloat16 or wider, within the bound.
No kernel may reach another device: no remote copies, remote signals or barrier semaphores. Data moves between devices by JAX's collectives and lax.ppermute only.
A program may use at most 192 MiB of HBM per device.

v0:
```python
import math

import jax
import jax.numpy as jnp
from jax import lax
from jax.sharding import PartitionSpec as P

HEAD_DIM = 64


epsilon = 1e-12
masked_score = -1000000000.0


def gather_features(values):
    return lax.all_gather(values, "col", axis=2, tiled=True)


def gather_grads(values):
    return lax.all_gather(values, "col", axis=2, tiled=True)


def scatter_forward(values):
    return lax.psum_scatter(values, "col", scatter_dimension=2, tiled=True)


def scatter_backward(values):
    return lax.psum_scatter(
        values.astype(jnp.bfloat16), "col", scatter_dimension=2, tiled=True
    ).astype(jnp.float32)


def normalize(values):
    width = values.shape[-1] * lax.axis_size("col")
    row_mean = lax.psum(jnp.sum(values, axis=-1), "col") / width
    centered = values - row_mean[..., None]
    row_var = lax.psum(jnp.sum(centered * centered, axis=-1), "col") / width
    inverse = lax.rsqrt(row_var + epsilon)[..., None]
    return ((values - row_mean[..., None]) * inverse, inverse)


def norm_back(grad_in, normed, inverse):
    width = normed.shape[-1] * lax.axis_size("col")
    grad_total, grad_proj = lax.psum(
        (jnp.sum(grad_in, axis=-1), jnp.sum(grad_in * normed, axis=-1)), "col"
    )
    return inverse * (
        grad_in - grad_total[..., None] / width - normed * grad_proj[..., None] / width
    )


def score_block(queries, key_rows, doc_mask):
    score_scale = 1.0 / math.sqrt(queries.shape[-1])
    scores = (
        jnp.einsum("qhd,khd->hqk", queries, key_rows, preferred_element_type=jnp.float32)
        * score_scale
    )
    return jnp.where(doc_mask[None], scores, masked_score)


def attend(packed):
    queries, key_value, doc_mask = packed
    scores = score_block(queries, key_value[:, :, 0], doc_mask)
    row_top = jnp.max(scores, axis=-1, keepdims=True)
    exponent = jnp.exp(scores - row_top)
    row_total = jnp.sum(exponent, axis=-1, keepdims=True)
    probs_low = (exponent / row_total).astype(jnp.bfloat16)
    mixed_heads = jnp.einsum(
        "hqk,khd->qhd", probs_low, key_value[:, :, 1], preferred_element_type=jnp.float32
    )
    log_total = (row_top + jnp.log(row_total))[..., 0]
    return (mixed_heads.astype(jnp.bfloat16).reshape(queries.shape[0], -1), log_total)


def attend_back(packed):
    queries, key_value, doc_mask, log_total, grad_mixed = packed
    score_scale = 1.0 / math.sqrt(queries.shape[-1])
    scores = score_block(queries, key_value[:, :, 0], doc_mask)
    probs = jnp.exp(scores - log_total[..., None])
    grad_heads = grad_mixed.reshape(queries.shape)
    grad_probs = jnp.einsum(
        "qhd,khd->hqk", grad_heads, key_value[:, :, 1], preferred_element_type=jnp.float32
    )
    inner_sum = jnp.sum(probs * grad_probs, axis=-1, keepdims=True)
    grad_scores = (probs * (grad_probs - inner_sum)).astype(jnp.bfloat16)
    grad_query = (
        jnp.einsum(
            "hqk,khd->qhd", grad_scores, key_value[:, :, 0], preferred_element_type=jnp.float32
        )
        * score_scale
    )
    grad_key = (
        jnp.einsum("hqk,qhd->khd", grad_scores, queries, preferred_element_type=jnp.float32)
        * score_scale
    )
    grad_value = jnp.einsum(
        "hqk,qhd->khd", probs.astype(jnp.bfloat16), grad_heads, preferred_element_type=jnp.float32
    )
    grad_stack = jnp.stack([grad_query, grad_key, grad_value], axis=2)
    return grad_stack.astype(jnp.bfloat16).reshape(queries.shape[0], -1)


def split_pack(packed, lengths):
    pieces = []
    offset = 0
    for length in lengths:
        pieces.append(packed[offset : offset + length])
        offset = offset + length
    return pieces


def body(
    tokens,
    segments,
    w_qkv,
    qv_bias,
    w_out,
    out_bias,
    gain_one,
    shift_one,
    w_in,
    in_bias,
    w_down,
    down_bias,
    gain_two,
    shift_two,
    cotangent,
):
    seq_count, seq_len, local_width = tokens.shape
    local_heads = qv_bias.shape[0] // (2 * HEAD_DIM)
    full_qkv, full_out, full_in, full_down = (
        lax.all_gather(w_qkv, "row", axis=0, tiled=True),
        lax.all_gather(w_out, "row", axis=1, tiled=True),
        lax.all_gather(w_in, "row", axis=0, tiled=True),
        lax.all_gather(w_down, "row", axis=1, tiled=True),
    )
    doc_mask = segments[:, :, None] == segments[:, None, :]
    tokens_wide = gather_features(tokens)
    qv_pairs = qv_bias.reshape(local_heads, 2, HEAD_DIM)
    bias_full = jnp.stack(
        [qv_pairs[:, 0], jnp.zeros_like(qv_pairs[:, 0]), qv_pairs[:, 1]], axis=1
    ).reshape(-1)
    projected = (
        jnp.einsum("sqd,df->sqf", tokens_wide, full_qkv, preferred_element_type=jnp.float32)
        + bias_full
    ).astype(jnp.bfloat16)
    qkv_grid = projected.reshape(seq_count, seq_len, local_heads, 3, HEAD_DIM)
    queries = qkv_grid[:, :, :, 0]
    key_value = qkv_grid[:, :, :, 1:]
    mixed_heads, log_total = lax.map(attend, (queries, key_value, doc_mask))
    attention = (
        scatter_forward(
            jnp.einsum("sqh,hd->sqd", mixed_heads, full_out, preferred_element_type=jnp.float32)
        )
        + out_bias
    )
    normed_one, inverse_one = normalize(tokens.astype(jnp.float32) + attention)
    first_out = normed_one * gain_one + shift_one
    first_wide = gather_features(first_out.astype(jnp.bfloat16))
    hidden_pre = (
        jnp.einsum("sqd,df->sqf", first_wide, full_in, preferred_element_type=jnp.float32) + in_bias
    )
    gauss_cdf = 0.5 * (1.0 + lax.erf(hidden_pre * (1.0 / math.sqrt(2.0))))
    hidden_act = (hidden_pre * gauss_cdf).astype(jnp.bfloat16)
    ffn_out = (
        scatter_forward(
            jnp.einsum("sqf,fd->sqd", hidden_act, full_down, preferred_element_type=jnp.float32)
        )
        + down_bias
    )
    normed_two, inverse_two = normalize(first_out + ffn_out)
    output = (normed_two * gain_two + shift_two).astype(jnp.bfloat16)
    grad_out = cotangent.astype(jnp.float32)
    grad_gain_two = jnp.sum(grad_out * normed_two, axis=(0, 1))
    grad_shift_two = jnp.sum(grad_out, axis=(0, 1))
    grad_pre_two = norm_back(grad_out * gain_two, normed_two, inverse_two)
    grad_ffn = grad_pre_two.astype(jnp.bfloat16)
    grad_down_bias = jnp.sum(grad_ffn, axis=(0, 1), dtype=jnp.float32)
    grad_ffn_wide = gather_grads(grad_ffn)
    grad_down_full = jnp.einsum(
        "sqf,sqd->fd", hidden_act, grad_ffn_wide, preferred_element_type=jnp.float32
    )
    grad_act = jnp.einsum(
        "sqd,fd->sqf", grad_ffn_wide, full_down, preferred_element_type=jnp.float32
    )
    gauss_pdf = jnp.exp(-0.5 * hidden_pre * hidden_pre) * (1.0 / math.sqrt(2.0 * math.pi))
    grad_hidden = (grad_act * (gauss_cdf + hidden_pre * gauss_pdf)).astype(jnp.bfloat16)
    grad_in_bias = jnp.sum(grad_hidden, axis=(0, 1), dtype=jnp.float32)
    grad_in_full = jnp.einsum(
        "sqd,sqf->df", first_wide, grad_hidden, preferred_element_type=jnp.float32
    )
    grad_normed = grad_pre_two + scatter_backward(
        jnp.einsum("sqf,df->sqd", grad_hidden, full_in, preferred_element_type=jnp.float32)
    )
    grad_gain_one = jnp.sum(grad_normed * normed_one, axis=(0, 1))
    grad_shift_one = jnp.sum(grad_normed, axis=(0, 1))
    grad_pre_one = norm_back(grad_normed * gain_one, normed_one, inverse_one)
    grad_attention = grad_pre_one.astype(jnp.bfloat16)
    grad_out_bias = jnp.sum(grad_attention, axis=(0, 1), dtype=jnp.float32)
    grad_attn_wide = gather_grads(grad_attention)
    grad_out_full = jnp.einsum(
        "sqh,sqd->hd", mixed_heads, grad_attn_wide, preferred_element_type=jnp.float32
    )
    grad_mixed = jnp.einsum(
        "sqd,hd->sqh", grad_attn_wide, full_out, preferred_element_type=jnp.float32
    ).astype(jnp.bfloat16)
    grad_projected = lax.map(attend_back, (queries, key_value, doc_mask, log_total, grad_mixed))
    bias_sums = jnp.sum(grad_projected, axis=(0, 1), dtype=jnp.float32).reshape(
        local_heads, 3, HEAD_DIM
    )
    grad_qv_bias = jnp.stack([bias_sums[:, 0], bias_sums[:, 2]], axis=1).reshape(-1)
    grad_qkv_full = jnp.einsum(
        "sqd,sqf->df", tokens_wide, grad_projected, preferred_element_type=jnp.float32
    )
    grad_tokens = (
        grad_pre_one
        + scatter_backward(
            jnp.einsum("sqf,df->sqd", grad_projected, full_qkv, preferred_element_type=jnp.float32)
        )
    ).astype(jnp.bfloat16)
    small_grads = jnp.concatenate(
        [
            grad_qv_bias,
            grad_out_bias,
            grad_gain_one,
            grad_shift_one,
            grad_in_bias,
            grad_down_bias,
            grad_gain_two,
            grad_shift_two,
        ]
    )
    paired_small = jnp.stack([small_grads, small_grads])
    rows_qkv, rows_out, rows_in, rows_down, rows_small = (
        lax.psum_scatter(
            grad_qkv_full.astype(jnp.bfloat16), "row", scatter_dimension=0, tiled=True
        ).astype(jnp.float32),
        lax.psum_scatter(
            grad_out_full.astype(jnp.bfloat16), "row", scatter_dimension=1, tiled=True
        ).astype(jnp.float32),
        lax.psum_scatter(
            grad_in_full.astype(jnp.bfloat16), "row", scatter_dimension=0, tiled=True
        ).astype(jnp.float32),
        lax.psum_scatter(
            grad_down_full.astype(jnp.bfloat16), "row", scatter_dimension=1, tiled=True
        ).astype(jnp.float32),
        lax.psum_scatter(
            paired_small.astype(jnp.bfloat16), "row", scatter_dimension=0, tiled=True
        ).astype(jnp.float32),
    )
    grad_w_qkv, grad_w_out, grad_w_in, grad_w_down, summed_pair = (
        lax.psum(rows_qkv.astype(jnp.bfloat16), "dp").astype(jnp.float32),
        lax.psum(rows_out.astype(jnp.bfloat16), "dp").astype(jnp.float32),
        lax.psum(rows_in.astype(jnp.bfloat16), "dp").astype(jnp.float32),
        lax.psum(rows_down.astype(jnp.bfloat16), "dp").astype(jnp.float32),
        lax.psum(rows_small.astype(jnp.bfloat16), "dp").astype(jnp.float32),
    )
    summed_small = summed_pair[0]
    lengths = [
        qv_bias.shape[0],
        out_bias.shape[0],
        gain_one.shape[0],
        shift_one.shape[0],
        in_bias.shape[0],
        down_bias.shape[0],
        gain_two.shape[0],
        shift_two.shape[0],
    ]
    g_qv, g_obias, g_gone, g_sone, g_ibias, g_dbias, g_gtwo, g_stwo = split_pack(
        summed_small, lengths
    )
    return (
        output,
        grad_tokens,
        grad_w_qkv,
        g_qv,
        grad_w_out,
        g_obias,
        g_gone,
        g_sone,
        grad_w_in,
        g_ibias,
        grad_w_down,
        g_dbias,
        g_gtwo,
        g_stwo,
    )


def solution(mesh):
    placed = (
        P(("dp", "row"), None, "col"),
        P(("dp", "row"), None),
        P("row", "col"),
        P("col"),
        P("col", "row"),
        P("col"),
        P("col"),
        P("col"),
        P("row", "col"),
        P("col"),
        P("col", "row"),
        P("col"),
        P("col"),
        P("col"),
        P(("dp", "row"), None, "col"),
    )
    return jax.shard_map(
        body,
        mesh=mesh,
        in_specs=placed,
        out_specs=(
            P(("dp", "row"), None, "col"),
            P(("dp", "row"), None, "col"),
            P("row", "col"),
            P("col"),
            P("col", "row"),
            P("col"),
            P("col"),
            P("col"),
            P("row", "col"),
            P("col"),
            P("col", "row"),
            P("col"),
            P("col"),
            P("col"),
        ),
        check_vma=False,
    )
```

profile of v0, /device:TPU:0, one launch (start us, length us, event | category | flops | bytes accessed | tf_op | source)
XLA Modules:
  0.0 901.6 jit_solution(3019049927173318943)
XLA Ops:
  10.8 10.0 %all_gather.26 = bf16[256,1024]{1,0:T(8,128)(2,1)} all-gather(bf16[256,512]{1,0:T(8,128)(2,1)S(1)} %copy-done.14), channel_id=1, replica_groups=mesh['dp'=4,'row'=2,'col'=4] {'row'}, dimensions={1}, use_global_device_ids=true | all-gather | bytes 786432 | tf_op jit(solution)/shard_map/all_gather | solution.py:133
  22.1 18.0 %all-gather.10.cloned.1.call-done = bf16[1024,768]{0,1:T(8,128)(2,1)} async-done(((bf16[512,768]{0,1:T(8,128)(2,1)}), bf16[1024,768]{0,1:T(8,128)(2,1)}) %all-gather.10.cloned.1.call-update) | async-done | bytes 1572880 | tf_op jit(solution)/shard_map/all_gather | solution.py:132
  40.1 36.6 %all-gather.8.cloned.1.call-done = bf16[2,1024,1024]{2,1,0:T(8,128)(2,1)} async-done(((bf16[2,1024,256]{2,1,0:T(8,128)(2,1)}), bf16[2,1024,1024]{2,1,0:T(8,128)(2,1)}) %all-gather.8.cloned.1.call-update) | async-done | bytes 4194320 | tf_op jit(solution)/shard_map/all_gather | solution.py:16
  76.7 6.1 add_convert_fusion
  84.6 28.5 %while.22 = (s32[]{:T(128)}, bf16[2,1024,256]{1,2,0:T(8,128)(2,1)}, f32[2,4,1024]{2,1,0:T(4,128)S(1)}, bf16[2,1024,4,2,64]{1,4,2,3,0:T(8,128)(2,1)}, pred[2,1024...) while((s32[]{:T(128)}, bf16[2,1024,256]{1,2,0:T(8,128)(2,1)}, ...), condition=%wide.region_3.4_spmd, body=%wide.region_0.3_spmd.sunk | while | flops 1124331520 | bytes 69337712 | solution.py:150
  93.0 5.0 fusion.100
  107.2 5.0 fusion.100
  113.1 6.6 fusion.55
  120.4 71.2 %reduce-scatter.9.cloned.1.call-done = f32[2,1024,256]{2,1,0:T(8,128)} async-done(((f32[2,1024,1024]{2,1,0:T(8,128)}), f32[2,1024,256]{2,1,0:T(8,128)}) %reduce-scatter.9.cloned.1.call-update) | async-done | bytes 2097168 | tf_op jit(solution)/shard_map/reduce_scatter | solution.py:24
  193.9 6.2 psum.91
  200.7 6.2 psum.92
  209.1 17.1 %all-gather.14.cloned.1.call-done = bf16[1024,1024]{1,0:T(8,128)(2,1)} async-done(((bf16[512,1024]{1,0:T(8,128)(2,1)}), bf16[1024,1024]{1,0:T(8,128)(2,1)}) %all-gather.14.cloned.1.call-update) | async-done | bytes 2097168 | tf_op jit(solution)/shard_map/all_gather | solution.py:134
  226.2 37.1 %all-gather.12.cloned.1.call-done = bf16[2,1024,1024]{2,1,0:T(8,128)(2,1)} async-done(((bf16[2,1024,256]{2,1,0:T(8,128)(2,1)}), bf16[2,1024,1024]{2,1,0:T(8,128)(2,1)}) %all-gather.12.cloned.1.call-update) | async-done | bytes 4194320 | tf_op jit(solution)/shard_map/all_gather | solution.py:16
  263.4 10.3 %multiply_convert_fusion.1 = (bf16[2,1024,1024]{2,1,0:T(8,128)(2,1)}, f32[2,1024,1024]{2,1,0:T(8,128)}) fusion(f32[1024]{0:T(1024)S(1)} %copy-done.38, bf16[2,1024,1024]{2,1,0:T(8,128)(2,1)} %all-gather.12.cloned.1.call-done, bf16[1024,1024]{1,0:T(8,128)(2,1)} %all-gather.14.cloned.1.call-done), kind=kOutput, calls=%fused_computation.55 | convolution fusion | flops 4307550208 | bytes 18878464 | tf_op jit(solution)/shard_map/sqd,df->sqf/dot_general | solution.py:161
  273.6 24.3 %all-gather.16.cloned.1.call-done = bf16[1024,1024]{1,0:T(8,128)(2,1)} async-done(((bf16[1024,512]{1,0:T(8,128)(2,1)}), bf16[1024,1024]{1,0:T(8,128)(2,1)}) %all-gather.16.cloned.1.call-update) | async-done | bytes 2097168 | tf_op jit(solution)/shard_map/all_gather | solution.py:135
  298.0 10.6 %fusion.43 = f32[2,1024,1024]{2,1,0:T(8,128)} fusion(bf16[2,1024,1024]{2,1,0:T(8,128)(2,1)} %get-tuple-element.216, bf16[1024,1024]{1,0:T(8,128)(2,1)} %all-gather.16.cloned.1.call-done), kind=kOutput, calls=%fused_computation.76 | convolution fusion | flops 4294967296 | bytes 14680064 | tf_op jit(solution)/shard_map/sqf,fd->sqd/dot_general | solution.py:167
  308.7 71.8 %reduce-scatter.11.cloned.1.call-done = f32[2,1024,256]{2,1,0:T(8,128)} async-done(((f32[2,1024,1024]{2,1,0:T(8,128)}), f32[2,1024,256]{2,1,0:T(8,128)}) %reduce-scatter.11.cloned.1.call-update) | async-done | bytes 2097168 | tf_op jit(solution)/shard_map/reduce_scatter | solution.py:24
  383.8 5.9 psum.93
  391.9 5.8 psum.94
  401.0 11.1 %all-reduce.2 = (f32[2,1024]{1,0:T(2,128)S(1)}, f32[2,1024]{1,0:T(2,128)S(1)}) all-reduce(f32[2,1024]{1,0:T(2,128)S(1)} %get-tuple-element.153, f32[2,1024]{1,0:T(2,128)S(1)} %get-tuple-element.156), channel_id=1, replica_groups=mesh['dp'=4,'row'=2,'col'=4] {'col'}, use_global_device_ids=true, to_apply=%region_17.18 | all-reduce | flops 4096 | bytes 32768 | tf_op jit(solution)/shard_map/psum | solution.py:44
  412.1 4.7 convert_reduce_fusion.3
  417.4 35.1 %all-gather.18.cloned.1.call-done = bf16[2,1024,1024]{2,1,0:T(8,128)(2,1)} async-done(((bf16[2,1024,256]{2,1,0:T(8,128)(2,1)}), bf16[2,1024,1024]{2,1,0:T(8,128)(2,1)}) %all-gather.18.cloned.1.call-update) | async-done | bytes 4194320 | tf_op jit(solution)/shard_map/all_gather | solution.py:20
  452.5 11.5 %convert_reduce_fusion = (f32[1024]{0:T(1024)}, bf16[2,1024,1024]{2,1,0:T(8,128)(2,1)S(1)}) fusion(f32[2,1024,1024]{2,1,0:T(8,128)} %get-tuple-element.217, f32[1024]{0:T(1024)S(1)} %copy-done.38, bf16[2,1024,1024]{2,1,0:T(8,128)(2,1)} %all-gather.18.cloned.1.call-done, bf16[1024,1024]{1,0:T(8,128)(2,1)} %all-gather.16.cloned.1.call-done), kind=kOutput, calls=%fused_computation.54 | convolution fusion | flops 4322229248 | bytes 18882560 | tf_op jit(solution)/shard_map/sqd,fd->sqf/dot_general | solution.py:183
  465.9 6.3 convolution_convert_fusion
  472.3 44.6 %reduce-scatter.13.cloned.1.call-done = bf16[2,1024,256]{2,1,0:T(8,128)(2,1)} async-done(((bf16[2,1024,1024]{2,1,0:T(8,128)(2,1)}), bf16[2,1024,256]{2,1,0:T(8,128)(2,1)}) %reduce-scatter.13.cloned.1.call-update) | async-done | bytes 1048592 | tf_op jit(solution)/shard_map/reduce_scatter | solution.py:28
  516.9 6.2 multiply_reduce_fusion.1
  523.1 10.1 %all-reduce.1 = (f32[2,1024]{1,0:T(2,128)S(1)}, f32[2,1024]{1,0:T(2,128)S(1)}) all-reduce(f32[2,1024]{1,0:T(2,128)S(1)} %get-tuple-element.151, f32[2,1024]{1,0:T(2,128)S(1)} %get-tuple-element.154), channel_id=1, replica_groups=mesh['dp'=4,'row'=2,'col'=4] {'col'}, use_global_device_ids=true, to_apply=%region_22.23 | all-reduce | flops 4096 | bytes 32768 | tf_op jit(solution)/shard_map/psum | solution.py:44
  533.3 4.6 convert_reduce_fusion.4
  538.0 9.4 %bitcast_convert_fusion = bf16[1024,1024]{1,0:T(8,128)(2,1)} fusion(bf16[2,1024,1024]{2,1,0:T(8,128)(2,1)} %get-tuple-element.216, bf16[2,1024,1024]{2,1,0:T(8,128)(2,1)} %all-gather.18.cloned.1.call-done), kind=kOutput, calls=%fused_computation.59 | convolution fusion | flops 4296015872 | bytes 10485760 | tf_op jit(solution)/shard_map/sqf,sqd->fd/dot_general | solution.py:180
  547.6 9.6 %bitcast_convert_fusion.1 = bf16[1024,1024]{1,0:T(8,128)(2,1)} fusion(bf16[2,1024,1024]{2,1,0:T(8,128)(2,1)} %all-gather.12.cloned.1.call-done, bf16[2,1024,1024]{2,1,0:T(8,128)(2,1)} %copy-done.40), kind=kOutput, calls=%fused_computation.60 | convolution fusion | flops 4296015872 | bytes 10485760 | tf_op jit(solution)/shard_map/sqd,sqf->df/dot_general | solution.py:189
  557.3 16.8 %all-gather.20.cloned.1.call-done = bf16[2,1024,1024]{2,1,0:T(8,128)(2,1)} async-done(((bf16[2,1024,256]{2,1,0:T(8,128)(2,1)}), bf16[2,1024,1024]{2,1,0:T(8,128)(2,1)}) %all-gather.20.cloned.1.call-update) | async-done | bytes 4194320 | tf_op jit(solution)/shard_map/all_gather | solution.py:20
  574.1 4.6 fusion.52
  583.2 101.8 %while.23 = (s32[]{:T(128)}, bf16[2,1024,768]{1,2,0:T(8,128)(2,1)}, bf16[2,1024,4,2,64]{1,4,2,3,0:T(8,128)(2,1)}, pred[2,1024,1024]{1,2,0:T(8,128)(4,1)}, bf16[2...) while((s32[]{:T(128)}, bf16[2,1024,768]{1,2,0:T(8,128)(2,1)}, ...), condition=%wide.region_25.26_spmd, body=%wide.region_23.25_spmd.sunk | while | flops 2724982784 | bytes 244400944 | solution.py:207
  585.0 8.1 fusion.107
  593.2 12.3 %multiply_reduce_fusion.7 = (f32[4,1024]{1,0:T(4,128)S(1)}, f32[4,1024,1024]{1,2,0:T(8,128)}) fusion(f32[4,1024,1024]{1,2,0:T(8,128)} %fusion.107, f32[4,1024]{1,0:T(4,128)S(1)} %dynamic-slice_bitcast_fusion.13, bf16[1024,4,2,64]{0,3,1,2:T(8,128)(2,1)S(1)} %dynamic-slice_bitcast_fusion.12, bf16[2,1024,4,64]{1,3,2,0:T(8,128)(2,1)S(1)} %get-tuple-element.349, ...), kind=kOutput, calls=%fused_computation.20.clone.1 | convolution fusion | flops 557838336 | bytes 35684356 | tf_op jit(solution)/shard_map/while/body/eval_jaxpr/qhd,khd->hqk/dot_general | solution.py:55
  605.5 12.1 %multiply_convert_fusion.3 = bf16[4,1024,1024]{1,2,0:T(8,128)(2,1)S(1)} fusion(f32[4,1024,1024]{1,2,0:T(8,128)} %get-tuple-element.306, f32[4,1024,1024]{1,2,0:T(8,128)} %fusion.107, f32[4,1024]{1,0:T(4,128)S(1)} %get-tuple-element.307), kind=kLoop, calls=%fused_computation.19.clone.1 | loop fusion | flops 12582912 | bytes 41959424 | tf_op jit(solution)/shard_map/while/body/eval_jaxpr/convert_element_type | solution.py:85
  623.4 6.6 fusion.109
  636.1 8.1 fusion.107
  644.3 12.3 %multiply_reduce_fusion.7 = (f32[4,1024]{1,0:T(4,128)S(1)}, f32[4,1024,1024]{1,2,0:T(8,128)}) fusion(f32[4,1024,1024]{1,2,0:T(8,128)} %fusion.107, f32[4,1024]{1,0:T(4,128)S(1)} %dynamic-slice_bitcast_fusion.13, bf16[1024,4,2,64]{0,3,1,2:T(8,128)(2,1)S(1)} %dynamic-slice_bitcast_fusion.12, bf16[2,1024,4,64]{1,3,2,0:T(8,128)(2,1)S(1)} %get-tuple-element.349, ...), kind=kOutput, calls=%fused_computation.20.clone.1 | convolution fusion | flops 557838336 | bytes 35684356 | tf_op jit(solution)/shard_map/while/body/eval_jaxpr/qhd,khd->hqk/dot_general | solution.py:55
  656.6 12.1 %multiply_convert_fusion.3 = bf16[4,1024,1024]{1,2,0:T(8,128)(2,1)S(1)} fusion(f32[4,1024,1024]{1,2,0:T(8,128)} %get-tuple-element.306, f32[4,1024,1024]{1,2,0:T(8,128)} %fusion.107, f32[4,1024]{1,0:T(4,128)S(1)} %get-tuple-element.307), kind=kLoop, calls=%fused_computation.19.clone.1 | loop fusion | flops 12582912 | bytes 41959424 | tf_op jit(solution)/shard_map/while/body/eval_jaxpr/convert_element_type | solution.py:85
  674.5 6.0 fusion.109
  685.0 7.7 fusion.51
  692.9 26.3 %reduce-scatter.17.cloned.1.call-done = bf16[512,768]{0,1:T(8,128)(2,1)} async-done(((bf16[1024,768]{0,1:T(8,128)(2,1)}), bf16[512,768]{0,1:T(8,128)(2,1)}) %reduce-scatter.17.cloned.1.call-update) | async-done | bytes 786448 | tf_op jit(solution)/shard_map/reduce_scatter | solution.py:235
  719.2 7.0 convolution_convert_fusion.1
  730.4 7.4 all-reduce
  738.4 20.4 %psum.100 = bf16[1,3072]{1,0:T(2,128)(2,1)S(1)} all-reduce(bf16[1,3072]{1,0:T(2,128)(2,1)S(1)} %constant_dynamic-slice_fusion.1), channel_id=1, replica_groups=mesh['dp'=4,'row'=2,'col'=4] {'dp'}, use_global_device_ids=true, to_apply=%region_38.39 | all-reduce | flops 3072 | bytes 12288 | tf_op jit(solution)/shard_map/psum | solution.py:256
  760.5 83.9 %all-reduce.6.cloned.1.call-done = (bf16[512,768]{0,1:T(8,128)(2,1)}, bf16[256,512]{1,0:T(8,128)(2,1)}, bf16[512,1024]{1,0:T(8,128)(2,1)}, bf16[1024,512]{1,0:T(8,128)(2,1)}) async-done(((bf16[512,768]{0,1:T(8,128)(2,1)}, bf16[256,512]{1,0:T(8,128)(2,1)}, bf16[512,1024]{1,0:T(8,128)(2,1)}, bf16[1024,512]{1,0:T(8,128)(2,1)}), (bf16[512,768]{0,1:T(8,128)(2,1)}, bf16[256,512]{1,0:T(8,128)(2,1)}, ...) | async-done | bytes 3145744 | tf_op jit(solution)/shard_map/psum | solution.py:252
  851.2 39.2 %reduce-scatter.15.cloned.1.call-done = bf16[2,1024,256]{2,1,0:T(8,128)(2,1)} async-done(((bf16[2,1024,1024]{2,1,0:T(8,128)(2,1)}), bf16[2,1024,256]{2,1,0:T(8,128)(2,1)}) %reduce-scatter.15.cloned.1.call-update) | async-done | bytes 1048592 | tf_op jit(solution)/shard_map/reduce_scatter | solution.py:28
  (228 shorter events, 88.2 us)
Async XLA Ops:
  7.2 13.5 %copy-start.18 = (s32[2,1024]{1,0:T(2,128)S(1)}, s32[2,1024]{1,0:T(2,128)}, u32[]{:S(2)}) copy-start(s32[2,1024]{1,0:T(2,128)} %param.20) | copy-start | bytes 24580
  7.2 32.9 %all-gather.10.cloned.1.call-start = ((), (), s32[]{:S(2)}) async-start(), calls=%async_computation.9 | async-start | bytes 2359296 | tf_op jit(solution)/shard_map/all_gather | solution.py:132
  9.6 67.1 %all-gather.8.cloned.1.call-start = ((), (), s32[]{:S(2)}) async-start(), calls=%async_computation.8 | async-start | bytes 5242880 | tf_op jit(solution)/shard_map/all_gather | solution.py:16
  10.4 181.2 %reduce-scatter.9.cloned.1.call-start = ((), (), s32[]{:S(2)}) async-start(), calls=%async_computation.10 | async-start | bytes 10485760 | tf_op jit(solution)/shard_map/reduce_scatter | solution.py:24
  113.1 6.6 copy-start.3
  119.7 71.9 %copy-start.35 = (f32[256]{0:T(256)S(1)}, f32[256]{0:T(256)}, u32[]{:S(2)}) copy-start(f32[256]{0:T(256)} %param.24) | copy-start | bytes 3076
  119.7 106.5 %all-gather.14.cloned.1.call-start = ((), (), s32[]{:S(2)}) async-start(), calls=%async_computation.12 | async-start | bytes 3145728 | tf_op jit(solution)/shard_map/all_gather | solution.py:134
  120.3 143.0 %all-gather.12.cloned.1.call-start = ((), (), s32[]{:S(2)}) async-start(), calls=%async_computation.11 | async-start | bytes 5242880 | tf_op jit(solution)/shard_map/all_gather | solution.py:16
  193.8 339.5 %copy-start.1 = (f32[2,1024,256]{2,1,0:T(8,128)}, f32[2,1024,256]{2,1,0:T(8,128)S(1)}, u32[]{:S(2)}) copy-start(f32[2,1024,256]{2,1,0:T(8,128)S(1)} %get-tuple-element.200) | copy-start | bytes 6291460
  193.8 13.1 %copy-start.21 = (f32[256]{0:T(256)S(1)}, f32[256]{0:T(256)}, u32[]{:S(2)}) copy-start(f32[256]{0:T(256)} %param.25) | copy-start | bytes 3076
  193.8 13.1 %copy-start.26 = (f32[256]{0:T(256)S(1)}, f32[256]{0:T(256)}, u32[]{:S(2)}) copy-start(f32[256]{0:T(256)} %param.26) | copy-start | bytes 3076
  200.1 333.2 %copy-start.10 = (f32[2,1024]{1,0:T(2,128)}, f32[2,1024]{1,0:T(2,128)S(1)}, u32[]{:S(2)}) copy-start(f32[2,1024]{1,0:T(2,128)S(1)} %broadcast_multiply_fusion.3) | copy-start | bytes 24580
  207.0 326.3 %copy-start.12 = (f32[2,1024]{1,0:T(2,128)}, f32[2,1024]{1,0:T(2,128)S(1)}, u32[]{:S(2)}) copy-start(f32[2,1024]{1,0:T(2,128)S(1)} %add_rsqrt_fusion.1) | copy-start | bytes 24580
  207.0 56.4 %copy-start.38 = (f32[1024]{0:T(1024)S(1)}, f32[1024]{0:T(1024)}, u32[]{:S(2)}) copy-start(f32[1024]{0:T(1024)} %param.28) | copy-start | bytes 12292
  208.5 89.4 %all-gather.16.cloned.1.call-start = ((), (), s32[]{:S(2)}) async-start(), calls=%async_computation.13 | async-start | bytes 3145728 | tf_op jit(solution)/shard_map/all_gather | solution.py:135
  209.1 171.4 %reduce-scatter.11.cloned.1.call-start = ((), (), s32[]{:S(2)}) async-start(), calls=%async_computation.14 | async-start | bytes 10485760 | tf_op jit(solution)/shard_map/reduce_scatter | solution.py:24
  308.6 71.9 %copy-start.33 = (f32[256]{0:T(256)S(1)}, f32[256]{0:T(256)}, u32[]{:S(2)}) copy-start(f32[256]{0:T(256)} %param.30) | copy-start | bytes 3076
  308.6 143.8 %all-gather.18.cloned.1.call-start = ((), (), s32[]{:S(2)}) async-start(), calls=%async_computation.15 | async-start | bytes 5242880 | tf_op jit(solution)/shard_map/all_gather | solution.py:20
  383.7 13.9 %copy-start.23 = (f32[256]{0:T(256)S(1)}, f32[256]{0:T(256)}, u32[]{:S(2)}) copy-start(f32[256]{0:T(256)} %param.31) | copy-start | bytes 3076
  416.9 100.0 %reduce-scatter.13.cloned.1.call-start = ((), (), s32[]{:S(2)}) async-start(), calls=%async_computation.16 | async-start | bytes 5242880 | tf_op jit(solution)/shard_map/reduce_scatter | solution.py:28
  452.5 13.4 %copy-start.36 = (bf16[1024,1024]{1,0:T(8,128)(2,1)S(1)}, bf16[1024,1024]{1,0:T(8,128)(2,1)}, u32[]{:S(2)}) copy-start(bf16[1024,1024]{1,0:T(8,128)(2,1)} %all-gather.14.cloned.1.call-done) | copy-start | bytes 6291460
  472.2 44.7 %copy-start.34 = (f32[256]{0:T(256)S(1)}, f32[256]{0:T(256)}, u32[]{:S(2)}) copy-start(f32[256]{0:T(256)} %param.32) | copy-start | bytes 3076
  472.2 101.9 %all-gather.20.cloned.1.call-start = ((), (), s32[]{:S(2)}) async-start(), calls=%async_computation.17 | async-start | bytes 5242880 | tf_op jit(solution)/shard_map/all_gather | solution.py:20
  533.3 4.6 copy-start.19
  537.9 154.9 %reduce-scatter.23.cloned.1.call-start = ((), (), s32[]{:S(2)}) async-start(), calls=%async_computation.22 | async-start | bytes 3145728 | tf_op jit(solution)/shard_map/reduce_scatter | solution.py:244
  547.4 145.5 %reduce-scatter.21.cloned.1.call-start = ((), (), s32[]{:S(2)}) async-start(), calls=%async_computation.21 | async-start | bytes 3145728 | tf_op jit(solution)/shard_map/reduce_scatter | solution.py:241
  557.2 135.7 %reduce-scatter.19.cloned.1.call-start = ((), (), s32[]{:S(2)}) async-start(), calls=%async_computation.20 | async-start | bytes 786432 | tf_op jit(solution)/shard_map/reduce_scatter | solution.py:238
  557.3 21.5 %copy-start.7 = (bf16[256,1024]{1,0:T(8,128)(2,1)S(1)}, bf16[256,1024]{1,0:T(8,128)(2,1)}, u32[]{:S(2)}) copy-start(bf16[256,1024]{1,0:T(8,128)(2,1)} %all_gather.26) | copy-start | bytes 1572868
  578.7 140.4 %reduce-scatter.17.cloned.1.call-start = ((), (), s32[]{:S(2)}) async-start(), calls=%async_computation.19 | async-start | bytes 2359296 | tf_op jit(solution)/shard_map/reduce_scatter | solution.py:235
  585.0 8.1 copy-start.4
  605.5 24.5 %slice-start = ((s8[16777216]{0:T(1024)(128)(4,1)}), s8[4194304]{0:T(1024)(128)(4,1)S(1)}, s32[]{:S(2)}) async-start(s8[16777216]{0:T(1024)(128)(4,1)} %bitcast.180), calls=%async_computation.24 | async-start | bytes 8388608 | tf_op jit(solution)/shard_map/while
  605.5 24.5 %slice-start.1 = ((s8[16777216]{0:T(1024)(128)(4,1)}), s8[4194304]{0:T(1024)(128)(4,1)S(1)}, s32[]{:S(2)}) async-start(s8[16777216]{0:T(1024)(128)(4,1)} %bitcast.180), calls=%async_computation.25 | async-start | bytes 8388608 | tf_op jit(solution)/shard_map/while
  605.5 24.5 %slice-start.2 = ((s8[16777216]{0:T(1024)(128)(4,1)}), s8[4194304]{0:T(1024)(128)(4,1)S(1)}, s32[]{:S(2)}) async-start(s8[16777216]{0:T(1024)(128)(4,1)} %bitcast.180), calls=%async_computation.26 | async-start | bytes 8388608 | tf_op jit(solution)/shard_map/while
  621.8 8.2 slice-start.3
  636.1 8.1 copy-start.4
  656.6 24.0 %slice-start = ((s8[16777216]{0:T(1024)(128)(4,1)}), s8[4194304]{0:T(1024)(128)(4,1)S(1)}, s32[]{:S(2)}) async-start(s8[16777216]{0:T(1024)(128)(4,1)} %bitcast.180), calls=%async_computation.24 | async-start | bytes 8388608 | tf_op jit(solution)/shard_map/while
  656.6 24.0 %slice-start.1 = ((s8[16777216]{0:T(1024)(128)(4,1)}), s8[4194304]{0:T(1024)(128)(4,1)S(1)}, s32[]{:S(2)}) async-start(s8[16777216]{0:T(1024)(128)(4,1)} %bitcast.180), calls=%async_computation.25 | async-start | bytes 8388608 | tf_op jit(solution)/shard_map/while
  656.6 24.0 %slice-start.2 = ((s8[16777216]{0:T(1024)(128)(4,1)}), s8[4194304]{0:T(1024)(128)(4,1)S(1)}, s32[]{:S(2)}) async-start(s8[16777216]{0:T(1024)(128)(4,1)} %bitcast.180), calls=%async_computation.26 | async-start | bytes 8388608 | tf_op jit(solution)/shard_map/while
  672.9 7.7 slice-start.3
  692.8 26.5 %copy-start.37 = (bf16[1024,768]{0,1:T(8,128)(2,1)S(1)}, bf16[1024,768]{0,1:T(8,128)(2,1)}, u32[]{:S(2)}) copy-start(bf16[1024,768]{0,1:T(8,128)(2,1)} %all-gather.10.cloned.1.call-done) | copy-start | bytes 4718596
  692.8 151.6 %all-reduce.6.cloned.1.call-start = ((), (), s32[]{:S(2)}) async-start(), calls=%async_computation.23 | async-start | bytes 6291456 | tf_op jit(solution)/shard_map/psum | solution.py:252
  719.2 171.3 %reduce-scatter.15.cloned.1.call-start = ((), (), s32[]{:S(2)}) async-start(), calls=%async_computation.18 | async-start | bytes 5242880 | tf_op jit(solution)/shard_map/reduce_scatter | solution.py:28
  848.9 41.5 %copy-start.2 = (f32[2,1024,256]{2,1,0:T(8,128)S(1)}, f32[2,1024,256]{2,1,0:T(8,128)}, u32[]{:S(2)}) copy-start(f32[2,1024,256]{2,1,0:T(8,128)} %copy-done.1) | copy-start | bytes 6291460
  848.9 41.5 %copy-start.11 = (f32[2,1024]{1,0:T(2,128)S(1)}, f32[2,1024]{1,0:T(2,128)}, u32[]{:S(2)}) copy-start(f32[2,1024]{1,0:T(2,128)} %copy-done.10) | copy-start | bytes 24580
  848.9 41.5 %copy-start.13 = (f32[2,1024]{1,0:T(2,128)S(1)}, f32[2,1024]{1,0:T(2,128)}, u32[]{:S(2)}) copy-start(f32[2,1024]{1,0:T(2,128)} %copy-done.12) | copy-start | bytes 24580
  848.9 41.5 %copy-start.17 = (f32[2,1024]{1,0:T(2,128)S(1)}, f32[2,1024]{1,0:T(2,128)}, u32[]{:S(2)}) copy-start(f32[2,1024]{1,0:T(2,128)} %copy-done.16) | copy-start | bytes 24580
  848.9 41.5 %copy-start.20 = (f32[2,1024]{1,0:T(2,128)S(1)}, f32[2,1024]{1,0:T(2,128)}, u32[]{:S(2)}) copy-start(f32[2,1024]{1,0:T(2,128)} %copy-done.19) | copy-start | bytes 24580
  848.9 41.5 %copy-start.22 = (f32[256]{0:T(256)S(1)}, f32[256]{0:T(256)}, u32[]{:S(2)}) copy-start(f32[256]{0:T(256)} %param.25) | copy-start | bytes 3076
  (21 other events, 63.4 us)
Sparse Core Ops, SparseCore 0:
  10.2 29.8 all-gather.9
  41.6 35.0 all-gather.7
  119.9 71.7 reduce-scatter.8
  193.1 33.1 all-gather.13
  228.3 35.0 all-gather.11
  264.8 33.1 all-gather.15
  308.7 71.7 reduce-scatter.10
  417.0 35.4 all-gather.17
  472.3 44.5 reduce-scatter.12
  538.0 36.0 all-gather.19
  576.5 31.8 reduce-scatter.22
  611.0 31.8 reduce-scatter.20
  645.8 14.5 reduce-scatter.18
  692.9 26.2 reduce-scatter.16
  721.8 122.5 all-reduce.5
  847.0 43.4 reduce-scatter.14
where the time goes:
time: 911 us; the launch traced here: 902 us
  waiting for transfers between devices  524 us (58%)
  matrix products  172 us (19%)
  blocking collectives  83 us (9%)
  other arithmetic  74 us (8%)
  local copies, waits for them, and re-layouts  31.6 us (3%)
  between operations  14.9 us (2%)
    reduce_scatter x2, waiting for transfers between devices, scatter_forward(): return lax.psum_scatter(values, 'col', scatter_dimension=2, tiled=True)  143 us
    psum x1, waiting for transfers between devices, body(): lax.psum(rows_qkv.astype(jnp.bfloat16), 'dp').astype(jnp.float32)  83.9 us
    reduce_scatter x2, waiting for transfers between devices, scatter_backward(): lax.psum_scatter(values.astype(jnp.bfloat16), 'col', scatter_dimension=2,...  83.9 us
    all_gather x2, waiting for transfers between devices, gather_features(): return lax.all_gather(values, 'col', axis=2, tiled=True)  73.7 us
    all_gather x2, waiting for transfers between devices, gather_grads(): return lax.all_gather(values, 'col', axis=2, tiled=True)  51.9 us
    dot_general x4, matrix products, score_block(): jnp.einsum('qhd,khd->hqk', queries, key_rows, preferred_element_type=jnp....  30.6 us
    reduce_scatter x1, waiting for transfers between devices, body(): lax.psum_scatter(grad_qkv_full.astype(jnp.bfloat16), 'row', scatter_dimen...  26.3 us
    all_gather x1, waiting for transfers between devices, body(): lax.all_gather(w_down, 'row', axis=1, tiled=True)  24.3 us
  transfers between devices with their start and end apart: 16, of which 13 were waited for; matrix products, arithmetic and copies ran while one was open for 18% of the time, Pallas kernels for 0%

commit v1 on v0

v1 whole, which is shorter than its diff:
```python
import functools
import math

import jax
import jax.numpy as jnp
from jax import lax
from jax.experimental import pallas as pl
from jax.experimental.pallas import tpu as pltpu
from jax.sharding import PartitionSpec as P

HEAD_DIM = 64
epsilon = 1e-12
f32 = jnp.float32
bf16 = jnp.bfloat16
NT = (((1,), (1,)), ((), ()))
NN = (((1,), (0,)), ((), ()))
TN = (((0,), (0,)), ((), ()))


def mm(left, right, dims=NN):
    return lax.dot_general(left, right, dims, preferred_element_type=f32)


def to_core(values):
    size = lax.axis_size("col")
    return lax.ppermute(values, "col", [(i, i ^ 1) for i in range(size)])


def to_chip(values):
    size = lax.axis_size("col")
    return lax.ppermute(values, "col", [(i, i ^ 2) for i in range(size)])


def to_row(values):
    return lax.ppermute(values, "row", [(0, 1), (1, 0)])


def attend_kernel(chunk, qkv_ref, mask_ref, exp_ref, mixed_ref, inv_ref):
    count = qkv_ref.shape[0]
    ones = jnp.ones((count, HEAD_DIM), bf16)
    for head in range(2):
        base = 3 * HEAD_DIM * head
        cols = slice(head * HEAD_DIM, (head + 1) * HEAD_DIM)
        query = qkv_ref[:, base : base + HEAD_DIM] * bf16(1.0 / math.sqrt(HEAD_DIM))
        key = qkv_ref[:, base + HEAD_DIM : base + 2 * HEAD_DIM]
        value = qkv_ref[:, base + 2 * HEAD_DIM : base + 3 * HEAD_DIM]
        query = jnp.concatenate([query, mask_ref[:, :HEAD_DIM]], axis=1)
        key = jnp.concatenate([key, mask_ref[:, HEAD_DIM:]], axis=1)
        value = jnp.concatenate([value, ones], axis=1)
        for start in range(0, count, chunk):
            rows = slice(start, start + chunk)
            scores = mm(query[rows], key, NT)
            top = jnp.max(scores, axis=-1, keepdims=True)
            exponent = jnp.exp(scores - top).astype(bf16)
            exp_ref[head, rows, :] = exponent
            mixed = mm(exponent, value)
            inverse = 1.0 / mixed[:, HEAD_DIM:]
            mixed_ref[rows, cols] = (mixed[:, :HEAD_DIM] * inverse).astype(bf16)
            inv_ref[rows, cols] = inverse


def attend(qkv, mask):
    count, width = qkv.shape
    pairs = width // (6 * HEAD_DIM)
    return pl.pallas_call(
        functools.partial(attend_kernel, min(512, count)),
        grid=(pairs,),
        in_specs=[
            pl.BlockSpec((count, 6 * HEAD_DIM), lambda p: (0, p)),
            pl.BlockSpec((count, 2 * HEAD_DIM), lambda p: (0, 0)),
        ],
        out_specs=[
            pl.BlockSpec((2, count, count), lambda p: (p, 0, 0)),
            pl.BlockSpec((count, 2 * HEAD_DIM), lambda p: (0, p)),
            pl.BlockSpec((count, 2 * HEAD_DIM), lambda p: (0, p)),
        ],
        out_shape=[
            jax.ShapeDtypeStruct((2 * pairs, count, count), bf16),
            jax.ShapeDtypeStruct((count, 2 * HEAD_DIM * pairs), bf16),
            jax.ShapeDtypeStruct((count, 2 * HEAD_DIM * pairs), f32),
        ],
        compiler_params=pltpu.CompilerParams(vmem_limit_bytes=48 * 2**20),
        cost_estimate=pl.CostEstimate(
            flops=32 * pairs * count * count * HEAD_DIM,
            bytes_accessed=4 * pairs * count * count,
            transcendentals=2 * pairs * count * count,
        ),
        name="attend",
    )(qkv, mask)


def attend_back_kernel(chunk, qkv_ref, exp_ref, mixed_ref, inv_ref, grad_ref, out_ref):
    count = qkv_ref.shape[0]
    lane = lax.broadcasted_iota(jnp.int32, (count, HEAD_DIM), 1)
    minus = jnp.where(lane < 2, -1.0, 0.0).astype(bf16)
    scale = 1.0 / math.sqrt(HEAD_DIM)
    for head in range(2):
        base = 3 * HEAD_DIM * head
        cols = slice(head * HEAD_DIM, (head + 1) * HEAD_DIM)
        query = qkv_ref[:, base : base + HEAD_DIM]
        key = qkv_ref[:, base + HEAD_DIM : base + 2 * HEAD_DIM]
        value = qkv_ref[:, base + 2 * HEAD_DIM : base + 3 * HEAD_DIM]
        value = jnp.concatenate([value, minus], axis=1)
        scaled = grad_ref[:, cols].astype(f32) * inv_ref[:, cols]
        scaled_low = scaled.astype(bf16)
        inner = jnp.sum(scaled * mixed_ref[:, cols].astype(f32), axis=1, keepdims=True)
        inner_high = inner.astype(bf16).astype(f32)
        inner_pair = jnp.where(
            lane == 0, inner_high, jnp.where(lane == 1, inner - inner_high, 0.0)
        ).astype(bf16)
        wide = jnp.concatenate([scaled_low, inner_pair], axis=1)
        grad_key = grad_value = None
        for start in range(0, count, chunk):
            rows = slice(start, start + chunk)
            exponent = exp_ref[head, rows, :]
            grad_probs = mm(wide[rows], value, NT)
            grad_scores = (exponent.astype(f32) * grad_probs).astype(bf16)
            out_ref[rows, base : base + HEAD_DIM] = (mm(grad_scores, key) * scale).astype(bf16)
            key_part = mm(query[rows], grad_scores, TN)
            value_part = mm(scaled_low[rows], exponent, TN)
            grad_key = key_part if grad_key is None else grad_key + key_part
            grad_value = value_part if grad_value is None else grad_value + value_part
        out_ref[:, base + HEAD_DIM : base + 2 * HEAD_DIM] = (grad_key.T * scale).astype(bf16)
        out_ref[:, base + 2 * HEAD_DIM : base + 3 * HEAD_DIM] = grad_value.T.astype(bf16)


def attend_back(qkv, exponent, mixed, inverse, grad_mixed):
    count, width = qkv.shape
    pairs = width // (6 * HEAD_DIM)
    return pl.pallas_call(
        functools.partial(attend_back_kernel, min(512, count)),
        grid=(pairs,),
        in_specs=[
            pl.BlockSpec((count, 6 * HEAD_DIM), lambda p: (0, p)),
            pl.BlockSpec((2, count, count), lambda p: (p, 0, 0)),
        ]
        + [pl.BlockSpec((count, 2 * HEAD_DIM), lambda p: (0, p))] * 3,
        out_specs=pl.BlockSpec((count, 6 * HEAD_DIM), lambda p: (0, p)),
        out_shape=jax.ShapeDtypeStruct((count, width), bf16),
        compiler_params=pltpu.CompilerParams(vmem_limit_bytes=48 * 2**20),
        cost_estimate=pl.CostEstimate(
            flops=40 * pairs * count * count * HEAD_DIM,
            bytes_accessed=4 * pairs * count * count,
            transcendentals=0,
        ),
        name="attend_back",
    )(qkv, exponent, mixed, inverse, grad_mixed)


def normalize(values):
    centered = values - jnp.mean(values, axis=-1, keepdims=True)
    inverse = lax.rsqrt(jnp.mean(centered * centered, axis=-1, keepdims=True) + epsilon)
    return centered * inverse, inverse


def norm_back(grad_in, normed, inverse):
    return inverse * (
        grad_in
        - jnp.mean(grad_in, axis=-1, keepdims=True)
        - normed * jnp.mean(grad_in * normed, axis=-1, keepdims=True)
    )


def pick(values, index, axis):
    return lax.dynamic_index_in_dim(values, index, axis, keepdims=False)


def body(
    tokens, segments, w_qkv, qv_bias, w_out, out_bias, gain_one, shift_one,
    w_in, in_bias, w_down, down_bias, gain_two, shift_two, cotangent,
):
    row = lax.axis_index("row")
    col = lax.axis_index("col")
    chip, core = col // 2, col % 2
    same = row == chip
    first_core = core == 0
    seq_count, count, width = tokens.shape
    half = count // 2
    model = width * lax.axis_size("col")
    heads = qv_bias.shape[0] // (2 * HEAD_DIM)
    hidden = in_bias.shape[0]

    def by_half(mine, other):
        return jnp.where(same, mine, other), jnp.where(same, other, mine)

    mine = pick(tokens, chip, 0)
    pair = jnp.stack(by_half(mine, to_chip(pick(tokens, 1 - chip, 0))))
    pair = pair.reshape(2, 2, half, width)
    own, away = pick(pair, core, 1), pick(pair, 1 - core, 1)
    here = jnp.stack([own, away])
    there = to_core(jnp.stack([away, own]))
    even, odd = jnp.where(first_core, here, there), jnp.where(first_core, there, here)
    wide = jnp.stack([even, odd], axis=2)
    wide = wide.transpose(0, 3, 1, 2, 4).reshape(count, model)

    def small_gather(values):
        low, high = by_half(values, to_chip(values))
        both = jnp.stack([low, high], axis=1)
        other = to_core(both)
        even, odd = jnp.where(first_core, both, other), jnp.where(first_core, other, both)
        return jnp.stack([even, odd], axis=2).reshape(values.shape[0], model)

    vectors = small_gather(
        jnp.stack([out_bias, gain_one, shift_one, down_bias, gain_two, shift_two])
    )
    out_bias_w, gain_one_w, shift_one_w, down_bias_w, gain_two_w, shift_two_w = vectors
    qv_pairs = qv_bias.reshape(heads, 2, HEAD_DIM)
    qkv_bias = jnp.stack(
        [qv_pairs[:, 0], jnp.zeros_like(qv_pairs[:, 0]), qv_pairs[:, 1]], axis=1
    ).reshape(-1)
    bias_pack = jnp.concatenate([qkv_bias, in_bias])
    bias_pack = [bias_pack, to_chip(bias_pack)]
    qkv_biases = [b[: 3 * heads * HEAD_DIM] for b in bias_pack]
    in_biases = [b[3 * heads * HEAD_DIM :] for b in bias_pack]

    segment = pick(segments, chip, 0).reshape(2, half)
    segment = jnp.concatenate([pick(segment, core, 0), pick(segment, 1 - core, 0)])
    ids = jnp.arange(HEAD_DIM)
    differs = jnp.where((segment[:, None] != ids) & (ids < 3), -(2.0**30), 0.0)
    mask = jnp.concatenate([differs, segment[:, None] == ids], axis=1).astype(bf16)

    qkv_mine = jnp.concatenate([w_qkv, to_row(w_qkv)], axis=0)
    qkv_near = to_chip(w_qkv)
    qkv_other = jnp.concatenate([qkv_near, to_row(qkv_near)], axis=0)
    out_row = to_row(w_out)
    out_mine = jnp.concatenate([w_out, out_row], axis=1)
    out_other = jnp.concatenate([to_chip(w_out), to_chip(out_row)], axis=1)
    in_mine = jnp.concatenate([w_in, to_row(w_in)], axis=0)
    in_near = to_chip(w_in)
    in_other = jnp.concatenate([in_near, to_row(in_near)], axis=0)
    down_row = to_row(w_down)
    down_mine = jnp.concatenate([w_down, down_row], axis=1)
    down_other = jnp.concatenate([to_chip(w_down), to_chip(down_row)], axis=1)
    w_qkvs, w_outs = [qkv_mine, qkv_other], [out_mine, out_other]
    w_ins, w_downs = [in_mine, in_other], [down_mine, down_other]

    cot = pick(cotangent, chip, 0)
    cot = jnp.stack(by_half(cot, to_chip(pick(cotangent, 1 - chip, 0))))
    cot = cot.reshape(2, 2, half, width)
    cot_here, cot_there = pick(cot, core, 1), to_core(pick(cot, 1 - core, 1))
    even = jnp.where(first_core, cot_here, cot_there)
    odd = jnp.where(first_core, cot_there, cot_here)
    cot = jnp.stack([even, odd], axis=1).transpose(2, 0, 1, 3).reshape(half, model)

    def core_scatter(lefts, rights, dims):
        other = sum(mm(l[half:], r, dims) for l, r in zip(lefts, rights))
        arrived = to_core(other.astype(bf16))
        own = sum(mm(l[:half], r, dims) for l, r in zip(lefts, rights))
        return own + arrived.astype(f32)

    def core_gather(values):
        return jnp.concatenate([values, to_core(values)], axis=0)

    qkvs = [(mm(wide, w) + b).astype(bf16) for w, b in zip(w_qkvs, qkv_biases)]
    attended = [attend(qkv, mask) for qkv in qkvs]
    mixed = [a[1] for a in attended]
    attention = core_scatter(mixed, w_outs, NN) + out_bias_w
    normed_one, inverse_one = normalize(wide[:half].astype(f32) + attention)
    first_out = normed_one * gain_one_w + shift_one_w
    first_wide = core_gather(first_out.astype(bf16))
    acts, slopes = [], []
    for w, b in zip(w_ins, in_biases):
        pre = mm(first_wide, w) + b
        cdf = 0.5 * (1.0 + lax.erf(pre * (1.0 / math.sqrt(2.0))))
        pdf = jnp.exp(-0.5 * pre * pre) * (1.0 / math.sqrt(2.0 * math.pi))
        acts.append((pre * cdf).astype(bf16))
        slopes.append((cdf + pre * pdf).astype(bf16))
    ffn_out = core_scatter(acts, w_downs, NN) + down_bias_w
    normed_two, inverse_two = normalize(first_out + ffn_out)
    output = (normed_two * gain_two_w + shift_two_w).astype(bf16)

    cot = cot.astype(f32)
    grad_gain_two = jnp.sum(cot * normed_two, axis=0)
    grad_shift_two = jnp.sum(cot, axis=0)
    grad_pre_two = norm_back(cot * gain_two_w, normed_two, inverse_two)
    grad_ffn = grad_pre_two.astype(bf16)
    grad_down_bias = jnp.sum(grad_ffn, axis=0, dtype=f32)
    grad_ffn_wide = core_gather(grad_ffn)
    grad_downs = [mm(a, grad_ffn_wide, TN).astype(bf16) for a in acts]
    grad_hiddens = [
        (mm(grad_ffn_wide, w, NT) * s.astype(f32)).astype(bf16) for w, s in zip(w_downs, slopes)
    ]
    grad_in_biases = [jnp.sum(g, axis=0, dtype=f32) for g in grad_hiddens]
    grad_normed = grad_pre_two + core_scatter(grad_hiddens, w_ins, NT)
    grad_ins = [mm(first_wide, g, TN).astype(bf16) for g in grad_hiddens]
    grad_gain_one = jnp.sum(grad_normed * normed_one, axis=0)
    grad_shift_one = jnp.sum(grad_normed, axis=0)
    grad_pre_one = norm_back(grad_normed * gain_one_w, normed_one, inverse_one)
    grad_attention = grad_pre_one.astype(bf16)
    grad_out_bias = jnp.sum(grad_attention, axis=0, dtype=f32)
    grad_attn_wide = core_gather(grad_attention)
    grad_outs = [mm(m, grad_attn_wide, TN).astype(bf16) for m in mixed]
    grad_mixed = [mm(grad_attn_wide, w, NT).astype(bf16) for w in w_outs]
    grad_qkvs = [
        attend_back(qkv, e, m, i, g)
        for qkv, (e, m, i), g in reversed(list(zip(qkvs, attended, grad_mixed)))
    ][::-1]
    grad_w_qkvs = [mm(wide, g, TN).astype(bf16) for g in reversed(grad_qkvs)][::-1]
    grad_wide = sum(mm(g, w, NT) for g, w in zip(grad_qkvs, w_qkvs))
    grad_wide = jnp.concatenate([grad_wide[:half] + grad_pre_one, grad_wide[half:]], axis=0)

    def chip_return(values):
        mine = jnp.where(same, values[:, 0], values[:, 1])
        away = jnp.where(same, values[:, 1], values[:, 0])
        arrived = to_chip(away)
        first = chip == 0
        return jnp.stack([jnp.where(first, mine, arrived), jnp.where(first, arrived, mine)])

    def token_order(own, other):
        return jnp.concatenate(
            [jnp.where(first_core, own, other), jnp.where(first_core, other, own)], axis=0
        )

    split = output.reshape(half, 2, 2, width)
    output = chip_return(token_order(pick(split, core, 2), to_core(pick(split, 1 - core, 2))))
    split = grad_wide.reshape(count, 2, 2, width)
    arrived = to_core(pick(split, 1 - core, 2).astype(bf16))
    arrived = jnp.concatenate([arrived[half:], arrived[:half]], axis=0)
    split = (pick(split, core, 2) + arrived.astype(f32)).astype(bf16)
    grad_tokens = chip_return(token_order(split[:half], split[half:]))

    def halves(values, axis):
        size = values.shape[axis] // 2
        return lax.slice_in_dim(values, 0, size, axis=axis), lax.slice_in_dim(
            values, size, 2 * size, axis=axis
        )

    def added(own, arrived):
        return (own.astype(f32) + arrived.astype(f32)).astype(bf16)

    def chip_first(mine, other, axis):
        own, away = halves(added(mine, to_chip(other)), axis)
        return added(own, to_row(away))

    def row_first(mine, other, axis):
        parts = [halves(v, axis) for v in (mine, other)]
        mine, other = [added(own, to_row(away)) for own, away in parts]
        return added(mine, to_chip(other))

    def over_dp(values):
        return lax.psum(values, "dp").astype(f32)

    grad_w_down = over_dp(row_first(*grad_downs, 1))
    grad_w_in = over_dp(chip_first(*grad_ins, 0))
    grad_w_out = over_dp(chip_first(*grad_outs, 1))
    cut = 3 * heads * HEAD_DIM // 2
    grad_w_qkv = over_dp(
        jnp.concatenate(
            [
                row_first(*[g[:, :cut] for g in grad_w_qkvs], 0),
                chip_first(*[g[:, cut:] for g in grad_w_qkvs], 0),
            ],
            axis=1,
        )
    )

    features = jnp.stack(
        [grad_out_bias, grad_gain_one, grad_shift_one, grad_down_bias, grad_gain_two, grad_shift_two]
    ).reshape(6, 2, 2, width)
    features = pick(features, core, 2) + to_core(pick(features, 1 - core, 2))
    feature_own = jnp.where(same, features[:, 0], features[:, 1])
    feature_away = jnp.where(same, features[:, 1], features[:, 0])
    qv_sums = []
    for g in grad_qkvs:
        sums = jnp.sum(g, axis=0, dtype=f32).reshape(heads, 3, HEAD_DIM)
        qv_sums.append(jnp.stack([sums[:, 0], sums[:, 2]], axis=1).reshape(-1))
    small = [
        jnp.concatenate([q, i, f.reshape(-1)])
        for q, i, f in zip(qv_sums, grad_in_biases, (feature_own, feature_away))
    ]
    small = lax.psum(small[0] + to_chip(small[1]), ("dp", "row"))
    qv_len = qv_bias.shape[0]
    g_qv, g_in = small[:qv_len], small[qv_len : qv_len + hidden]
    g_out, g_gone, g_sone, g_down, g_gtwo, g_stwo = small[qv_len + hidden :].reshape(6, width)
    return (
        output, grad_tokens, grad_w_qkv, g_qv, grad_w_out, g_out, g_gone, g_sone,
        grad_w_in, g_in, grad_w_down, g_down, g_gtwo, g_stwo,
    )


def solution(mesh):
    tokens = P(("dp", "row"), None, "col")
    feature = P("col")
    by_row, by_col = P("row", "col"), P("col", "row")
    return jax.shard_map(
        body,
        mesh=mesh,
        in_specs=(
            tokens, P(("dp", "row"), None), by_row, feature, by_col, feature, feature, feature,
            by_row, feature, by_col, feature, feature, feature, tokens,
        ),
        out_specs=(
            tokens, tokens, by_row, feature, by_col, feature, feature, feature,
            by_row, feature, by_col, feature, feature, feature,
        ),
        check_vma=False,
    )
```

time: 911 us -> 553 us (0.61)
  waiting for transfers between devices: 524 us -> 200 us
  matrix products: 172 us -> 81.4 us
  local copies, waits for them, and re-layouts: 31.6 us -> 84.6 us
  Pallas kernels: 0 us -> 45.2 us
  blocking collectives: 83 us -> 39.7 us
  starting transfers between devices: 1.29 us -> 33 us
  other arithmetic: 74 us -> 47.3 us
    reduce_scatter x8 -> x0, waiting for transfers between devices: 253 us -> none  [the longest x2 143 us: scatter_forward(): return lax.psum_scatter(values, 'col', scatter_dimension=2, tiled=True)]
    all_gather x7 -> x0, waiting for transfers between devices: 185 us -> none  [the longest x2 73.7 us: gather_features(): return lax.all_gather(values, 'col', axis=2, tiled=True)]
    ppermute x0 -> x43, waiting for transfers between devices: none -> 137 us  [the longest x13 77.5 us: to_row(): return lax.ppermute(values, 'row', [(0, 1), (1, 0)])]
    dot_general x26 -> x30, matrix products: 172 us -> 81.4 us  [mm(): return lax.dot_general(left, right, dims, preferred_element_type=f32)]
    pallas_call x0 -> x4, Pallas kernels: none -> 45.2 us  [the longest x2 24.8 us: attend_back(): pl.pallas_call(functools.partial(attend_back_kernel, min(512, count)), gr...]
    ppermute x0 -> x43, starting transfers between devices: none -> 33 us  [the longest x13 15.7 us: to_row(): return lax.ppermute(values, 'row', [(0, 1), (1, 0)])]
    psum x7 -> x1, blocking collectives: 65.6 us -> 39.7 us  [body(): small = lax.psum(small[0] + to_chip(small[1]), ('dp', 'row'))]
    reduce_sum x11, other arithmetic: 36.9 us -> 15 us  [the longest x1 4.56 us: body(): grad_out_bias = jnp.sum(grad_attention, axis=0, dtype=f32)]
  transfers between devices with their start and end apart: 16 -> 44, of which waited for: 13 -> 12; matrix products, arithmetic and copies ran while one was open for 18% -> 32% of each run, Pallas kernels for 0% -> 8%
where the time goes in v1:
time: 553 us; the launch traced here: 547 us
  waiting for transfers between devices  200 us (36%)
  local copies, waits for them, and re-layouts  84.6 us (15%)
  matrix products  81.4 us (15%)
  other arithmetic  47.3 us (9%)
  Pallas kernels  45.2 us (8%)
  blocking collectives  39.7 us (7%)
  starting transfers between devices  33 us (6%)
  between operations  15.8 us (3%)
    dot_general x30, matrix products, mm(): return lax.dot_general(left, right, dims, preferred_element_type=f32)  81.4 us
    ppermute x13, waiting for transfers between devices, to_row(): return lax.ppermute(values, 'row', [(0, 1), (1, 0)])  77.5 us
    psum x1, waiting for transfers between devices, over_dp(): return lax.psum(values, 'dp').astype(f32)  62.5 us
    ppermute x18, waiting for transfers between devices, to_chip(): return lax.ppermute(values, 'col', [(i, i ^ 2) for i in range(size)])  59.9 us
    psum x1, blocking collectives, body(): small = lax.psum(small[0] + to_chip(small[1]), ('dp', 'row'))  39.7 us
    unnamed x175, local copies, waits for them, and re-layouts  29.7 us
    pallas_call x2, Pallas kernels, attend_back(): pl.pallas_call(functools.partial(attend_back_kernel, min(512, count)), gr...  24.8 us
    pallas_call x2, Pallas kernels, attend(): pl.pallas_call(functools.partial(attend_kernel, min(512, count)), grid=(p...  20.5 us
  transfers between devices with their start and end apart: 44, of which 12 were waited for; matrix products, arithmetic and copies ran while one was open for 32% of the time, Pallas kernels for 8%

profile of v1, /device:TPU:0, one launch (start us, length us, event | category | flops | bytes accessed | tf_op | source)
XLA Modules:
  0.0 547.0 jit_solution(5881124831329623641)
XLA Ops:
  7.3 3.0 collective-permute-start.3
  27.1 19.6 %collective-permute-done.6 = f32[1792]{0:T(1024)S(1)} collective-permute-done((f32[1792]{0:T(1024)S(1)}, f32[1792]{0:T(1024)S(1)}, u32[]{:S(2)}, u32[]{:S(2)}) %collective-permute-start.6) | collective-permute-done | bytes 7200 | tf_op jit(solution)/shard_map/ppermute | solution.py:31
  53.6 11.3 %collective-permute-done.8 = bf16[256,512]{1,0:T(8,128)(2,1)S(1)} collective-permute-done((bf16[256,512]{1,0:T(8,128)(2,1)}, bf16[256,512]{1,0:T(8,128)(2,1)S(1)}, u32[]{:S(2)}, u32[]{:S(2)}) %collective-permute-start.8) | collective-permute-done | bytes 262176 | tf_op jit(solution)/shard_map/ppermute | solution.py:31
  77.8 3.3 reshape.189
  81.0 3.8 add_convert_fusion.2.qkv_ref
  84.9 10.2 %attend.2 = (bf16[4,1024,1024]{2,1,0:T(8,128)(2,1)}, bf16[1024,256]{1,0:T(8,128)(2,1)S(1)}, f32[1024,256]{1,0:T(8,128)S(1)}) custom-call(bf16[1024,768]{1,0:T(8,128)(2,1)S(1)} %add_convert_fusion.2.qkv_ref, bf16[1024,128]{1,0:T(8,128)(2,1)S(1)} %pad_maximum_fusion.12.mask_ref), custom_call_target="tpu_custom_call" | custom-call | flops 4294967296 | bytes 8388608 | tf_op jit(solution)/shard_map/attend/pallas_call | solution.py:65
  95.6 36.9 %collective-permute-done.5 = bf16[512,768]{1,0:T(8,128)(2,1)} collective-permute-done((bf16[512,768]{1,0:T(8,128)(2,1)}, bf16[512,768]{1,0:T(8,128)(2,1)}, u32[]{:S(2)}, u32[]{:S(2)}) %collective-permute-start.5) | collective-permute-done | bytes 786464 | tf_op jit(solution)/shard_map/ppermute | solution.py:35
  135.5 10.3 %attend.3 = (bf16[4,1024,1024]{2,1,0:T(8,128)(2,1)}, bf16[1024,256]{1,0:T(8,128)(2,1)S(1)}, f32[1024,256]{1,0:T(8,128)S(1)}) custom-call(bf16[1024,768]{1,0:T(8,128)(2,1)S(1)} %add_convert_fusion.1.qkv_ref, bf16[1024,128]{1,0:T(8,128)(2,1)S(1)} %pad_maximum_fusion.12.mask_ref), custom_call_target="tpu_custom_call" | custom-call | flops 4294967296 | bytes 8388608 | tf_op jit(solution)/shard_map/attend/pallas_call | solution.py:65
  151.0 2.9 copy.61
  154.0 3.9 reshape.198
  171.4 14.1 %collective-permute-done.18 = bf16[1024,512]{1,0:T(8,128)(2,1)S(1)} collective-permute-done((bf16[1024,512]{1,0:T(8,128)(2,1)}, bf16[1024,512]{1,0:T(8,128)(2,1)S(1)}, u32[]{:S(2)}, u32[]{:S(2)}) %collective-permute-start.18) | collective-permute-done | bytes 1048608 | tf_op jit(solution)/shard_map/ppermute | solution.py:31
  185.8 5.5 %multiply_convert_fusion.3 = (bf16[1024,1024]{1,0:T(8,128)(2,1)S(1)}, f32[1024,1024]{1,0:T(8,128)}) fusion(f32[1024]{0:T(1024)S(1)} %copy-done.65, bf16[1024,1024]{1,0:T(8,128)(2,1)S(1)} %constant_dynamic-update-slice_fusion.8, bf16[512,1024]{1,0:T(8,128)(2,1)S(1)} %collective-permute-done.12, bf16[512,1024]{1,0:T(8,128)(2,1)S(1)} %fusion.11), kind=kOutput, calls=%fused_computation.20 | convolution fusion | flops 2157969408 | bytes 10489856 | tf_op jit(solution)/shard_map/dot_general | solution.py:21
  192.7 5.7 %multiply_convert_fusion.2 = (bf16[1024,1024]{1,0:T(8,128)(2,1)S(1)}, f32[1024,1024]{1,0:T(8,128)}) fusion(f32[1024]{0:T(1024)S(1)} %slice.241, bf16[1024,1024]{1,0:T(8,128)(2,1)S(1)} %constant_dynamic-update-slice_fusion.12, bf16[512,1024]{1,0:T(8,128)(2,1)S(1)} %collective-permute-done.12, bf16[512,1024]{1,0:T(8,128)(2,1)S(1)} %fusion.11), kind=kOutput, calls=%fused_computation.18 | convolution fusion | flops 2157969408 | bytes 10489856 | tf_op jit(solution)/shard_map/dot_general | solution.py:21
  200.9 2.9 copy.67
  203.8 3.9 reshape.199
  207.7 3.3 fusion.27
  216.0 2.9 convert_reduce_fusion.4
  221.6 3.1 constant_dynamic-slice_fusion.3
  225.7 4.0 convolution_convert_fusion
  232.4 4.1 convolution_convert_fusion.1
  240.3 5.6 %convert_reduce_fusion = (f32[1024]{0:T(1024)S(1)}, bf16[1024,1024]{1,0:T(8,128)(2,1)S(1)}) fusion(f32[1024,1024]{1,0:T(8,128)S(1)} %copy-done.76, f32[1024]{0:T(1024)S(1)} %slice.241, bf16[1024,1024]{1,0:T(8,128)(2,1)S(1)} %copy-done.56, bf16[512,1024]{1,0:T(8,128)(2,1)} %collective-permute-done.24, bf16[512,1024]{1,0:T(8,128)(2,1)} %get-tuple-element.97), kind=kOutput, calls=%fused_computation.14 | convolution fusion | flops 2167405568 | bytes 10493952 | tf_op jit(solution)/shard_map/dot_general | solution.py:21
  248.8 5.7 %convert_reduce_fusion.1 = (f32[1024]{0:T(1024)S(1)}, bf16[1024,1024]{1,0:T(8,128)(2,1)S(1)}) fusion(f32[1024,1024]{1,0:T(8,128)S(1)} %copy-done.75, f32[1024]{0:T(1024)S(1)} %copy-done.65, bf16[1024,1024]{1,0:T(8,128)(2,1)S(1)} %copy-done.51, bf16[512,1024]{1,0:T(8,128)(2,1)} %collective-permute-done.24, bf16[512,1024]{1,0:T(8,128)(2,1)} %get-tuple-element.97), kind=kOutput, calls=%fused_computation.15 | convolution fusion | flops 2167405568 | bytes 10493952 | tf_op jit(solution)/shard_map/dot_general | solution.py:21
  257.4 3.7 convolution_convert_fusion.2
  262.8 3.8 fusion.66
  266.6 2.4 multiply_reduce_fusion.1
  269.0 4.6 convert_reduce_fusion.5
  273.8 12.8 %collective-permute-done.41 = bf16[1024,512]{1,0:T(8,128)(2,1)} collective-permute-done((bf16[1024,512]{1,0:T(8,128)(2,1)}, bf16[1024,512]{1,0:T(8,128)(2,1)}, u32[]{:S(2)}, u32[]{:S(2)}) %collective-permute-start.41) | collective-permute-done | bytes 1048608 | tf_op jit(solution)/shard_map/ppermute | solution.py:35
  286.7 2.9 add_convert_fusion.4
  290.0 2.4 convolution_convert_fusion.8.grad_ref
  292.4 12.4 %attend_back.2 = bf16[1024,768]{1,0:T(8,128)(2,1)S(1)} custom-call(bf16[1024,768]{1,0:T(8,128)(2,1)S(1)} %copy-done.3, bf16[4,1024,1024]{2,1,0:T(8,128)(2,1)} %get-tuple-element.22.exp_ref, bf16[1024,256]{1,0:T(8,128)(2,1)S(1)} %get-tuple-element.20.mixed_ref, f32[1024,256]{1,0:T(8,128)S(1)} %get-tuple-element.23.inv_ref, ...), custom_call_target="tpu_custom_call" | custom-call | flops 5368709120 | bytes 8388608 | tf_op jit(solution)/shard_map/attend_back/pallas_call | solution.py:130
  305.1 3.0 convolution_convert_fusion.4
  310.3 12.4 %attend_back.3 = bf16[1024,768]{1,0:T(8,128)(2,1)S(1)} custom-call(bf16[1024,768]{1,0:T(8,128)(2,1)S(1)} %copy-done.5, bf16[4,1024,1024]{2,1,0:T(8,128)(2,1)} %get-tuple-element.24.exp_ref, bf16[1024,256]{1,0:T(8,128)(2,1)S(1)} %get-tuple-element.21.mixed_ref, f32[1024,256]{1,0:T(8,128)S(1)} %copy-done.7, ...), custom_call_target="tpu_custom_call" | custom-call | flops 5368709120 | bytes 8388608 | tf_op jit(solution)/shard_map/attend_back/pallas_call | solution.py:130
  327.0 3.9 fusion.76
  331.1 3.2 convolution_convert_fusion.5
  340.7 2.6 pad_maximum_fusion
  343.3 6.9 %reshape.193 = f32[1024,2,2,256]{3,2,1,0:T(2,128)} reshape(f32[1024,1024]{1,0:T(8,128)} %pad_maximum_fusion) | data formatting | bytes 8388608 | tf_op jit(solution)/shard_map/reshape | solution.py:316
  352.3 3.1 add_convert_fusion.3
  358.9 2.6 add_convert_fusion
  361.5 8.3 %collective-permute-done.30 = bf16[512,384]{0,1:T(8,128)(2,1)S(1)} collective-permute-done((bf16[512,384]{0,1:T(8,128)(2,1)}, bf16[512,384]{0,1:T(8,128)(2,1)S(1)}, u32[]{:S(2)}, u32[]{:S(2)}) %collective-permute-start.30) | collective-permute-done | bytes 393248 | tf_op jit(solution)/shard_map/ppermute | solution.py:35
  375.2 2.8 collective-permute-done.32
  379.9 4.9 collective-permute-done.31
  386.4 15.1 %collective-permute-done.37 = bf16[256,512]{1,0:T(8,128)(2,1)S(1)} collective-permute-done((bf16[256,512]{1,0:T(8,128)(2,1)S(1)}, bf16[256,512]{1,0:T(8,128)(2,1)S(1)}, u32[]{:S(2)}, u32[]{:S(2)}) %collective-permute-start.37) | collective-permute-done | bytes 262176 | tf_op jit(solution)/shard_map/ppermute | solution.py:35
  403.8 4.3 collective-permute-done.33
  409.7 4.0 constant_dynamic-slice_fusion.1
  418.2 39.7 %psum.36 = f32[3072]{0:T(1024)S(1)} all-reduce(f32[3072]{0:T(1024)S(1)} %maximum_add_fusion), channel_id=1, replica_groups=mesh['dp'=4,'row'=2,'col'=4] {'dp','row'}, use_global_device_ids=true, to_apply=%region_19.20 | all-reduce | flops 3072 | bytes 24576 | tf_op jit(solution)/shard_map/psum | solution.py:371
  461.4 7.1 %collective-permute-done.21 = bf16[1024,256]{1,0:T(8,128)(2,1)S(1)} collective-permute-done((bf16[1024,256]{1,0:T(8,128)(2,1)S(1)}, bf16[1024,256]{1,0:T(8,128)(2,1)S(1)}, u32[]{:S(2)}, u32[]{:S(2)}) %collective-permute-start.21) | collective-permute-done | bytes 524320 | tf_op jit(solution)/shard_map/ppermute | solution.py:31
  469.8 62.5 %all-reduce.3.cloned.1.call-done = (bf16[512,768]{0,1:T(8,128)(2,1)}, bf16[256,512]{1,0:T(8,128)(2,1)}, bf16[512,1024]{1,0:T(8,128)(2,1)}, bf16[1024,512]{1,0:T(8,128)(2,1)}) async-done(((bf16[512,768]{0,1:T(8,128)(2,1)}, bf16[256,512]{1,0:T(8,128)(2,1)}, bf16[512,1024]{1,0:T(8,128)(2,1)}, bf16[1024,512]{1,0:T(8,128)(2,1)}), (bf16[512,768]{0,1:T(8,128)(2,1)}, bf16[256,512]{1,0:T(8,128)(2,1)}, ...) | async-done | bytes 3145744 | tf_op jit(solution)/shard_map/psum | solution.py:341
  534.3 2.5 copy.77
  (386 shorter events, 131.1 us)
Async XLA Ops:
  7.2 525.1 %all-reduce.3.cloned.1.call-start = ((), (), s32[]{:S(2)}) async-start(), calls=%async_computation | async-start | bytes 6291456 | tf_op jit(solution)/shard_map/psum | solution.py:341
  7.3 43.0 %collective-permute-start.3 = (bf16[256,512]{1,0:T(8,128)(2,1)}, bf16[256,512]{1,0:T(8,128)(2,1)}, u32[]{:S(2)}, u32[]{:S(2)}) collective-permute-start(bf16[256,512]{1,0:T(8,128)(2,1)} %param.19), channel_id=1, source_target_pairs={{0,4},{4,0},{1,5},{5,1},{2,6},{6,2},{3,7},{7,3},{8,12},{12,8},{9,1... | collective-permute-start | bytes 786440 | tf_op jit(solution)/shard_map/ppermute | solution.py:35
  10.3 40.8 %collective-permute-start.7 = (bf16[256,512]{1,0:T(8,128)(2,1)}, bf16[256,512]{1,0:T(8,128)(2,1)}, u32[]{:S(2)}, u32[]{:S(2)}) collective-permute-start(bf16[256,512]{1,0:T(8,128)(2,1)} %param.19), channel_id=1, source_target_pairs={{0,2},{1,3},{2,0},{3,1},{4,6},{5,7},{6,4},{7,5},{8,10},{9,11},{10,... | collective-permute-start | bytes 786440 | tf_op jit(solution)/shard_map/ppermute | solution.py:31
  12.6 12.9 %collective-permute-start.10 = (f32[6,256]{1,0:T(8,128)S(1)}, f32[6,256]{1,0:T(8,128)S(1)}, u32[]{:S(2)}, u32[]{:S(2)}) collective-permute-start(f32[6,256]{1,0:T(8,128)S(1)} %stack.154), channel_id=1, source_target_pairs={{0,2},{1,3},{2,0},{3,1},{4,6},{5,7},{6,4},{7,5},{8,10},{9,11},{10,... | collective-permute-start | bytes 18440 | tf_op jit(solution)/shard_map/ppermute | solution.py:31
  15.0 33.2 %collective-permute-start = (bf16[1024,256]{1,0:T(8,128)(2,1)}, bf16[1024,256]{1,0:T(8,128)(2,1)}, u32[]{:S(2)}, u32[]{:S(2)}) collective-permute-start(bf16[1024,256]{1,0:T(8,128)(2,1)} %dynamic-slice_bitcast_fusion.1), channel_id=1, source_target_pairs={{0,2},{1,3},{2,0},{3,1},{4,6},{5,7},{6,4},{7,5},{8,10},{9,11},{10,... | collective-permute-start | bytes 1572872 | tf_op jit(solution)/shard_map/ppermute | solution.py:31
  16.5 51.3 %collective-permute-start.4 = (bf16[512,768]{1,0:T(8,128)(2,1)}, bf16[512,768]{1,0:T(8,128)(2,1)}, u32[]{:S(2)}, u32[]{:S(2)}) collective-permute-start(bf16[512,768]{1,0:T(8,128)(2,1)} %param.17), channel_id=1, source_target_pairs={{0,2},{1,3},{2,0},{3,1},{4,6},{5,7},{6,4},{7,5},{8,10},{9,11},{10,... | collective-permute-start | bytes 2359304 | tf_op jit(solution)/shard_map/ppermute | solution.py:31
  25.5 21.2 %collective-permute-start.6 = (f32[1792]{0:T(1024)S(1)}, f32[1792]{0:T(1024)S(1)}, u32[]{:S(2)}, u32[]{:S(2)}) collective-permute-start(f32[1792]{0:T(1024)S(1)} %pad_maximum_fusion.16), channel_id=1, source_target_pairs={{0,2},{1,3},{2,0},{3,1},{4,6},{5,7},{6,4},{7,5},{8,10},{9,11},{10,... | collective-permute-start | bytes 21512 | tf_op jit(solution)/shard_map/ppermute | solution.py:31
  46.7 18.9 %collective-permute-start.22 = (bf16[1024,256]{1,0:T(8,128)(2,1)S(1)}, bf16[1024,256]{1,0:T(8,128)(2,1)S(1)}, u32[]{:S(2)}, u32[]{:S(2)}) collective-permute-start(bf16[1024,256]{1,0:T(8,128)(2,1)S(1)} %copy-done.57), channel_id=1, source_target_pairs={{0,2},{1,3},{2,0},{3,1},{4,6},{5,7},{6,4},{7,5},{8,10},{9,11},{10,... | collective-permute-start | bytes 1572872 | tf_op jit(solution)/shard_map/ppermute | solution.py:31
  48.2 1.4 collective-permute-start.11
  49.7 22.4 %collective-permute-start.1 = (bf16[2,2,512,256]{3,2,1,0:T(8,128)(2,1)S(1)}, bf16[2,2,512,256]{3,2,1,0:T(8,128)(2,1)S(1)}, u32[]{:S(2)}, u32[]{:S(2)}) collective-permute-start(bf16[2,2,512,256]{3,2,1,0:T(8,128)(2,1)S(1)} %pad_maximum_fusion.5), channel_id=1, source_target_pairs={{0,1},{1,0},{2,3},{3,2},{4,5},{5,4},{6,7},{7,6},{8,9},{9,8},{10,11... | collective-permute-start | bytes 3145736 | tf_op jit(solution)/shard_map/ppermute | solution.py:26
  50.6 21.0 %collective-permute-start.2 = (bf16[512,768]{1,0:T(8,128)(2,1)S(1)}, bf16[512,768]{1,0:T(8,128)(2,1)S(1)}, u32[]{:S(2)}, u32[]{:S(2)}) collective-permute-start(bf16[512,768]{1,0:T(8,128)(2,1)S(1)} %copy-done.44), channel_id=1, source_target_pairs={{0,4},{4,0},{1,5},{5,1},{2,6},{6,2},{3,7},{7,3},{8,12},{12,8},{9,1... | collective-permute-start | bytes 2359304 | tf_op jit(solution)/shard_map/ppermute | solution.py:35
  51.1 13.8 %collective-permute-start.8 = (bf16[256,512]{1,0:T(8,128)(2,1)}, bf16[256,512]{1,0:T(8,128)(2,1)S(1)}, u32[]{:S(2)}, u32[]{:S(2)}) collective-permute-start(bf16[256,512]{1,0:T(8,128)(2,1)} %collective-permute-done.3), channel_id=1, source_target_pairs={{0,2},{1,3},{2,0},{3,1},{4,6},{5,7},{6,4},{7,5},{8,10},{9,11},{10,... | collective-permute-start | bytes 786440 | tf_op jit(solution)/shard_map/ppermute | solution.py:31
  64.9 102.4 %collective-permute-start.13 = (bf16[512,1024]{1,0:T(8,128)(2,1)}, bf16[512,1024]{1,0:T(8,128)(2,1)}, u32[]{:S(2)}, u32[]{:S(2)}) collective-permute-start(bf16[512,1024]{1,0:T(8,128)(2,1)} %param.23), channel_id=1, source_target_pairs={{0,4},{4,0},{1,5},{5,1},{2,6},{6,2},{3,7},{7,3},{8,12},{12,8},{9,1... | collective-permute-start | bytes 3145736 | tf_op jit(solution)/shard_map/ppermute | solution.py:35
  66.4 81.6 %collective-permute-start.15 = (bf16[512,1024]{1,0:T(8,128)(2,1)}, bf16[512,1024]{1,0:T(8,128)(2,1)}, u32[]{:S(2)}, u32[]{:S(2)}) collective-permute-start(bf16[512,1024]{1,0:T(8,128)(2,1)} %param.23), channel_id=1, source_target_pairs={{0,2},{1,3},{2,0},{3,1},{4,6},{5,7},{6,4},{7,5},{8,10},{9,11},{10,... | collective-permute-start | bytes 3145736 | tf_op jit(solution)/shard_map/ppermute | solution.py:31
  67.9 92.0 %collective-permute-start.14 = (bf16[1024,512]{1,0:T(8,128)(2,1)}, bf16[1024,512]{1,0:T(8,128)(2,1)}, u32[]{:S(2)}, u32[]{:S(2)}) collective-permute-start(bf16[1024,512]{1,0:T(8,128)(2,1)} %param.25), channel_id=1, source_target_pairs={{0,4},{4,0},{1,5},{5,1},{2,6},{6,2},{3,7},{7,3},{8,12},{12,8},{9,1... | collective-permute-start | bytes 3145736 | tf_op jit(solution)/shard_map/ppermute | solution.py:35
  71.5 92.6 %collective-permute-start.17 = (bf16[1024,512]{1,0:T(8,128)(2,1)}, bf16[1024,512]{1,0:T(8,128)(2,1)}, u32[]{:S(2)}, u32[]{:S(2)}) collective-permute-start(bf16[1024,512]{1,0:T(8,128)(2,1)} %param.25), channel_id=1, source_target_pairs={{0,2},{1,3},{2,0},{3,1},{4,6},{5,7},{6,4},{7,5},{8,10},{9,11},{10,... | collective-permute-start | bytes 3145736 | tf_op jit(solution)/shard_map/ppermute | solution.py:31
  73.2 59.2 %collective-permute-start.5 = (bf16[512,768]{1,0:T(8,128)(2,1)}, bf16[512,768]{1,0:T(8,128)(2,1)}, u32[]{:S(2)}, u32[]{:S(2)}) collective-permute-start(bf16[512,768]{1,0:T(8,128)(2,1)} %collective-permute-done.4), channel_id=1, source_target_pairs={{0,4},{4,0},{1,5},{5,1},{2,6},{6,2},{3,7},{7,3},{8,12},{12,8},{9,1... | collective-permute-start | bytes 2359304 | tf_op jit(solution)/shard_map/ppermute | solution.py:35
  95.1 37.3 %copy-start.61 = (bf16[1024,768]{1,0:T(8,128)(2,1)S(1)}, bf16[1024,768]{1,0:T(8,128)(2,1)}, u32[]{:S(2)}) copy-start(bf16[1024,768]{1,0:T(8,128)(2,1)} %constant_dynamic-update-slice_fusion.5) | copy-start | bytes 4718596
  95.1 38.5 %copy-start.28 = (bf16[1024,1024]{1,0:T(8,128)(2,1)S(1)}, bf16[1024,1024]{1,0:T(8,128)(2,1)}, u32[]{:S(2)}) copy-start(bf16[1024,1024]{1,0:T(8,128)(2,1)} %reshape.189) | copy-start | bytes 6291460
  95.1 38.5 %slice-start = ((f32[1792]{0:T(1024)}), f32[768]{0:T(1024)S(1)}, s32[]{:S(2)}) async-start(f32[1792]{0:T(1024)} %copy-done.64), calls=%async_computation.1 | async-start | bytes 8192 | tf_op jit(solution)/shard_map/slice | solution.py:213
  147.2 13.3 %collective-permute-start.9 = (bf16[512,1024]{1,0:T(8,128)(2,1)}, bf16[512,1024]{1,0:T(8,128)(2,1)}, u32[]{:S(2)}, u32[]{:S(2)}) collective-permute-start(bf16[512,1024]{1,0:T(8,128)(2,1)} %add_convert_fusion.10), channel_id=1, source_target_pairs={{0,1},{1,0},{2,3},{3,2},{4,5},{5,4},{6,7},{7,6},{8,9},{9,8},{10,11... | collective-permute-start | bytes 3145736 | tf_op jit(solution)/shard_map/ppermute | solution.py:26
  148.1 21.3 %collective-permute-start.23 = (bf16[2,512,256]{2,1,0:T(8,128)(2,1)}, bf16[2,512,256]{2,1,0:T(8,128)(2,1)}, u32[]{:S(2)}, u32[]{:S(2)}) collective-permute-start(bf16[2,512,256]{2,1,0:T(8,128)(2,1)} %fusion.34), channel_id=1, source_target_pairs={{0,1},{1,0},{2,3},{3,2},{4,5},{5,4},{6,7},{7,6},{8,9},{9,8},{10,11... | collective-permute-start | bytes 1572872 | tf_op jit(solution)/shard_map/ppermute | solution.py:26
  159.9 25.8 %collective-permute-start.16 = (bf16[512,1024]{1,0:T(8,128)(2,1)}, bf16[512,1024]{1,0:T(8,128)(2,1)S(1)}, u32[]{:S(2)}, u32[]{:S(2)}) collective-permute-start(bf16[512,1024]{1,0:T(8,128)(2,1)} %collective-permute-done.15), channel_id=1, source_target_pairs={{0,4},{4,0},{1,5},{5,1},{2,6},{6,2},{3,7},{7,3},{8,12},{12,8},{9,1... | collective-permute-start | bytes 3145736 | tf_op jit(solution)/shard_map/ppermute | solution.py:35
  160.5 25.0 %collective-permute-start.18 = (bf16[1024,512]{1,0:T(8,128)(2,1)}, bf16[1024,512]{1,0:T(8,128)(2,1)S(1)}, u32[]{:S(2)}, u32[]{:S(2)}) collective-permute-start(bf16[1024,512]{1,0:T(8,128)(2,1)} %collective-permute-done.14), channel_id=1, source_target_pairs={{0,2},{1,3},{2,0},{3,1},{4,6},{5,7},{6,4},{7,5},{8,10},{9,11},{10,... | collective-permute-start | bytes 3145736 | tf_op jit(solution)/shard_map/ppermute | solution.py:31
  164.1 28.4 %copy-start.38 = (bf16[512,1024]{1,0:T(8,128)(2,1)}, bf16[512,1024]{1,0:T(8,128)(2,1)S(1)}, u32[]{:S(2)}) copy-start(bf16[512,1024]{1,0:T(8,128)(2,1)S(1)} %fusion.11) | copy-start | bytes 3145732
  164.2 21.6 %collective-permute-start.12 = (bf16[512,1024]{1,0:T(8,128)(2,1)S(1)}, bf16[512,1024]{1,0:T(8,128)(2,1)S(1)}, u32[]{:S(2)}, u32[]{:S(2)}) collective-permute-start(bf16[512,1024]{1,0:T(8,128)(2,1)S(1)} %fusion.11), channel_id=1, source_target_pairs={{0,1},{1,0},{2,3},{3,2},{4,5},{5,4},{6,7},{7,6},{8,9},{9,8},{10,11... | collective-permute-start | bytes 3145736 | tf_op jit(solution)/shard_map/ppermute | solution.py:26
  200.7 11.6 %collective-permute-start.19 = (bf16[512,1024]{1,0:T(8,128)(2,1)}, bf16[512,1024]{1,0:T(8,128)(2,1)S(1)}, u32[]{:S(2)}, u32[]{:S(2)}) collective-permute-start(bf16[512,1024]{1,0:T(8,128)(2,1)} %add_convert_fusion.9), channel_id=1, source_target_pairs={{0,1},{1,0},{2,3},{3,2},{4,5},{5,4},{6,7},{7,6},{8,9},{9,8},{10,11... | collective-permute-start | bytes 3145736 | tf_op jit(solution)/shard_map/ppermute | solution.py:26
  218.9 6.8 %collective-permute-start.24 = (bf16[512,1024]{1,0:T(8,128)(2,1)}, bf16[512,1024]{1,0:T(8,128)(2,1)}, u32[]{:S(2)}, u32[]{:S(2)}) collective-permute-start(bf16[512,1024]{1,0:T(8,128)(2,1)} %get-tuple-element.97), channel_id=1, source_target_pairs={{0,1},{1,0},{2,3},{3,2},{4,5},{5,4},{6,7},{7,6},{8,9},{9,8},{10,11... | collective-permute-start | bytes 3145736 | tf_op jit(solution)/shard_map/ppermute | solution.py:26
  225.6 188.4 %collective-permute-start.20 = (bf16[512,2,256]{2,0,1:T(8,128)(2,1)}, bf16[512,2,256]{2,0,1:T(8,128)(2,1)}, u32[]{:S(2)}, u32[]{:S(2)}) collective-permute-start(bf16[512,2,256]{2,0,1:T(8,128)(2,1)} %bitcast.153), channel_id=1, source_target_pairs={{0,1},{1,0},{2,3},{3,2},{4,5},{5,4},{6,7},{7,6},{8,9},{9,8},{10,11... | collective-permute-start | bytes 1572872 | tf_op jit(solution)/shard_map/ppermute | solution.py:26
  238.3 111.9 %collective-permute-start.40 = (bf16[1024,512]{1,0:T(8,128)(2,1)}, bf16[1024,512]{1,0:T(8,128)(2,1)}, u32[]{:S(2)}, u32[]{:S(2)}) collective-permute-start(bf16[1024,512]{1,0:T(8,128)(2,1)} %slice.280), channel_id=1, source_target_pairs={{0,4},{4,0},{1,5},{5,1},{2,6},{6,2},{3,7},{7,3},{8,12},{12,8},{9,1... | collective-permute-start | bytes 3145736 | tf_op jit(solution)/shard_map/ppermute | solution.py:35
  239.8 46.9 %collective-permute-start.41 = (bf16[1024,512]{1,0:T(8,128)(2,1)}, bf16[1024,512]{1,0:T(8,128)(2,1)}, u32[]{:S(2)}, u32[]{:S(2)}) collective-permute-start(bf16[1024,512]{1,0:T(8,128)(2,1)} %slice.282), channel_id=1, source_target_pairs={{0,4},{4,0},{1,5},{5,1},{2,6},{6,2},{3,7},{7,3},{8,12},{12,8},{9,1... | collective-permute-start | bytes 3145736 | tf_op jit(solution)/shard_map/ppermute | solution.py:35
  257.1 9.4 %collective-permute-start.25 = (bf16[512,1024]{1,0:T(8,128)(2,1)S(1)}, bf16[512,1024]{1,0:T(8,128)(2,1)S(1)}, u32[]{:S(2)}, u32[]{:S(2)}) collective-permute-start(bf16[512,1024]{1,0:T(8,128)(2,1)S(1)} %add_convert_fusion.7), channel_id=1, source_target_pairs={{0,1},{1,0},{2,3},{3,2},{4,5},{5,4},{6,7},{7,6},{8,9},{9,8},{10,11... | collective-permute-start | bytes 3145736 | tf_op jit(solution)/shard_map/ppermute | solution.py:26
  261.1 96.4 %collective-permute-start.38 = (bf16[1024,1024]{1,0:T(8,128)(2,1)}, bf16[1024,1024]{1,0:T(8,128)(2,1)}, u32[]{:S(2)}, u32[]{:S(2)}) collective-permute-start(bf16[1024,1024]{1,0:T(8,128)(2,1)} %convolution_convert_fusion.2), channel_id=1, source_target_pairs={{0,2},{1,3},{2,0},{3,1},{4,6},{5,7},{6,4},{7,5},{8,10},{9,11},{10,... | collective-permute-start | bytes 6291464 | tf_op jit(solution)/shard_map/ppermute | solution.py:31
  273.6 16.3 %collective-permute-start.26 = (bf16[512,1024]{1,0:T(8,128)(2,1)}, bf16[512,1024]{1,0:T(8,128)(2,1)}, u32[]{:S(2)}, u32[]{:S(2)}) collective-permute-start(bf16[512,1024]{1,0:T(8,128)(2,1)} %get-tuple-element.100), channel_id=1, source_target_pairs={{0,1},{1,0},{2,3},{3,2},{4,5},{5,4},{6,7},{7,6},{8,9},{9,8},{10,11... | collective-permute-start | bytes 3145736 | tf_op jit(solution)/shard_map/ppermute | solution.py:26
  286.7 2.9 collective-permute-start.34
  289.5 62.2 %collective-permute-start.42 = (bf16[1024,512]{1,0:T(8,128)(2,1)}, bf16[1024,512]{1,0:T(8,128)(2,1)}, u32[]{:S(2)}, u32[]{:S(2)}) collective-permute-start(bf16[1024,512]{1,0:T(8,128)(2,1)} %add_convert_fusion.4), channel_id=1, source_target_pairs={{0,2},{1,3},{2,0},{3,1},{4,6},{5,7},{6,4},{7,5},{8,10},{9,11},{10,... | collective-permute-start | bytes 3145736 | tf_op jit(solution)/shard_map/ppermute | solution.py:31
  334.3 38.2 %collective-permute-start.36 = (bf16[256,1024]{1,0:T(8,128)(2,1)}, bf16[256,1024]{1,0:T(8,128)(2,1)}, u32[]{:S(2)}, u32[]{:S(2)}) collective-permute-start(bf16[256,1024]{1,0:T(8,128)(2,1)} %convolution_convert_fusion.5), channel_id=1, source_target_pairs={{0,2},{1,3},{2,0},{3,1},{4,6},{5,7},{6,4},{7,5},{8,10},{9,11},{10,... | collective-permute-start | bytes 1572872 | tf_op jit(solution)/shard_map/ppermute | solution.py:31
  350.2 28.2 %collective-permute-start.29 = (bf16[512,384]{0,1:T(8,128)(2,1)}, bf16[512,384]{0,1:T(8,128)(2,1)S(1)}, u32[]{:S(2)}, u32[]{:S(2)}) collective-permute-start(bf16[512,384]{0,1:T(8,128)(2,1)} %slice.260), channel_id=1, source_target_pairs={{0,4},{4,0},{1,5},{5,1},{2,6},{6,2},{3,7},{7,3},{8,12},{12,8},{9,1... | collective-permute-start | bytes 1179656 | tf_op jit(solution)/shard_map/ppermute | solution.py:35
  351.8 18.1 %collective-permute-start.30 = (bf16[512,384]{0,1:T(8,128)(2,1)}, bf16[512,384]{0,1:T(8,128)(2,1)S(1)}, u32[]{:S(2)}, u32[]{:S(2)}) collective-permute-start(bf16[512,384]{0,1:T(8,128)(2,1)} %slice.262), channel_id=1, source_target_pairs={{0,4},{4,0},{1,5},{5,1},{2,6},{6,2},{3,7},{7,3},{8,12},{12,8},{9,1... | collective-permute-start | bytes 1179656 | tf_op jit(solution)/shard_map/ppermute | solution.py:35
  357.5 20.5 %collective-permute-start.32 = (bf16[1024,384]{0,1:T(8,128)(2,1)S(1)}, bf16[1024,384]{0,1:T(8,128)(2,1)S(1)}, u32[]{:S(2)}, u32[]{:S(2)}) collective-permute-start(bf16[1024,384]{0,1:T(8,128)(2,1)S(1)} %slice.264), channel_id=1, source_target_pairs={{0,2},{1,3},{2,0},{3,1},{4,6},{5,7},{6,4},{7,5},{8,10},{9,11},{10,... | collective-permute-start | bytes 2359304 | tf_op jit(solution)/shard_map/ppermute | solution.py:31
  369.9 32.5 %collective-permute-start.39 = (bf16[512,1024]{1,0:T(8,128)(2,1)S(1)}, bf16[512,1024]{1,0:T(8,128)(2,1)S(1)}, u32[]{:S(2)}, u32[]{:S(2)}) collective-permute-start(bf16[512,1024]{1,0:T(8,128)(2,1)S(1)} %slice.277), channel_id=1, source_target_pairs={{0,4},{4,0},{1,5},{5,1},{2,6},{6,2},{3,7},{7,3},{8,12},{12,8},{9,1... | collective-permute-start | bytes 3145736 | tf_op jit(solution)/shard_map/ppermute | solution.py:35
  372.5 12.3 %collective-permute-start.31 = (bf16[512,384]{0,1:T(8,128)(2,1)S(1)}, bf16[512,384]{0,1:T(8,128)(2,1)S(1)}, u32[]{:S(2)}, u32[]{:S(2)}) collective-permute-start(bf16[512,384]{0,1:T(8,128)(2,1)S(1)} %add_convert_fusion.14), channel_id=1, source_target_pairs={{0,2},{1,3},{2,0},{3,1},{4,6},{5,7},{6,4},{7,5},{8,10},{9,11},{10,... | collective-permute-start | bytes 1179656 | tf_op jit(solution)/shard_map/ppermute | solution.py:31
  378.0 35.6 %collective-permute-start.27 = (bf16[1024,2,256]{2,0,1:T(8,128)(2,1)S(1)}, bf16[1024,2,256]{2,0,1:T(8,128)(2,1)S(1)}, u32[]{:S(2)}, u32[]{:S(2)}) collective-permute-start(bf16[1024,2,256]{2,0,1:T(8,128)(2,1)S(1)} %bitcast.160), channel_id=1, source_target_pairs={{0,1},{1,0},{2,3},{3,2},{4,5},{5,4},{6,7},{7,6},{8,9},{9,8},{10,11... | collective-permute-start | bytes 3145736 | tf_op jit(solution)/shard_map/ppermute | solution.py:26
  378.4 23.2 %collective-permute-start.37 = (bf16[256,512]{1,0:T(8,128)(2,1)S(1)}, bf16[256,512]{1,0:T(8,128)(2,1)S(1)}, u32[]{:S(2)}, u32[]{:S(2)}) collective-permute-start(bf16[256,512]{1,0:T(8,128)(2,1)S(1)} %slice.275), channel_id=1, source_target_pairs={{0,4},{4,0},{1,5},{5,1},{2,6},{6,2},{3,7},{7,3},{8,12},{12,8},{9,1... | collective-permute-start | bytes 786440 | tf_op jit(solution)/shard_map/ppermute | solution.py:35
  384.8 23.3 %collective-permute-start.33 = (bf16[512,384]{0,1:T(8,128)(2,1)S(1)}, bf16[512,384]{0,1:T(8,128)(2,1)S(1)}, u32[]{:S(2)}, u32[]{:S(2)}) collective-permute-start(bf16[512,384]{0,1:T(8,128)(2,1)S(1)} %slice.266), channel_id=1, source_target_pairs={{0,4},{4,0},{1,5},{5,1},{2,6},{6,2},{3,7},{7,3},{8,12},{12,8},{9,1... | collective-permute-start | bytes 1179656 | tf_op jit(solution)/shard_map/ppermute | solution.py:35
  409.3 8.9 %collective-permute-start.35 = (f32[3072]{0:T(1024)S(1)}, f32[3072]{0:T(1024)S(1)}, u32[]{:S(2)}, u32[]{:S(2)}) collective-permute-start(f32[3072]{0:T(1024)S(1)} %pad_maximum_fusion.14), channel_id=1, source_target_pairs={{0,2},{1,3},{2,0},{3,1},{4,6},{5,7},{6,4},{7,5},{8,10},{9,11},{10,... | collective-permute-start | bytes 36872 | tf_op jit(solution)/shard_map/ppermute | solution.py:31
  416.4 43.6 %collective-permute-start.28 = (bf16[1024,256]{1,0:T(8,128)(2,1)S(1)}, bf16[1024,256]{1,0:T(8,128)(2,1)S(1)}, u32[]{:S(2)}, u32[]{:S(2)}) collective-permute-start(bf16[1024,256]{1,0:T(8,128)(2,1)S(1)} %select_bitcast_fusion.2), channel_id=1, source_target_pairs={{0,2},{1,3},{2,0},{3,1},{4,6},{5,7},{6,4},{7,5},{8,10},{9,11},{10,... | collective-permute-start | bytes 1572872 | tf_op jit(solution)/shard_map/ppermute | solution.py:31
  459.2 9.2 %collective-permute-start.21 = (bf16[1024,256]{1,0:T(8,128)(2,1)S(1)}, bf16[1024,256]{1,0:T(8,128)(2,1)S(1)}, u32[]{:S(2)}, u32[]{:S(2)}) collective-permute-start(bf16[1024,256]{1,0:T(8,128)(2,1)S(1)} %select_bitcast_fusion.5), channel_id=1, source_target_pairs={{0,2},{1,3},{2,0},{3,1},{4,6},{5,7},{6,4},{7,5},{8,10},{9,11},{10,... | collective-permute-start | bytes 1572872 | tf_op jit(solution)/shard_map/ppermute | solution.py:31
  (74 other events, 479.3 us)
Sparse Core Ops, SparseCore 0:
  409.3 123.0 all-reduce.2

commit v2 on v1

v2 whole, which is shorter than its diff:
```python
import functools
import math

import jax
import jax.numpy as jnp
from jax import lax
from jax.experimental import pallas as pl
from jax.experimental.pallas import tpu as pltpu
from jax.sharding import PartitionSpec as P

HEAD_DIM = 64
epsilon = 1e-12
f32 = jnp.float32
bf16 = jnp.bfloat16
NT = (((1,), (1,)), ((), ()))
NN = (((1,), (0,)), ((), ()))
TN = (((0,), (0,)), ((), ()))


QUICK = pl.CostEstimate(flops=1024, bytes_accessed=1024, transcendentals=0)


def mm(left, right, dims=NN):
    return lax.dot_general(left, right, dims, preferred_element_type=f32)


def to_core(values):
    size = lax.axis_size("col")
    return lax.ppermute(values, "col", [(i, i ^ 1) for i in range(size)])


def to_chip(values):
    size = lax.axis_size("col")
    return lax.ppermute(values, "col", [(i, i ^ 2) for i in range(size)])


def to_row(values):
    return lax.ppermute(values, "row", [(0, 1), (1, 0)])


def attend_kernel(chunk, wide_ref, left_ref, right_ref, bias_ref, mask_ref, qkv_ref, exp_ref, mixed_ref, inv_ref):
    count, side = wide_ref.shape[0], left_ref.shape[0]
    projected = mm(wide_ref[:, :side], left_ref[...]) + mm(wide_ref[:, side:], right_ref[...])
    qkv_ref[...] = (projected + bias_ref[...]).astype(bf16)
    ones = jnp.ones((count, HEAD_DIM), bf16)
    for head in range(2):
        base = 3 * HEAD_DIM * head
        cols = slice(head * HEAD_DIM, (head + 1) * HEAD_DIM)
        query = qkv_ref[:, base : base + HEAD_DIM] * bf16(1.0 / math.sqrt(HEAD_DIM))
        key = qkv_ref[:, base + HEAD_DIM : base + 2 * HEAD_DIM]
        value = qkv_ref[:, base + 2 * HEAD_DIM : base + 3 * HEAD_DIM]
        query = jnp.concatenate([query, mask_ref[:, :HEAD_DIM]], axis=1)
        key = jnp.concatenate([key, mask_ref[:, HEAD_DIM:]], axis=1)
        value = jnp.concatenate([value, ones], axis=1)
        for start in range(0, count, chunk):
            rows = slice(start, start + chunk)
            scores = mm(query[rows], key, NT)
            top = jnp.max(scores, axis=-1, keepdims=True)
            exponent = jnp.exp(scores - top).astype(bf16)
            exp_ref[head, rows, :] = exponent
            mixed = mm(exponent, value)
            inverse = 1.0 / mixed[:, HEAD_DIM:]
            mixed_ref[rows, cols] = (mixed[:, :HEAD_DIM] * inverse).astype(bf16)
            inv_ref[rows, cols] = inverse


def attend(wide, left, right, bias, mask):
    count, model = wide.shape
    side, width = left.shape
    six = 6 * HEAD_DIM
    pairs = width // six
    return pl.pallas_call(
        functools.partial(attend_kernel, min(512, count)),
        grid=(pairs,),
        in_specs=[
            pl.BlockSpec((count, model), lambda p: (0, 0)),
            pl.BlockSpec((side, six), lambda p: (0, p)),
            pl.BlockSpec((side, six), lambda p: (0, p)),
            pl.BlockSpec((1, six), lambda p: (0, p)),
            pl.BlockSpec((count, 2 * HEAD_DIM), lambda p: (0, 0)),
        ],
        out_specs=[
            pl.BlockSpec((count, six), lambda p: (0, p)),
            pl.BlockSpec((2, count, count), lambda p: (p, 0, 0)),
            pl.BlockSpec((count, 2 * HEAD_DIM), lambda p: (0, p)),
            pl.BlockSpec((count, 2 * HEAD_DIM), lambda p: (0, p)),
        ],
        out_shape=[
            jax.ShapeDtypeStruct((count, width), bf16),
            jax.ShapeDtypeStruct((2 * pairs, count, count), bf16),
            jax.ShapeDtypeStruct((count, 2 * HEAD_DIM * pairs), bf16),
            jax.ShapeDtypeStruct((count, 2 * HEAD_DIM * pairs), f32),
        ],
        compiler_params=pltpu.CompilerParams(vmem_limit_bytes=52 * 2**20),
        cost_estimate=QUICK,
        name="attend",
    )(wide, left, right, bias.reshape(1, width), mask)


def attend_back_kernel(chunk, qkv_ref, exp_ref, mixed_ref, inv_ref, grad_ref, out_ref):
    count = qkv_ref.shape[0]
    lane = lax.broadcasted_iota(jnp.int32, (count, HEAD_DIM), 1)
    minus = jnp.where(lane < 2, -1.0, 0.0).astype(bf16)
    scale = 1.0 / math.sqrt(HEAD_DIM)
    for head in range(2):
        base = 3 * HEAD_DIM * head
        cols = slice(head * HEAD_DIM, (head + 1) * HEAD_DIM)
        query = qkv_ref[:, base : base + HEAD_DIM]
        key = qkv_ref[:, base + HEAD_DIM : base + 2 * HEAD_DIM]
        value = qkv_ref[:, base + 2 * HEAD_DIM : base + 3 * HEAD_DIM]
        value = jnp.concatenate([value, minus], axis=1)
        scaled = grad_ref[:, cols].astype(f32) * inv_ref[:, cols]
        scaled_low = scaled.astype(bf16)
        inner = jnp.sum(scaled * mixed_ref[:, cols].astype(f32), axis=1, keepdims=True)
        inner_high = inner.astype(bf16).astype(f32)
        inner_pair = jnp.where(
            lane == 0, inner_high, jnp.where(lane == 1, inner - inner_high, 0.0)
        ).astype(bf16)
        wide = jnp.concatenate([scaled_low, inner_pair], axis=1)
        grad_key = grad_value = None
        for start in range(0, count, chunk):
            rows = slice(start, start + chunk)
            exponent = exp_ref[head, rows, :]
            grad_probs = mm(wide[rows], value, NT)
            grad_scores = (exponent.astype(f32) * grad_probs).astype(bf16)
            out_ref[rows, base : base + HEAD_DIM] = (mm(grad_scores, key) * scale).astype(bf16)
            key_part = mm(query[rows], grad_scores, TN)
            value_part = mm(scaled_low[rows], exponent, TN)
            grad_key = key_part if grad_key is None else grad_key + key_part
            grad_value = value_part if grad_value is None else grad_value + value_part
        out_ref[:, base + HEAD_DIM : base + 2 * HEAD_DIM] = (grad_key.T * scale).astype(bf16)
        out_ref[:, base + 2 * HEAD_DIM : base + 3 * HEAD_DIM] = grad_value.T.astype(bf16)


def attend_back(qkv, exponent, mixed, inverse, grad_mixed):
    count, width = qkv.shape
    pairs = width // (6 * HEAD_DIM)
    return pl.pallas_call(
        functools.partial(attend_back_kernel, min(512, count)),
        grid=(pairs,),
        in_specs=[
            pl.BlockSpec((count, 6 * HEAD_DIM), lambda p: (0, p)),
            pl.BlockSpec((2, count, count), lambda p: (p, 0, 0)),
        ]
        + [pl.BlockSpec((count, 2 * HEAD_DIM), lambda p: (0, p))] * 3,
        out_specs=pl.BlockSpec((count, 6 * HEAD_DIM), lambda p: (0, p)),
        out_shape=jax.ShapeDtypeStruct((count, width), bf16),
        compiler_params=pltpu.CompilerParams(vmem_limit_bytes=48 * 2**20),
        cost_estimate=QUICK,
        name="attend_back",
    )(qkv, exponent, mixed, inverse, grad_mixed)


def centre(values):
    centered = values - jnp.mean(values, axis=-1, keepdims=True)
    inverse = lax.rsqrt(jnp.mean(centered * centered, axis=-1, keepdims=True) + epsilon)
    return centered * inverse, inverse


def centre_back(grad, normed, inverse):
    return inverse * (
        grad
        - jnp.mean(grad, axis=-1, keepdims=True)
        - normed * jnp.mean(grad * normed, axis=-1, keepdims=True)
    )


def keep_sums(sums_ref, *values):
    @pl.when(pl.program_id(0) == 0)
    def _():
        sums_ref[...] = jnp.zeros_like(sums_ref)

    for i, value in enumerate(values):
        sums_ref[i : i + 1, :] += jnp.sum(value, axis=0, keepdims=True)


def norm_one_kernel(flags, vec_ref, tokens_ref, own_ref, arrived_ref, normed_ref, inv_ref, first_ref, low_ref):
    values = tokens_ref[...].astype(f32) + own_ref[...] + arrived_ref[...].astype(f32) + vec_ref[0:1, :]
    normed, inverse = centre(values)
    first = normed * vec_ref[1:2, :] + vec_ref[2:3, :]
    normed_ref[...] = normed
    inv_ref[...] = jnp.broadcast_to(inverse, inv_ref.shape)
    first_ref[...] = first
    low_ref[...] = first.astype(bf16)


def norm_two_kernel(
    flags, vec_ref, first_ref, own_ref, arrived_ref, cot_ref, keep_ref, give_ref, grad_ref, low_ref, sums_ref
):
    core = flags[1]
    values = first_ref[...] + own_ref[...] + arrived_ref[...].astype(f32) + vec_ref[3:4, :]
    normed, inverse = centre(values)
    output = (normed * vec_ref[4:5, :] + vec_ref[5:6, :]).astype(bf16)
    width = output.shape[1] // 4
    for part in range(2):
        even = output[:, 2 * part * width : (2 * part + 1) * width]
        odd = output[:, (2 * part + 1) * width : (2 * part + 2) * width]
        cols = slice(part * width, (part + 1) * width)
        keep_ref[:, cols] = jnp.where(core == 0, even, odd)
        give_ref[:, cols] = jnp.where(core == 0, odd, even)
    cot = cot_ref[...].astype(f32)
    grad = centre_back(cot * vec_ref[4:5, :], normed, inverse)
    low = grad.astype(bf16)
    grad_ref[...] = grad
    low_ref[...] = low
    keep_sums(sums_ref, cot * normed, cot, low.astype(f32))


def norm_back_kernel(
    flags, vec_ref, above_ref, own_ref, arrived_ref, normed_ref, inv_ref, grad_ref, low_ref, sums_ref
):
    normed = normed_ref[...]
    above = above_ref[...] + own_ref[...] + arrived_ref[...].astype(f32)
    grad = centre_back(above * vec_ref[1:2, :], normed, inv_ref[:, :1])
    low = grad.astype(bf16)
    grad_ref[...] = grad
    low_ref[...] = low
    keep_sums(sums_ref, above * normed, above, low.astype(f32))


def by_rows(kernel, flags, vec, operands, outs, name):
    rows, model = operands[1].shape
    tile = min(128, rows)

    def spec(width):
        return pl.BlockSpec((tile, width), lambda i, f: (i, 0))

    shapes = [
        jax.ShapeDtypeStruct((rows, width) if width else (8, model), dtype) for width, dtype in outs
    ]
    return pl.pallas_call(
        kernel,
        grid_spec=pltpu.PrefetchScalarGridSpec(
            num_scalar_prefetch=1,
            grid=(rows // tile,),
            in_specs=[pl.BlockSpec(vec.shape, lambda i, f: (0, 0))] + [spec(o.shape[1]) for o in operands],
            out_specs=[
                spec(width) if width else pl.BlockSpec((8, model), lambda i, f: (0, 0))
                for width, _ in outs
            ],
        ),
        out_shape=shapes,
        compiler_params=pltpu.CompilerParams(vmem_limit_bytes=40 * 2**20),
        cost_estimate=QUICK,
        name=name,
    )(flags, vec, *operands)


def feed_kernel(wide_ref, left_ref, right_ref, bias_ref, act_ref, slope_ref):
    side = left_ref.shape[0]
    pre = mm(wide_ref[:, :side], left_ref[...]) + mm(wide_ref[:, side:], right_ref[...]) + bias_ref[...]
    cdf = 0.5 * (1.0 + lax.erf(pre * (1.0 / math.sqrt(2.0))))
    pdf = jnp.exp(-0.5 * pre * pre) * (1.0 / math.sqrt(2.0 * math.pi))
    act_ref[...] = (pre * cdf).astype(bf16)
    slope_ref[...] = (cdf + pre * pdf).astype(bf16)


def feed(wide, left, right, bias):
    count, model = wide.shape
    side, width = left.shape
    tile = min(256, width)
    cols = lambda rows: pl.BlockSpec((rows, tile), lambda i: (0, i))
    return pl.pallas_call(
        feed_kernel,
        grid=(width // tile,),
        in_specs=[pl.BlockSpec((count, model), lambda i: (0, 0)), cols(side), cols(side), cols(1)],
        out_specs=[cols(count), cols(count)],
        out_shape=[jax.ShapeDtypeStruct((count, width), bf16)] * 2,
        compiler_params=pltpu.CompilerParams(vmem_limit_bytes=40 * 2**20),
        cost_estimate=QUICK,
        name="feed",
    )(wide, left, right, bias.reshape(1, width))


def feed_back_kernel(grad_ref, left_ref, right_ref, slope_ref, out_ref, sums_ref):
    side = left_ref.shape[1]
    product = mm(grad_ref[:, :side], left_ref[...], NT) + mm(grad_ref[:, side:], right_ref[...], NT)
    low = (product * slope_ref[...].astype(f32)).astype(bf16)
    out_ref[...] = low
    sums_ref[...] = jnp.sum(low.astype(f32), axis=0, keepdims=True)


def feed_back(grad, left, right, slope):
    count, model = grad.shape
    width, side = left.shape
    tile = min(256, width)
    cols = lambda rows: pl.BlockSpec((rows, tile), lambda i: (0, i))
    rows = pl.BlockSpec((tile, side), lambda i: (i, 0))
    return pl.pallas_call(
        feed_back_kernel,
        grid=(width // tile,),
        in_specs=[pl.BlockSpec((count, model), lambda i: (0, 0)), rows, rows, cols(count)],
        out_specs=[cols(count), cols(1)],
        out_shape=[jax.ShapeDtypeStruct((count, width), bf16), jax.ShapeDtypeStruct((1, width), f32)],
        compiler_params=pltpu.CompilerParams(vmem_limit_bytes=40 * 2**20),
        cost_estimate=QUICK,
        name="feed_back",
    )(grad, left, right, slope)


def weight_kernel(other_ref, mine_ref, right_ref, away_ref, own_ref, other_out, mine_out):
    step, part = pl.program_id(0), pl.num_programs(0) // 4
    side = own_ref.shape[1]

    def product(ref):
        return mm(ref[...], right_ref[...], TN).astype(bf16)

    def split(ref):
        value = product(ref)
        own_ref[...] = value[:, :side]
        away_ref[...] = value[:, side:]

    @pl.when(step < part)
    def _():
        split(other_ref)

    @pl.when((step >= part) & (step < 2 * part))
    def _():
        other_out[...] = product(other_ref)

    @pl.when((step >= 2 * part) & (step < 3 * part))
    def _():
        split(mine_ref)

    @pl.when(step >= 3 * part)
    def _():
        mine_out[...] = product(mine_ref)


def weight_grads(other, mine, right):
    count, width = other.shape
    model = right.shape[1]
    side = model // 2
    tile = min(256, width // 2)
    n = width // tile
    p = n // 2

    def stacked(i):
        return jnp.where(i < p, i, jnp.where(i < 2 * p, p - 1, jnp.minimum(i - p, 2 * p - 1)))

    return pl.pallas_call(
        weight_kernel,
        grid=(2 * n,),
        in_specs=[
            pl.BlockSpec((count, tile), lambda i: (0, jnp.minimum(i, n - 1))),
            pl.BlockSpec((count, tile), lambda i: (0, jnp.maximum(i - n, 0))),
            pl.BlockSpec((count, model), lambda i: (0, 0)),
        ],
        out_specs=[
            pl.BlockSpec((tile, side), lambda i: (stacked(i), 0)),
            pl.BlockSpec((tile, side), lambda i: (stacked(i), 0)),
            pl.BlockSpec((tile, model), lambda i: (jnp.clip(i - p, 0, p - 1), 0)),
            pl.BlockSpec((tile, model), lambda i: (jnp.clip(i - 3 * p, 0, p - 1), 0)),
        ],
        out_shape=[jax.ShapeDtypeStruct((width, side), bf16)] * 2
        + [jax.ShapeDtypeStruct((width // 2, model), bf16)] * 2,
        compiler_params=pltpu.CompilerParams(vmem_limit_bytes=40 * 2**20),
        cost_estimate=QUICK,
        name="weight_grads",
    )(other, mine, right)


def transposed_kernel(left_ref, right_ref, out_ref):
    out_ref[...] = mm(left_ref[...], right_ref[...], TN).astype(bf16)


def transposed(left, right):
    count, width = left.shape
    model = right.shape[1]
    tile = 384 if width % 384 == 0 else min(256, width)
    return pl.pallas_call(
        transposed_kernel,
        grid=(width // tile,),
        in_specs=[
            pl.BlockSpec((count, tile), lambda i: (0, i)), pl.BlockSpec((count, model), lambda i: (0, 0))
        ],
        out_specs=pl.BlockSpec((tile, model), lambda i: (i, 0)),
        out_shape=jax.ShapeDtypeStruct((width, model), bf16),
        compiler_params=pltpu.CompilerParams(vmem_limit_bytes=40 * 2**20),
        cost_estimate=QUICK,
        name="transposed",
    )(left, right)


def placed(kernel, flags, operands, shapes, name):
    return pl.pallas_call(
        kernel,
        grid_spec=pltpu.PrefetchScalarGridSpec(
            num_scalar_prefetch=1,
            grid=(1,),
            in_specs=[pl.BlockSpec(o.shape, lambda i, f, n=o.ndim: (0,) * n) for o in operands],
            out_specs=[pl.BlockSpec(s.shape, lambda i, f, n=len(s.shape): (0,) * n) for s in shapes],
        ),
        out_shape=shapes,
        compiler_params=pltpu.CompilerParams(vmem_limit_bytes=40 * 2**20),
        cost_estimate=QUICK,
        name=name,
    )(flags, *operands)


def block(index, size):
    return pl.ds(pl.multiple_of(index * size, size), size)


def join_wide_kernel(flags, mine_ref, near_ref, core_mine_ref, core_near_ref, out_ref):
    chip, core, place = flags[0], flags[1], flags[2]
    width, half = near_ref.shape[1], near_ref.shape[0] // 2
    own, away = block(core, half), block(1 - core, half)
    mine_at, near_at = 2 * place, 2 * (1 - place)
    for at, ref in ((mine_at + 1 - core, core_mine_ref), (near_at + core, near_ref), (near_at + 1 - core, core_near_ref)):
        out_ref[:half, block(at, width)] = ref[own, :]
        out_ref[half:, block(at, width)] = ref[away, :]
    out_ref[:half, block(mine_at + core, width)] = mine_ref[chip, own, :]
    out_ref[half:, block(mine_at + core, width)] = mine_ref[chip, away, :]


def give_core_kernel(flags, mine_ref, near_ref, out_ref):
    chip, core = flags[0], flags[1]
    width, half = near_ref.shape[1], near_ref.shape[0] // 2
    away = block(1 - core, half)
    out_ref[:, :width] = mine_ref[chip, away, :]
    out_ref[:, width:] = near_ref[away, :]


def join_own_kernel(flags, mine_ref, near_ref, core_ref, out_ref):
    chip, core, place = flags[0], flags[1], flags[2]
    width, half = near_ref.shape[1], near_ref.shape[0] // 2
    own = block(core, half)
    mine_at, near_at = 2 * place, 2 * (1 - place)
    out_ref[:, block(mine_at + core, width)] = mine_ref[chip, own, :]
    out_ref[:, block(near_at + core, width)] = near_ref[own, :]
    out_ref[:, block(mine_at + 1 - core, width)] = core_ref[:, :width]
    out_ref[:, block(near_at + 1 - core, width)] = core_ref[:, width:]


def split_core_kernel(flags, in_ref, keep_ref, send_ref):
    core = flags[1]
    width = in_ref.shape[1] // 4
    for part in range(2):
        cols = slice(part * width, (part + 1) * width)
        keep_ref[:, cols] = in_ref[:, block(2 * part + core, width)].astype(keep_ref.dtype)
        send_ref[:, cols] = in_ref[:, block(2 * part + 1 - core, width)].astype(send_ref.dtype)


def split_chip_kernel(flags, own_ref, away_ref, keep_ref, send_ref):
    core, place = flags[1], flags[2]
    half, width = own_ref.shape[0], own_ref.shape[1] // 2
    for rows, ref in ((block(core, half), own_ref), (block(1 - core, half), away_ref)):
        keep_ref[rows, :] = ref[:, block(place, width)]
        send_ref[rows, :] = ref[:, block(1 - place, width)]


def add_split_chip_kernel(flags, here_ref, there_ref, keep_ref, send_ref):
    core, place = flags[1], flags[2]
    half, width = here_ref.shape[0] // 2, here_ref.shape[1] // 2
    for rows, here, there in (
        (block(core, half), slice(0, half), slice(half, None)),
        (block(1 - core, half), slice(half, None), slice(0, half)),
    ):
        for ref, at in ((keep_ref, place), (send_ref, 1 - place)):
            cols = block(at, width)
            ref[rows, :] = (here_ref[here, cols] + there_ref[there, cols].astype(f32)).astype(bf16)


def join_sequences_kernel(flags, keep_ref, near_ref, out_ref):
    chip = flags[0]
    out_ref[chip] = keep_ref[...]
    out_ref[1 - chip] = near_ref[...]


def pick(values, index, axis=0):
    return lax.dynamic_index_in_dim(values, index, axis, keepdims=False)


def after(values, *others):
    return lax.optimization_barrier((values, *others))[0]


def hold(values, *arrived):
    return lax.optimization_barrier((values, *arrived))


def added(own, arrived):
    return (own.astype(f32) + arrived.astype(f32)).astype(bf16)


class PairSum:
    def __init__(self, values):
        self.values = values
        self.size = lax.axis_size("dp")
        self.index = lax.axis_index("dp")
        self.undo = []
        self.todo = []
        rows, bit = values.shape[0], 1
        while self.size & (self.size - 1) == 0 and bit < self.size and rows % 32 == 0:
            self.todo.append(("halve", bit))
            rows, bit = rows // 2, bit * 2
        if bit < self.size:
            self.todo.append(("rest", bit))
        self.todo += [("double", b) for kind, b in reversed(self.todo) if kind == "halve"]

    def send(self):
        kind, bit = self.todo[0]
        pairs = [(i, i ^ bit) for i in range(self.size)]
        upper = (self.index & bit) != 0
        if kind == "halve":
            rows = self.values.shape[0] // 2
            low, high = self.values[:rows], self.values[rows:]
            self.values, give = jnp.where(upper, high, low), jnp.where(upper, low, high)
            self.arrived = lax.ppermute(give, "dp", pairs)
        elif kind == "double":
            self.arrived = lax.ppermute(self.values, "dp", pairs)
        else:
            groups = [[i + bit * j for j in range(self.size // bit)] for i in range(bit)]
            self.arrived = lax.psum(self.values, "dp", axis_index_groups=groups)

    def receive(self):
        kind, bit = self.todo.pop(0)
        upper = (self.index & bit) != 0
        if kind == "halve":
            self.values = added(self.values, self.arrived)
        elif kind == "double":
            pair = (self.arrived, self.values), (self.values, self.arrived)
            self.values = jnp.where(upper, jnp.concatenate(pair[0]), jnp.concatenate(pair[1]))
        else:
            self.values = self.arrived

    def step(self, *others):
        if not self.todo:
            return others
        self.arrived, *others = hold(self.arrived, *others)
        self.receive()
        if self.todo:
            self.send()
        return others

    def finish(self):
        while self.todo:
            self.step()
        return self.values


def body(
    tokens, segments, w_qkv, qv_bias, w_out, out_bias, gain_one, shift_one,
    w_in, in_bias, w_down, down_bias, gain_two, shift_two, cotangent,
):
    row = lax.axis_index("row")
    col = lax.axis_index("col")
    chip, core = col // 2, col % 2
    same = row == chip
    first_core = core == 0
    flags = jnp.stack([chip, core, jnp.where(same, 0, 1)]).astype(jnp.int32)
    seq_count, count, width = tokens.shape
    half = count // 2
    model = width * lax.axis_size("col")
    heads = qv_bias.shape[0] // (2 * HEAD_DIM)
    hidden = in_bias.shape[0]
    cut, mid = 3 * heads * HEAD_DIM // 2, hidden // 2

    def shape(*dims, dtype=bf16):
        return jax.ShapeDtypeStruct(dims, dtype)

    qv_pairs = qv_bias.reshape(heads, 2, HEAD_DIM)
    qkv_bias = jnp.stack(
        [qv_pairs[:, 0], jnp.zeros_like(qv_pairs[:, 0]), qv_pairs[:, 1]], axis=1
    ).reshape(-1)
    vectors = jnp.concatenate([out_bias, gain_one, shift_one, down_bias, gain_two, shift_two])
    small = jnp.concatenate([vectors, qkv_bias, in_bias])
    small_near = to_chip(small)

    near = to_chip(pick(tokens, 1 - chip))
    qkv_row = to_row(w_qkv)
    core_mine = to_core(pick(tokens, chip))
    core_near = to_core(near)
    wide = placed(
        join_wide_kernel, flags, [tokens, near, core_mine, core_near], [shape(count, model)], "join_wide"
    )[0]

    segment = pick(segments, chip).reshape(2, half)
    segment = jnp.concatenate([pick(segment, core), pick(segment, 1 - core)])
    ids = jnp.arange(HEAD_DIM)
    differs = jnp.where((segment[:, None] != ids) & (ids < 3), -(2.0**30), 0.0)
    mask = jnp.concatenate([differs, segment[:, None] == ids], axis=1).astype(bf16)

    qkv_own = after(w_qkv, near)
    near_a, near_b = to_chip(qkv_own[:, :cut]), to_chip(qkv_own[:, cut:])
    far_a = to_row(near_a)
    wide, small_near, qkv_row = hold(wide, small_near, qkv_row)
    far_b = to_chip(qkv_row[:, cut:])
    out_row = to_row(after(w_out, wide))
    in_row = to_row(after(w_in, wide))
    mine = attend(wide, w_qkv, qkv_row, qkv_bias, mask)
    qkv_bias_near = small_near[6 * width : 6 * width + 2 * cut]
    wide_a, near_b, far_a, far_b, out_row = hold(after(wide, mine[0]), near_b, far_a, far_b, out_row)
    out_near = to_chip(after(w_out, out_row))
    out_far = to_chip(out_row)
    in_near = to_chip(after(w_in, out_row))
    down_row = to_row(after(w_down, out_row))
    other_a = attend(wide_a, near_a, far_a, qkv_bias_near[:cut], mask)
    wide_b, out_near, out_far, in_row = hold(after(wide, other_a[0]), out_near, out_far, in_row)
    down_near = to_chip(after(w_down, out_near))
    other_b = attend(wide_b, near_b, far_b, qkv_bias_near[cut:], mask)
    parts = [mine, other_a, other_b]
    lefts = [w_qkv, near_a, near_b]
    rights = [qkv_row, far_a, far_b]
    mixed = [mine[2], jnp.concatenate([other_a[2], other_b[2]], axis=1)]
    w_outs = [
        jnp.concatenate([w_out, out_row], axis=1), jnp.concatenate([out_near, out_far], axis=1)
    ]

    vec = vectors.reshape(6, width)
    vec_near = small_near[: 6 * width].reshape(6, width)
    low, high = jnp.where(same, vec, vec_near), jnp.where(same, vec_near, vec)
    both = jnp.concatenate([low, high], axis=1)
    there = to_core(after(both, mine[0]))
    even, odd = jnp.where(first_core, both, there), jnp.where(first_core, there, both)
    wide_vec = jnp.concatenate(
        [even[:, :width], odd[:, :width], even[:, width:], odd[:, width:]], axis=1
    )
    wide_vec = jnp.concatenate([wide_vec, jnp.zeros((2, model), f32)], axis=0)
    in_biases = [in_bias, small_near[6 * width + 2 * cut :]]

    def core_gather(values):
        return jnp.concatenate([values, to_core(values)], axis=0)

    arrived = to_core(sum(mm(m[half:], w) for m, w in zip(mixed, w_outs)).astype(bf16))
    own = sum(mm(m[:half], w) for m, w in zip(mixed, w_outs))
    normed_one, inverse_one, first_out, first_low = by_rows(
        norm_one_kernel, flags, wide_vec, [wide[:half], own, arrived],
        [(model, f32), (128, f32), (model, f32), (model, bf16)], "norm_one",
    )
    first_wide = core_gather(first_low)

    first_wide, in_near = hold(first_wide, in_near)
    in_far = to_row(in_near)
    act_mine, slope_mine = feed(first_wide, w_in, in_row, in_biases[0])
    down_mine = jnp.concatenate([w_down, down_row], axis=1)
    down_far_a = to_chip(down_row[:mid])
    ffn_mine = [mm(act_mine[half:], down_mine), mm(act_mine[:half], down_mine)]
    cot_near = to_chip(after(pick(cotangent, 1 - chip), down_row))
    down_near, *ffn_mine = hold(down_near, *ffn_mine)
    down_far_b = to_row(down_near[mid:])
    act_other, slope_other = feed(after(first_wide, down_near), in_near, in_far, in_biases[1])
    down_far = jnp.concatenate([down_far_a, down_far_b], axis=0)
    down_other = jnp.concatenate([down_near, down_far], axis=1)
    arrived = to_core((ffn_mine[0] + mm(act_other[half:], down_other)).astype(bf16))
    own = ffn_mine[1] + mm(act_other[:half], down_other)
    cot_give = placed(give_core_kernel, flags, [cotangent, cot_near], [shape(half, 2 * width)], "give_core")[0]
    cot_core = to_core(cot_give)
    cot = placed(
        join_own_kernel, flags, [cotangent, cot_near, cot_core], [shape(half, model)], "join_own"
    )[0]
    out_keep, out_give, grad_pre_two, grad_ffn, sums_two = by_rows(
        norm_two_kernel, flags, wide_vec, [first_out, own, arrived, cot],
        [(2 * width, bf16), (2 * width, bf16), (model, f32), (model, bf16), (0, f32)], "norm_two",
    )

    side = model // 2

    def second_sends(own_a, arrived_a, mine_b, arrived_b):
        size = own_a.shape[0] // 2
        sum_a, sum_b = added(own_a, arrived_a), added(mine_b, arrived_b)
        return (sum_a[size:], to_chip(sum_a[:size])), (sum_b[:, :side], to_row(sum_b[:, side:]))

    gw = core_gather(grad_ffn)
    down_away_a, down_own_a, down_other_b, down_mine_b = weight_grads(act_other, act_mine, gw)
    down_first = [to_row(down_away_a), to_chip(down_other_b)]
    hid_mine, in_sum_mine = feed_back(gw, w_down, down_row, slope_mine)
    hid_other, in_sum_other = feed_back(gw, down_near, down_far, slope_other)
    grad_in_biases = [in_sum_mine[0], in_sum_other[0]]
    in_mine = jnp.concatenate([w_in, in_row], axis=0)
    in_other = jnp.concatenate([in_near, in_far], axis=0)
    arrived = to_core((mm(hid_mine[half:], in_mine, NT) + mm(hid_other[half:], in_other, NT)).astype(bf16))
    own = mm(hid_mine[:half], in_mine, NT) + mm(hid_other[:half], in_other, NT)
    in_away_a, in_own_a, in_other_b, in_mine_b = weight_grads(hid_other, hid_mine, first_wide)
    own, arrived, *down_first = hold(own, arrived, *down_first)
    (da, da_near), (db, db_row) = second_sends(down_own_a, down_first[0], down_mine_b, down_first[1])
    in_first = [to_row(after(in_away_a, da)), to_chip(after(in_other_b, db))]

    grad_pre_one, grad_attention, sums_one = by_rows(
        norm_back_kernel, flags, wide_vec, [grad_pre_two, own, arrived, normed_one, inverse_one],
        [(model, f32), (model, bf16), (0, f32)], "norm_back",
    )
    grad_attn_wide = core_gather(grad_attention)
    grad_mixed = [mm(grad_attn_wide, w, NT).astype(bf16) for w in w_outs[::-1]][::-1]
    narrow = grad_mixed[1].shape[1] // 2
    grad_outs = [transposed(m, grad_attn_wide) for m in mixed]
    grad_outs[0], grad_outs[1], grad_mixed[1], da_near, db_row = hold(*grad_outs, grad_mixed[1], da_near, db_row)
    sum_down = PairSum(jnp.concatenate([added(da, da_near), added(db, db_row)], axis=0))
    sum_down.send()
    go_a = attend_back(*other_a, after(grad_mixed[1][:, :narrow], sum_down.values))
    wt_oa = transposed(go_a, wide)
    go_b = attend_back(*other_b, after(grad_mixed[1][:, narrow:], go_a))
    wt_ob = transposed(go_b, wide)
    (gm, go_b, wt_oa, wt_ob, *in_first) = sum_down.step(grad_mixed[0], go_b, wt_oa, wt_ob, *in_first)
    (ia, ia_near), (ib, ib_row) = second_sends(in_own_a, in_first[0], in_mine_b, in_first[1])
    qkv_a_other = to_row(after(wt_oa[:, side:], ib))
    go_m = attend_back(*mine, after(gm, ia, ib))
    out_row_grads = to_row(jnp.concatenate([g[:, side:] for g in grad_outs[::-1]], axis=0))
    go_m, ia_near, ib_row = sum_down.step(go_m, ia_near, ib_row)
    grad_mine = go_m
    sum_in = PairSum(jnp.concatenate([added(ia, ia_near), added(ib, ib_row)], axis=0))
    sum_in.send()
    wt_m = transposed(grad_mine, wide)
    qkv_a_mine = to_row(wt_m[:cut, side:])
    rows = grad_outs[0].shape[0]
    out_sums = added(
        jnp.concatenate([g[:, :side] for g in grad_outs[::-1]], axis=0), out_row_grads
    )
    out_near_grad = to_chip(out_sums[:rows])

    features = jnp.concatenate([sums_one[2:3], sums_one[:2], sums_two[2:3], sums_two[:2]], axis=0)
    f0, f1, f2, f3 = [features[:, i * width : (i + 1) * width] for i in range(4)]
    keep = jnp.concatenate([jnp.where(first_core, f0, f1), jnp.where(first_core, f2, f3)], axis=1)
    give = jnp.concatenate([jnp.where(first_core, f1, f0), jnp.where(first_core, f3, f2)], axis=1)
    features = keep + to_core(give)
    feature_mine = jnp.where(same, features[:, :width], features[:, width:])
    feature_near = jnp.where(same, features[:, width:], features[:, :width])
    extras = []
    for g, i, f in zip(((grad_mine,), (go_a, go_b)), grad_in_biases, (feature_mine, feature_near)):
        sums = jnp.concatenate([jnp.sum(v, axis=0, dtype=f32) for v in g]).reshape(heads, 3, HEAD_DIM)
        sums = jnp.stack([sums[:, 0], sums[:, 2]], axis=1).reshape(-1)
        flat = jnp.concatenate([sums, i, f.reshape(-1)])
        lines = -(-flat.shape[0] // (64 * side)) * 64
        flat = jnp.pad(flat, (0, lines * side - flat.shape[0])).reshape(lines, side).astype(bf16)
        extras.append(jnp.concatenate([flat, flat], axis=1))

    b_near = to_chip(jnp.concatenate([wt_ob, extras[1]], axis=0))
    sum_mine = added(wt_m[:cut, :side], qkv_a_mine)
    a_near = to_chip(added(wt_oa[:, :side], qkv_a_other))
    sum_b = added(jnp.concatenate([wt_m[cut:], extras[0]], axis=0), b_near)
    b_row = to_row(sum_b[:, side:])
    grads = [grad_mine, go_a, go_b]
    grad_left, grad_right = [sum(mm(g, w, NT) for g, w in zip(grads, ws)) for ws in (lefts, rights)]
    grad_left, grad_right = sum_down.step(grad_left, grad_right)
    sum_in.step()
    sum_qkv = PairSum(
        jnp.concatenate(
            [added(sum_mine, a_near), added(sum_b[:, :side], b_row), added(out_sums[rows:], out_near_grad)], axis=0
        )
    )
    sum_qkv.send()
    sum_down.step()
    for _ in range(8):
        sum_qkv.step()
        sum_in.step()
    grad_w_down = sum_down.finish()
    grad_w_in = sum_in.finish()
    summed = sum_qkv.finish().astype(f32)
    grad_w_qkv = summed[: 2 * cut].T
    part_b = summed[2 * cut : -rows]
    grad_w_out = summed[-rows:]
    small = part_b.reshape(-1)
    qv_len = qv_bias.shape[0]
    g_qv, g_in = small[:qv_len], small[qv_len : qv_len + hidden]
    g_out, g_gone, g_sone, g_down, g_gtwo, g_stwo = small[
        qv_len + hidden : qv_len + hidden + 6 * width
    ].reshape(6, width)

    grad_wide = jnp.concatenate([grad_left, grad_right], axis=1)
    grad_wide = jnp.concatenate([grad_wide[:half] + grad_pre_one, grad_wide[half:]], axis=0)

    keep, give = placed(
        split_chip_kernel, flags, [out_keep, to_core(out_give)], [shape(count, width)] * 2, "split_chip"
    )
    output = placed(
        join_sequences_kernel, flags, [keep, to_chip(give)], [shape(2, count, width)], "join_sequences"
    )[0]
    keep, give = placed(
        split_core_kernel, flags, [grad_wide],
        [shape(count, 2 * width, dtype=f32), shape(count, 2 * width)], "split_core",
    )
    keep, give = placed(
        add_split_chip_kernel, flags, [keep, to_core(give)], [shape(count, width)] * 2, "add_split_chip"
    )
    grad_tokens = placed(
        join_sequences_kernel, flags, [keep, to_chip(give)], [shape(2, count, width)], "join_sequences"
    )[0]
    return (
        output, grad_tokens, grad_w_qkv, g_qv, grad_w_out, g_out, g_gone, g_sone,
        grad_w_in.astype(f32).T, g_in, grad_w_down.astype(f32), g_down, g_gtwo, g_stwo,
    )


def solution(mesh):
    tokens = P(("dp", "row"), None, "col")
    feature = P("col")
    by_row, by_col = P("row", "col"), P("col", "row")
    return jax.shard_map(
        body,
        mesh=mesh,
        in_specs=(
            tokens, P(("dp", "row"), None), by_row, feature, by_col, feature, feature, feature,
            by_row, feature, by_col, feature, feature, feature, tokens,
        ),
        out_specs=(
            tokens, tokens, by_row, feature, by_col, feature, feature, feature,
            by_row, feature, by_col, feature, feature, feature,
        ),
        check_vma=False,
    )
```

time: 553 us -> 468 us (0.85)
  Pallas kernels: 45.2 us -> 114 us
  matrix products: 81.4 us -> 37.3 us
  waiting for transfers between devices: 200 us -> 158 us
  blocking collectives: 39.7 us -> 0 us
  local copies, waits for them, and re-layouts: 84.6 us -> 55.6 us
  starting transfers between devices: 33 us -> 49.7 us
  between operations: 15.8 us -> 3.12 us
    ppermute x0 -> x12, waiting for transfers between devices: none -> 63.4 us  [the longest x6 33 us: send(): self.arrived = lax.ppermute(self.values, 'dp', pairs)]
    psum x1 -> x0, waiting for transfers between devices: 62.5 us -> none  [over_dp(): return lax.psum(values, 'dp').astype(f32)]
    pallas_call x0 -> x22, Pallas kernels: none -> 56.7 us  [the longest x2 15.9 us: weight_grads(): pl.pallas_call(weight_kernel, grid=(2 * n,), in_specs=[pl.BlockSpec((coun...]
    dot_general x30 -> x20, matrix products: 81.4 us -> 37.3 us  [mm(): return lax.dot_general(left, right, dims, preferred_element_type=f32)]
    psum x1 -> x0, blocking collectives: 39.7 us -> none  [body(): small = lax.psum(small[0] + to_chip(small[1]), ('dp', 'row'))]
    ppermute x18 -> x20, waiting for transfers between devices: 59.9 us -> 35.9 us  [to_chip(): return lax.ppermute(values, 'col', [(i, i ^ 2) for i in range(size)])]
    ppermute x13 -> x15, waiting for transfers between devices: 77.5 us -> 56.8 us  [to_row(): return lax.ppermute(values, 'row', [(0, 1), (1, 0)])]
    reduce_sum x11 -> x3, other arithmetic: 15 us -> 0.63 us  [body(): jnp.sum(v, axis=0, dtype=f32)]
  transfers between devices with their start and end apart: 44 -> 60, of which waited for: 12 -> 24; matrix products, arithmetic and copies ran while one was open for 32% -> 22% of each run, Pallas kernels for 8% -> 22%
where the time goes in v2:
time: 468 us; the launch traced here: 461 us
  waiting for transfers between devices  158 us (34%)
  Pallas kernels  114 us (24%)
  local copies, waits for them, and re-layouts  55.6 us (12%)
  starting transfers between devices  49.7 us (11%)
  other arithmetic  43.8 us (9%)
  matrix products  37.3 us (8%)
    ppermute x15, waiting for transfers between devices, to_row(): return lax.ppermute(values, 'row', [(0, 1), (1, 0)])  56.8 us
    dot_general x20, matrix products, mm(): return lax.dot_general(left, right, dims, preferred_element_type=f32)  37.3 us
    ppermute x20, waiting for transfers between devices, to_chip(): return lax.ppermute(values, 'col', [(i, i ^ 2) for i in range(size)])  35.9 us
    unnamed x246, local copies, waits for them, and re-layouts  34.9 us
    ppermute x6, waiting for transfers between devices, send(): self.arrived = lax.ppermute(self.values, 'dp', pairs)  33 us
    ppermute x6, waiting for transfers between devices, send(): self.arrived = lax.ppermute(give, 'dp', pairs)  30.5 us
    pallas_call x3, Pallas kernels, attend(): pl.pallas_call(functools.partial(attend_kernel, min(512, count)), grid=(p...  30.4 us
    pallas_call x3, Pallas kernels, attend_back(): pl.pallas_call(functools.partial(attend_back_kernel, min(512, count)), gr...  26.6 us
  transfers between devices with their start and end apart: 60, of which 24 were waited for; matrix products, arithmetic and copies ran while one was open for 22% of the time, Pallas kernels for 22%

profile of v2, /device:TPU:0, one launch (start us, length us, event | category | flops | bytes accessed | tf_op | source)
XLA Modules:
  0.0 461.3 jit_solution(1557343155833295348)
XLA Ops:
  3.0 3.0 collective-permute-start
  9.5 8.5 %collective-permute-done.near_ref = bf16[1024,256]{1,0:T(8,128)(2,1)S(1)} collective-permute-done((bf16[1024,256]{1,0:T(8,128)(2,1)S(1)}, bf16[1024,256]{1,0:T(8,128)(2,1)S(1)}, u32[]{:S(2)}, u32[]{:S(2)}) %collective-permute-start) | collective-permute-done | bytes 524320 | tf_op jit(solution)/shard_map/ppermute | solution.py:34
  23.9 2.8 collective-permute-done.4.right_ref
  38.3 14.2 %attend.3 = (bf16[1024,768]{1,0:T(8,128)(2,1)}, bf16[4,1024,1024]{2,1,0:T(8,128)(2,1)}, bf16[1024,256]{1,0:T(8,128)(2,1)S(1)}, f32[1024,256]{1,0:T(8,128)}) custom-call(bf16[1024,1024]{1,0:T(8,128)(2,1)} %copy-done.2, bf16[512,768]{1,0:T(8,128)(2,1)S(1)} %copy-done.22, bf16[512,768]{1,0:T(8,128)(2,1)} %collective-permute-done.4.right_ref, ...), custom_call_target="tpu_custom_call" | custom-call | flops 1024 | bytes 1024 | tf_op jit(solution)/shard_map/attend/pallas_call | solution.py:72
  52.5 13.3 %collective-permute-done.10 = bf16[256,512]{1,0:T(8,128)(2,1)} collective-permute-done((bf16[256,512]{1,0:T(8,128)(2,1)}, bf16[256,512]{1,0:T(8,128)(2,1)}, u32[]{:S(2)}, u32[]{:S(2)}) %collective-permute-start.10) | collective-permute-done | bytes 262176 | tf_op jit(solution)/shard_map/ppermute | solution.py:38
  68.0 8.2 %attend.4 = (bf16[1024,384]{1,0:T(8,128)(2,1)}, bf16[2,1024,1024]{2,1,0:T(8,128)(2,1)}, bf16[1024,128]{1,0:T(8,128)(2,1)S(1)}, f32[1024,128]{1,0:T(8,128)S(1)}) custom-call(bf16[1024,1024]{1,0:T(8,128)(2,1)} %copy-done.2, bf16[512,384]{1,0:T(8,128)(2,1)} %collective-permute-done.7.left_ref, bf16[512,384]{1,0:T(8,128)(2,1)} %collective-permute-done.8.right_ref, ...), custom_call_target="tpu_custom_call" | custom-call | flops 1024 | bytes 1024 | tf_op jit(solution)/shard_map/attend/pallas_call | solution.py:72
  79.8 8.0 %attend.5 = (bf16[1024,384]{1,0:T(8,128)(2,1)}, bf16[2,1024,1024]{2,1,0:T(8,128)(2,1)}, bf16[1024,128]{1,0:T(8,128)(2,1)S(1)}, f32[1024,128]{1,0:T(8,128)S(1)}) custom-call(bf16[1024,1024]{1,0:T(8,128)(2,1)} %copy-done.2, bf16[512,384]{1,0:T(8,128)(2,1)S(1)} %copy-done.47, bf16[512,384]{1,0:T(8,128)(2,1)} %collective-permute-done.9.right_ref, ...), custom_call_target="tpu_custom_call" | custom-call | flops 1024 | bytes 1024 | tf_op jit(solution)/shard_map/attend/pallas_call | solution.py:72
  97.1 17.4 %collective-permute-done.18.right_ref = bf16[1024,512]{1,0:T(8,128)(2,1)S(1)} collective-permute-done((bf16[1024,512]{1,0:T(8,128)(2,1)S(1)}, bf16[1024,512]{1,0:T(8,128)(2,1)S(1)}, u32[]{:S(2)}, u32[]{:S(2)}) %collective-permute-start.18) | collective-permute-done | bytes 1048608 | tf_op jit(solution)/shard_map/ppermute | solution.py:38
  116.0 5.1 %collective-permute-done.17.left_ref = bf16[512,1024]{1,0:T(8,128)(2,1)S(1)} collective-permute-done((bf16[512,1024]{1,0:T(8,128)(2,1)}, bf16[512,1024]{1,0:T(8,128)(2,1)S(1)}, u32[]{:S(2)}, u32[]{:S(2)}) %collective-permute-start.17) | collective-permute-done | bytes 1048608 | tf_op jit(solution)/shard_map/ppermute | solution.py:34
  122.1 5.6 %feed.2 = (bf16[1024,1024]{1,0:T(8,128)(2,1)S(1)}, bf16[1024,1024]{1,0:T(8,128)(2,1)S(1)}) custom-call(bf16[1024,1024]{1,0:T(8,128)(2,1)S(1)} %pad_maximum_fusion.1.wide_ref.right_ref, bf16[512,1024]{1,0:T(8,128)(2,1)} %left_ref.4, bf16[512,1024]{1,0:T(8,128)(2,1)} %collective-permute-done.13.right_ref, f32[1,1024]{1,0:T(1,128)S(1)} %bitcast.54), custom_call_target="tpu_custom_call" | custom-call | flops 1024 | bytes 1024 | tf_op jit(solution)/shard_map/feed/pallas_call | solution.py:263
  127.7 2.6 fusion.12
  130.3 2.9 fusion.14
  133.2 10.3 %collective-permute-done.15.left_ref = bf16[1024,512]{1,0:T(8,128)(2,1)S(1)} collective-permute-done((bf16[1024,512]{1,0:T(8,128)(2,1)S(1)}, bf16[1024,512]{1,0:T(8,128)(2,1)S(1)}, u32[]{:S(2)}, u32[]{:S(2)}) %collective-permute-start.15) | collective-permute-done | bytes 1048608 | tf_op jit(solution)/shard_map/ppermute | solution.py:34
  146.3 8.5 %collective-permute-done.20 = bf16[512,512]{1,0:T(8,128)(2,1)S(1)} collective-permute-done((bf16[512,512]{1,0:T(8,128)(2,1)S(1)}, bf16[512,512]{1,0:T(8,128)(2,1)S(1)}, u32[]{:S(2)}, u32[]{:S(2)}) %collective-permute-start.20) | collective-permute-done | bytes 524320 | tf_op jit(solution)/shard_map/ppermute | solution.py:34
  156.6 4.8 %feed.3 = (bf16[1024,1024]{1,0:T(8,128)(2,1)S(1)}, bf16[1024,1024]{1,0:T(8,128)(2,1)S(1)}) custom-call(bf16[1024,1024]{1,0:T(8,128)(2,1)S(1)} %pad_maximum_fusion.1.wide_ref.right_ref, bf16[512,1024]{1,0:T(8,128)(2,1)S(1)} %collective-permute-done.17.left_ref, bf16[512,1024]{1,0:T(8,128)(2,1)S(1)} %collective-permute-done.19.right_ref, f32[1,1024]{1,0:T(1,128)S(1)} %bitcast.55), custom_call_target="tpu_custom_call" | custom-call | flops 1024 | bytes 1024 | tf_op jit(solution)/shard_map/feed/pallas_call | solution.py:263
  173.3 3.1 norm_two.1
  184.3 8.0 %weight_grads.2 = (bf16[1024,512]{1,0:T(8,128)(2,1)}, bf16[1024,512]{1,0:T(8,128)(2,1)S(1)}, bf16[512,1024]{1,0:T(8,128)(2,1)}, bf16[512,1024]{1,0:T(8,128)(2,1)S(1)}) custom-call(bf16[1024,1024]{1,0:T(8,128)(2,1)S(1)} %copy-done.33, bf16[1024,1024]{1,0:T(8,128)(2,1)S(1)} %copy-done.29, ...), custom_call_target="tpu_custom_call" | custom-call | flops 1024 | bytes 1024 | tf_op jit(solution)/shard_map/weight_grads/pallas_call | solution.py:341
  194.8 4.0 feed_back.3
  198.8 3.6 fusion.4
  202.4 3.6 feed_back.2
  206.0 2.3 add_convert_fusion.4
  211.5 8.0 %weight_grads.3 = (bf16[1024,512]{1,0:T(8,128)(2,1)}, bf16[1024,512]{1,0:T(8,128)(2,1)S(1)}, bf16[512,1024]{1,0:T(8,128)(2,1)}, bf16[512,1024]{1,0:T(8,128)(2,1)S(1)}) custom-call(bf16[1024,1024]{1,0:T(8,128)(2,1)S(1)} %copy-done.35, bf16[1024,1024]{1,0:T(8,128)(2,1)S(1)} %copy-done.37, bf16[1024,1024]{1,0:T(8,128)(2,1)S(1)} %pad_maximum_fusion.1.wide_ref.right_ref), custom_call_target="tpu_custom_call" | custom-call | flops 1024 | bytes 1024 | tf_op jit(solution)/shard_map/weight_grads/pallas_call | solution.py:341
  222.1 3.0 fusion.7
  227.3 4.1 norm_back.1
  231.5 2.4 add_convert_fusion.3
  243.3 14.3 %collective-permute-done.33 = bf16[512,512]{1,0:T(8,128)(2,1)} collective-permute-done((bf16[512,512]{1,0:T(8,128)(2,1)}, bf16[512,512]{1,0:T(8,128)(2,1)}, u32[]{:S(2)}, u32[]{:S(2)}) %collective-permute-start.33) | collective-permute-done | bytes 524320 | tf_op jit(solution)/shard_map/ppermute | solution.py:38
  258.3 2.5 broadcast_select_fusion.3
  260.9 7.2 %attend_back.3.left_ref = bf16[1024,384]{1,0:T(8,128)(2,1)S(1)} custom-call(bf16[1024,384]{1,0:T(8,128)(2,1)S(1)} %copy-done.65, bf16[2,1024,1024]{2,1,0:T(8,128)(2,1)} %get-tuple-element.183.exp_ref, bf16[1024,128]{1,0:T(8,128)(2,1)S(1)} %copy-done.62, f32[1024,128]{1,0:T(8,128)S(1)} %copy-done.70, bf16[1024,128]{1,0:T(8,128)(2,1)S(1)} %get-tuple-element.185.grad_ref), custom_call_target="tpu_custom_call" | custom-call | flops 1024 | bytes 1024 | tf_op jit(solution)/shard_map/attend_back/pallas_call | solution.py:138
  268.9 7.2 %attend_back.4.left_ref = bf16[1024,384]{1,0:T(8,128)(2,1)S(1)} custom-call(bf16[1024,384]{1,0:T(8,128)(2,1)S(1)} %copy-done.66, bf16[2,1024,1024]{2,1,0:T(8,128)(2,1)} %get-tuple-element.180.exp_ref, bf16[1024,128]{1,0:T(8,128)(2,1)S(1)} %copy-done.64, f32[1024,128]{1,0:T(8,128)S(1)} %copy-done.72, bf16[1024,128]{1,0:T(8,128)(2,1)S(1)} %get-tuple-element.186.grad_ref), custom_call_target="tpu_custom_call" | custom-call | flops 1024 | bytes 1024 | tf_op jit(solution)/shard_map/attend_back/pallas_call | solution.py:138
  287.9 3.4 fusion.50
  292.9 3.1 fusion.48
  304.5 2.6 collective-permute-start.37
  318.3 12.3 %attend_back.5.left_ref = bf16[1024,768]{1,0:T(8,128)(2,1)S(1)} custom-call(bf16[1024,768]{1,0:T(8,128)(2,1)S(1)} %copy-done.49, bf16[4,1024,1024]{2,1,0:T(8,128)(2,1)} %get-tuple-element.192.exp_ref, bf16[1024,256]{1,0:T(8,128)(2,1)S(1)} %get-tuple-element.123.left_ref.mixed_ref, f32[1024,256]{1,0:T(8,128)S(1)} %copy-done.60, bf16[1024,256]{1,0:T(8,128)(2,1)S(1)} %copy-done.73), custom_call_target="tpu_custom_call" | custom-call | flops 1024 | bytes 1024 | tf_op jit(solution)/shard_map/attend_back/pallas_call | solution.py:138
  336.4 3.5 fusion.49
  339.9 2.5 transposed.9
  343.2 2.3 add_convert_fusion.23
  345.8 2.3 broadcast_select_fusion.1
  350.2 3.2 add_add_fusion
  364.0 7.4 %collective-permute-done.45 = bf16[448,512]{1,0:T(8,128)(2,1)S(1)} collective-permute-done((bf16[448,512]{1,0:T(8,128)(2,1)S(1)}, bf16[448,512]{1,0:T(8,128)(2,1)S(1)}, u32[]{:S(2)}, u32[]{:S(2)}) %collective-permute-start.45) | collective-permute-done | bytes 458784 | tf_op jit(solution)/shard_map/ppermute | solution.py:38
  376.2 9.3 %collective-permute-done.51 = bf16[544,512]{1,0:T(8,128)(2,1)S(1)} collective-permute-done((bf16[544,512]{1,0:T(8,128)(2,1)S(1)}, bf16[544,512]{1,0:T(8,128)(2,1)S(1)}, u32[]{:S(2)}, u32[]{:S(2)}) %collective-permute-start.51) | collective-permute-done | bytes 557088 | tf_op jit(solution)/shard_map/ppermute | solution.py:510
  388.1 9.8 %collective-permute-done.56 = bf16[256,512]{1,0:T(8,128)(2,1)S(1)} collective-permute-done((bf16[256,512]{1,0:T(8,128)(2,1)S(1)}, bf16[256,512]{1,0:T(8,128)(2,1)S(1)}, u32[]{:S(2)}, u32[]{:S(2)}) %collective-permute-start.56) | collective-permute-done | bytes 262176 | tf_op jit(solution)/shard_map/ppermute | solution.py:510
  398.0 11.4 %collective-permute-done.52 = bf16[272,512]{1,0:T(8,128)(2,1)S(1)} collective-permute-done((bf16[272,512]{1,0:T(8,128)(2,1)S(1)}, bf16[272,512]{1,0:T(8,128)(2,1)S(1)}, u32[]{:S(2)}, u32[]{:S(2)}) %collective-permute-start.52) | collective-permute-done | bytes 278560 | tf_op jit(solution)/shard_map/ppermute | solution.py:510
  412.9 8.2 %collective-permute-done.57 = bf16[256,512]{1,0:T(8,128)(2,1)S(1)} collective-permute-done((bf16[256,512]{1,0:T(8,128)(2,1)S(1)}, bf16[256,512]{1,0:T(8,128)(2,1)S(1)}, u32[]{:S(2)}, u32[]{:S(2)}) %collective-permute-start.57) | collective-permute-done | bytes 262176 | tf_op jit(solution)/shard_map/ppermute | solution.py:512
  421.4 4.8 %collective-permute-done.53 = bf16[272,512]{1,0:T(8,128)(2,1)S(1)} collective-permute-done((bf16[272,512]{1,0:T(8,128)(2,1)S(1)}, bf16[272,512]{1,0:T(8,128)(2,1)S(1)}, u32[]{:S(2)}, u32[]{:S(2)}) %collective-permute-start.53) | collective-permute-done | bytes 278560 | tf_op jit(solution)/shard_map/ppermute | solution.py:512
  429.8 5.4 %collective-permute-done.59 = bf16[512,512]{1,0:T(8,128)(2,1)S(1)} collective-permute-done((bf16[512,512]{1,0:T(8,128)(2,1)S(1)}, bf16[512,512]{1,0:T(8,128)(2,1)S(1)}, u32[]{:S(2)}, u32[]{:S(2)}) %collective-permute-start.59) | collective-permute-done | bytes 524320 | tf_op jit(solution)/shard_map/ppermute | solution.py:512
  436.8 9.6 %collective-permute-done.58 = bf16[512,512]{1,0:T(8,128)(2,1)S(1)} collective-permute-done((bf16[512,512]{1,0:T(8,128)(2,1)S(1)}, bf16[512,512]{1,0:T(8,128)(2,1)S(1)}, u32[]{:S(2)}, u32[]{:S(2)}) %collective-permute-start.58) | collective-permute-done | bytes 524320 | tf_op jit(solution)/shard_map/ppermute | solution.py:512
  448.1 2.9 copy.32
  452.6 3.5 collective-permute-done.54
  (496 shorter events, 162.5 us)
Async XLA Ops:
  3.0 15.1 %collective-permute-start = (bf16[1024,256]{1,0:T(8,128)(2,1)S(1)}, bf16[1024,256]{1,0:T(8,128)(2,1)S(1)}, u32[]{:S(2)}, u32[]{:S(2)}) collective-permute-start(bf16[1024,256]{1,0:T(8,128)(2,1)S(1)} %get-tuple-element.257), channel_id=1, source_target_pairs={{0,2},{1,3},{2,0},{3,1},{4,6},{5,7},{6,4},{7,5},{8,10},{9,11},{10,... | collective-permute-start | bytes 1572872 | tf_op jit(solution)/shard_map/ppermute | solution.py:34
  6.0 15.8 %collective-permute-start.1 = (bf16[1024,256]{1,0:T(8,128)(2,1)}, bf16[1024,256]{1,0:T(8,128)(2,1)S(1)}, u32[]{:S(2)}, u32[]{:S(2)}) collective-permute-start(bf16[1024,256]{1,0:T(8,128)(2,1)} %get-tuple-element.256), channel_id=1, source_target_pairs={{0,1},{1,0},{2,3},{3,2},{4,5},{5,4},{6,7},{7,6},{8,9},{9,8},{10,11... | collective-permute-start | bytes 1572872 | tf_op jit(solution)/shard_map/ppermute | solution.py:29
  6.5 17.5 %collective-permute-start.3 = (f32[3328]{0:T(1024)S(1)}, f32[3328]{0:T(1024)S(1)}, u32[]{:S(2)}, u32[]{:S(2)}) collective-permute-start(f32[3328]{0:T(1024)S(1)} %constant_dynamic-update-slice_fusion.34), channel_id=1, source_target_pairs={{0,2},{1,3},{2,0},{3,1},{4,6},{5,7},{6,4},{7,5},{8,10},{9,11},{10,... | collective-permute-start | bytes 39944 | tf_op jit(solution)/shard_map/ppermute | solution.py:34
  6.5 20.1 %collective-permute-start.4 = (bf16[512,768]{1,0:T(8,128)(2,1)S(1)}, bf16[512,768]{1,0:T(8,128)(2,1)}, u32[]{:S(2)}, u32[]{:S(2)}) collective-permute-start(bf16[512,768]{1,0:T(8,128)(2,1)S(1)} %copy-done.21), channel_id=1, source_target_pairs={{0,4},{4,0},{1,5},{5,1},{2,6},{6,2},{3,7},{7,3},{8,12},{12,8},{9,1... | collective-permute-start | bytes 2359304 | tf_op jit(solution)/shard_map/ppermute | solution.py:38
  19.0 13.8 %collective-permute-start.7 = (bf16[512,384]{1,0:T(8,128)(2,1)}, bf16[512,384]{1,0:T(8,128)(2,1)}, u32[]{:S(2)}, u32[]{:S(2)}) collective-permute-start(bf16[512,384]{1,0:T(8,128)(2,1)} %get-tuple-element.258), channel_id=1, source_target_pairs={{0,2},{1,3},{2,0},{3,1},{4,6},{5,7},{6,4},{7,5},{8,10},{9,11},{10,... | collective-permute-start | bytes 1179656 | tf_op jit(solution)/shard_map/ppermute | solution.py:34
  26.7 52.0 %collective-permute-start.13 = (bf16[512,1024]{1,0:T(8,128)(2,1)}, bf16[512,1024]{1,0:T(8,128)(2,1)}, u32[]{:S(2)}, u32[]{:S(2)}) collective-permute-start(bf16[512,1024]{1,0:T(8,128)(2,1)} %left_ref.4), channel_id=1, source_target_pairs={{0,4},{4,0},{1,5},{5,1},{2,6},{6,2},{3,7},{7,3},{8,12},{12,8},{9,1... | collective-permute-start | bytes 3145736 | tf_op jit(solution)/shard_map/ppermute | solution.py:38
  31.2 21.3 %collective-permute-start.6 = (bf16[512,384]{1,0:T(8,128)(2,1)}, bf16[512,384]{1,0:T(8,128)(2,1)S(1)}, u32[]{:S(2)}, u32[]{:S(2)}) collective-permute-start(bf16[512,384]{1,0:T(8,128)(2,1)} %get-tuple-element.259), channel_id=1, source_target_pairs={{0,2},{1,3},{2,0},{3,1},{4,6},{5,7},{6,4},{7,5},{8,10},{9,11},{10,... | collective-permute-start | bytes 1179656 | tf_op jit(solution)/shard_map/ppermute | solution.py:34
  32.8 33.0 %collective-permute-start.8 = (bf16[512,384]{1,0:T(8,128)(2,1)}, bf16[512,384]{1,0:T(8,128)(2,1)}, u32[]{:S(2)}, u32[]{:S(2)}) collective-permute-start(bf16[512,384]{1,0:T(8,128)(2,1)} %collective-permute-done.7.left_ref), channel_id=1, source_target_pairs={{0,4},{4,0},{1,5},{5,1},{2,6},{6,2},{3,7},{7,3},{8,12},{12,8},{9,1... | collective-permute-start | bytes 1179656 | tf_op jit(solution)/shard_map/ppermute | solution.py:38
  35.1 30.7 %collective-permute-start.9 = (bf16[512,384]{1,0:T(8,128)(2,1)}, bf16[512,384]{1,0:T(8,128)(2,1)}, u32[]{:S(2)}, u32[]{:S(2)}) collective-permute-start(bf16[512,384]{1,0:T(8,128)(2,1)} %slice.281), channel_id=1, source_target_pairs={{0,2},{1,3},{2,0},{3,1},{4,6},{5,7},{6,4},{7,5},{8,10},{9,11},{10,... | collective-permute-start | bytes 1179656 | tf_op jit(solution)/shard_map/ppermute | solution.py:34
  35.9 29.9 %collective-permute-start.10 = (bf16[256,512]{1,0:T(8,128)(2,1)}, bf16[256,512]{1,0:T(8,128)(2,1)}, u32[]{:S(2)}, u32[]{:S(2)}) collective-permute-start(bf16[256,512]{1,0:T(8,128)(2,1)} %param.19), channel_id=1, source_target_pairs={{0,4},{4,0},{1,5},{5,1},{2,6},{6,2},{3,7},{7,3},{8,12},{12,8},{9,1... | collective-permute-start | bytes 786440 | tf_op jit(solution)/shard_map/ppermute | solution.py:38
  68.0 20.9 %collective-permute-start.5 = (f32[6,512]{1,0:T(8,128)S(1)}, f32[6,512]{1,0:T(8,128)S(1)}, u32[]{:S(2)}, u32[]{:S(2)}) collective-permute-start(f32[6,512]{1,0:T(8,128)S(1)} %constant_dynamic-update-slice_fusion.2), channel_id=1, source_target_pairs={{0,1},{1,0},{2,3},{3,2},{4,5},{5,4},{6,7},{7,6},{8,9},{9,8},{10,11... | collective-permute-start | bytes 36872 | tf_op jit(solution)/shard_map/ppermute | solution.py:29
  89.5 25.0 %collective-permute-start.18 = (bf16[1024,512]{1,0:T(8,128)(2,1)S(1)}, bf16[1024,512]{1,0:T(8,128)(2,1)S(1)}, u32[]{:S(2)}, u32[]{:S(2)}) collective-permute-start(bf16[1024,512]{1,0:T(8,128)(2,1)S(1)} %copy-done.16), channel_id=1, source_target_pairs={{0,4},{4,0},{1,5},{5,1},{2,6},{6,2},{3,7},{7,3},{8,12},{12,8},{9,1... | collective-permute-start | bytes 3145736 | tf_op jit(solution)/shard_map/ppermute | solution.py:38
  94.8 21.0 %collective-permute-start.16 = (bf16[512,1024]{1,0:T(8,128)(2,1)S(1)}, bf16[512,1024]{1,0:T(8,128)(2,1)S(1)}, u32[]{:S(2)}, u32[]{:S(2)}) collective-permute-start(bf16[512,1024]{1,0:T(8,128)(2,1)S(1)} %get-tuple-element.143), channel_id=1, source_target_pairs={{0,1},{1,0},{2,3},{3,2},{4,5},{5,4},{6,7},{7,6},{8,9},{9,8},{10,11... | collective-permute-start | bytes 3145736 | tf_op jit(solution)/shard_map/ppermute | solution.py:29
  94.9 26.2 %collective-permute-start.17 = (bf16[512,1024]{1,0:T(8,128)(2,1)}, bf16[512,1024]{1,0:T(8,128)(2,1)S(1)}, u32[]{:S(2)}, u32[]{:S(2)}) collective-permute-start(bf16[512,1024]{1,0:T(8,128)(2,1)} %left_ref.4), channel_id=1, source_target_pairs={{0,2},{1,3},{2,0},{3,1},{4,6},{5,7},{6,4},{7,5},{8,10},{9,11},{10,... | collective-permute-start | bytes 3145736 | tf_op jit(solution)/shard_map/ppermute | solution.py:34
  96.2 47.4 %collective-permute-start.15 = (bf16[1024,512]{1,0:T(8,128)(2,1)S(1)}, bf16[1024,512]{1,0:T(8,128)(2,1)S(1)}, u32[]{:S(2)}, u32[]{:S(2)}) collective-permute-start(bf16[1024,512]{1,0:T(8,128)(2,1)S(1)} %copy-done.16), channel_id=1, source_target_pairs={{0,2},{1,3},{2,0},{3,1},{4,6},{5,7},{6,4},{7,5},{8,10},{9,11},{10,... | collective-permute-start | bytes 3145736 | tf_op jit(solution)/shard_map/ppermute | solution.py:34
  114.6 40.3 %collective-permute-start.20 = (bf16[512,512]{1,0:T(8,128)(2,1)S(1)}, bf16[512,512]{1,0:T(8,128)(2,1)S(1)}, u32[]{:S(2)}, u32[]{:S(2)}) collective-permute-start(bf16[512,512]{1,0:T(8,128)(2,1)S(1)} %slice.360), channel_id=1, source_target_pairs={{0,2},{1,3},{2,0},{3,1},{4,6},{5,7},{6,4},{7,5},{8,10},{9,11},{10,... | collective-permute-start | bytes 1572872 | tf_op jit(solution)/shard_map/ppermute | solution.py:34
  121.1 35.4 %collective-permute-start.19 = (bf16[512,1024]{1,0:T(8,128)(2,1)S(1)}, bf16[512,1024]{1,0:T(8,128)(2,1)S(1)}, u32[]{:S(2)}, u32[]{:S(2)}) collective-permute-start(bf16[512,1024]{1,0:T(8,128)(2,1)S(1)} %collective-permute-done.17.left_ref), channel_id=1, source_target_pairs={{0,4},{4,0},{1,5},{5,1},{2,6},{6,2},{3,7},{7,3},{8,12},{12,8},{9,1... | collective-permute-start | bytes 3145736 | tf_op jit(solution)/shard_map/ppermute | solution.py:38
  144.7 20.8 %collective-permute-start.23 = (bf16[1024,256]{1,0:T(8,128)(2,1)S(1)}, bf16[1024,256]{1,0:T(8,128)(2,1)S(1)}, u32[]{:S(2)}, u32[]{:S(2)}) collective-permute-start(bf16[1024,256]{1,0:T(8,128)(2,1)S(1)} %dynamic-slice_bitcast_fusion), channel_id=1, source_target_pairs={{0,2},{1,3},{2,0},{3,1},{4,6},{5,7},{6,4},{7,5},{8,10},{9,11},{10,... | collective-permute-start | bytes 1572872 | tf_op jit(solution)/shard_map/ppermute | solution.py:34
  192.3 34.2 %collective-permute-start.29 = (bf16[1024,512]{1,0:T(8,128)(2,1)}, bf16[1024,512]{1,0:T(8,128)(2,1)}, u32[]{:S(2)}, u32[]{:S(2)}) collective-permute-start(bf16[1024,512]{1,0:T(8,128)(2,1)} %get-tuple-element.166), channel_id=1, source_target_pairs={{0,4},{4,0},{1,5},{5,1},{2,6},{6,2},{3,7},{7,3},{8,12},{12,8},{9,1... | collective-permute-start | bytes 3145736 | tf_op jit(solution)/shard_map/ppermute | solution.py:38
  193.2 33.2 %collective-permute-start.30 = (bf16[512,1024]{1,0:T(8,128)(2,1)}, bf16[512,1024]{1,0:T(8,128)(2,1)}, u32[]{:S(2)}, u32[]{:S(2)}) collective-permute-start(bf16[512,1024]{1,0:T(8,128)(2,1)} %get-tuple-element.167), channel_id=1, source_target_pairs={{0,2},{1,3},{2,0},{3,1},{4,6},{5,7},{6,4},{7,5},{8,10},{9,11},{10,... | collective-permute-start | bytes 3145736 | tf_op jit(solution)/shard_map/ppermute | solution.py:34
  208.3 18.2 %collective-permute-start.28 = (bf16[512,1024]{1,0:T(8,128)(2,1)}, bf16[512,1024]{1,0:T(8,128)(2,1)}, u32[]{:S(2)}, u32[]{:S(2)}) collective-permute-start(bf16[512,1024]{1,0:T(8,128)(2,1)} %add_convert_fusion.4), channel_id=1, source_target_pairs={{0,1},{1,0},{2,3},{3,2},{4,5},{5,4},{6,7},{7,6},{8,9},{9,8},{10,11... | collective-permute-start | bytes 3145736 | tf_op jit(solution)/shard_map/ppermute | solution.py:29
  220.4 75.6 %collective-permute-start.35 = (bf16[1024,512]{1,0:T(8,128)(2,1)}, bf16[1024,512]{1,0:T(8,128)(2,1)}, u32[]{:S(2)}, u32[]{:S(2)}) collective-permute-start(bf16[1024,512]{1,0:T(8,128)(2,1)} %get-tuple-element.188), channel_id=1, source_target_pairs={{0,4},{4,0},{1,5},{5,1},{2,6},{6,2},{3,7},{7,3},{8,12},{12,8},{9,1... | collective-permute-start | bytes 3145736 | tf_op jit(solution)/shard_map/ppermute | solution.py:38
  221.4 74.6 %collective-permute-start.36 = (bf16[512,1024]{1,0:T(8,128)(2,1)}, bf16[512,1024]{1,0:T(8,128)(2,1)}, u32[]{:S(2)}, u32[]{:S(2)}) collective-permute-start(bf16[512,1024]{1,0:T(8,128)(2,1)} %get-tuple-element.190), channel_id=1, source_target_pairs={{0,2},{1,3},{2,0},{3,1},{4,6},{5,7},{6,4},{7,5},{8,10},{9,11},{10,... | collective-permute-start | bytes 3145736 | tf_op jit(solution)/shard_map/ppermute | solution.py:34
  234.8 22.8 %collective-permute-start.33 = (bf16[512,512]{1,0:T(8,128)(2,1)}, bf16[512,512]{1,0:T(8,128)(2,1)}, u32[]{:S(2)}, u32[]{:S(2)}) collective-permute-start(bf16[512,512]{1,0:T(8,128)(2,1)} %slice.363), channel_id=1, source_target_pairs={{0,4},{4,0},{1,5},{5,1},{2,6},{6,2},{3,7},{7,3},{8,12},{12,8},{9,1... | collective-permute-start | bytes 1572872 | tf_op jit(solution)/shard_map/ppermute | solution.py:38
  238.8 19.4 %collective-permute-start.32 = (bf16[512,512]{1,0:T(8,128)(2,1)}, bf16[512,512]{1,0:T(8,128)(2,1)}, u32[]{:S(2)}, u32[]{:S(2)}) collective-permute-start(bf16[512,512]{1,0:T(8,128)(2,1)} %slice.362), channel_id=1, source_target_pairs={{0,2},{1,3},{2,0},{3,1},{4,6},{5,7},{6,4},{7,5},{8,10},{9,11},{10,... | collective-permute-start | bytes 1572872 | tf_op jit(solution)/shard_map/ppermute | solution.py:34
  281.3 14.7 %collective-permute-start.34 = (bf16[512,512]{1,0:T(8,128)(2,1)}, bf16[512,512]{1,0:T(8,128)(2,1)}, u32[]{:S(2)}, u32[]{:S(2)}) collective-permute-start(bf16[512,512]{1,0:T(8,128)(2,1)} %get-tuple-element.253), channel_id=1, source_target_pairs={{0,8},{8,0},{16,24},{24,16},{1,9},{9,1},{17,25},{25,17},{2,10},{10... | collective-permute-start | bytes 1572872 | tf_op jit(solution)/shard_map/ppermute | solution.py:510
  286.9 22.5 %collective-permute-start.46 = (bf16[512,512]{1,0:T(8,128)(2,1)}, bf16[512,512]{1,0:T(8,128)(2,1)}, u32[]{:S(2)}, u32[]{:S(2)}) collective-permute-start(bf16[512,512]{1,0:T(8,128)(2,1)} %pad_maximum_fusion.7), channel_id=1, source_target_pairs={{0,4},{4,0},{1,5},{5,1},{2,6},{6,2},{3,7},{7,3},{8,12},{12,8},{9,1... | collective-permute-start | bytes 1572872 | tf_op jit(solution)/shard_map/ppermute | solution.py:38
  298.6 37.8 %collective-permute-start.38 = (bf16[512,512]{1,0:T(8,128)(2,1)}, bf16[512,512]{1,0:T(8,128)(2,1)}, u32[]{:S(2)}, u32[]{:S(2)}) collective-permute-start(bf16[512,512]{1,0:T(8,128)(2,1)} %slice.369), channel_id=1, source_target_pairs={{0,2},{1,3},{2,0},{3,1},{4,6},{5,7},{6,4},{7,5},{8,10},{9,11},{10,... | collective-permute-start | bytes 1572872 | tf_op jit(solution)/shard_map/ppermute | solution.py:34
  301.5 34.8 %collective-permute-start.39 = (bf16[512,512]{1,0:T(8,128)(2,1)}, bf16[512,512]{1,0:T(8,128)(2,1)}, u32[]{:S(2)}, u32[]{:S(2)}) collective-permute-start(bf16[512,512]{1,0:T(8,128)(2,1)} %fusion.35), channel_id=1, source_target_pairs={{0,4},{4,0},{1,5},{5,1},{2,6},{6,2},{3,7},{7,3},{8,12},{12,8},{9,1... | collective-permute-start | bytes 1572872 | tf_op jit(solution)/shard_map/ppermute | solution.py:38
  304.5 31.8 %collective-permute-start.37 = (bf16[256,512]{1,0:T(8,128)(2,1)}, bf16[256,512]{1,0:T(8,128)(2,1)}, u32[]{:S(2)}, u32[]{:S(2)}) collective-permute-start(bf16[256,512]{1,0:T(8,128)(2,1)} %broadcast_select_fusion.6), channel_id=1, source_target_pairs={{0,16},{8,24},{16,0},{24,8},{1,17},{9,25},{17,1},{25,9},{2,18},{10... | collective-permute-start | bytes 786440 | tf_op jit(solution)/shard_map/ppermute | solution.py:510
  307.9 25.1 %collective-permute-start.49 = (bf16[384,512]{1,0:T(8,128)(2,1)}, bf16[384,512]{1,0:T(8,128)(2,1)}, u32[]{:S(2)}, u32[]{:S(2)}) collective-permute-start(bf16[384,512]{1,0:T(8,128)(2,1)} %slice.339), channel_id=1, source_target_pairs={{0,4},{4,0},{1,5},{5,1},{2,6},{6,2},{3,7},{7,3},{8,12},{12,8},{9,1... | collective-permute-start | bytes 1179656 | tf_op jit(solution)/shard_map/ppermute | solution.py:38
  312.2 18.4 %collective-permute-start.47 = (bf16[256,512]{1,0:T(8,128)(2,1)}, bf16[256,512]{1,0:T(8,128)(2,1)}, u32[]{:S(2)}, u32[]{:S(2)}) collective-permute-start(bf16[256,512]{1,0:T(8,128)(2,1)} %slice.387), channel_id=1, source_target_pairs={{0,2},{1,3},{2,0},{3,1},{4,6},{5,7},{6,4},{7,5},{8,10},{9,11},{10,... | collective-permute-start | bytes 786440 | tf_op jit(solution)/shard_map/ppermute | solution.py:34
  330.6 27.3 %collective-permute-start.44 = (bf16[448,1024]{1,0:T(8,128)(2,1)}, bf16[448,1024]{1,0:T(8,128)(2,1)}, u32[]{:S(2)}, u32[]{:S(2)}) collective-permute-start(bf16[448,1024]{1,0:T(8,128)(2,1)} %maximum_maximum_fusion), channel_id=1, source_target_pairs={{0,2},{1,3},{2,0},{3,1},{4,6},{5,7},{6,4},{7,5},{8,10},{9,11},{10,... | collective-permute-start | bytes 2752520 | tf_op jit(solution)/shard_map/ppermute | solution.py:34
  334.8 27.3 %collective-permute-start.50 = (bf16[384,512]{1,0:T(8,128)(2,1)}, bf16[384,512]{1,0:T(8,128)(2,1)}, u32[]{:S(2)}, u32[]{:S(2)}) collective-permute-start(bf16[384,512]{1,0:T(8,128)(2,1)} %add_convert_fusion.18), channel_id=1, source_target_pairs={{0,2},{1,3},{2,0},{3,1},{4,6},{5,7},{6,4},{7,5},{8,10},{9,11},{10,... | collective-permute-start | bytes 1179656 | tf_op jit(solution)/shard_map/ppermute | solution.py:34
  348.1 26.1 %collective-permute-start.55 = (bf16[512,512]{1,0:T(8,128)(2,1)}, bf16[512,512]{1,0:T(8,128)(2,1)}, u32[]{:S(2)}, u32[]{:S(2)}) collective-permute-start(bf16[512,512]{1,0:T(8,128)(2,1)} %broadcast_select_fusion.1), channel_id=1, source_target_pairs={{0,8},{8,0},{16,24},{24,16},{1,9},{9,1},{17,25},{25,17},{2,10},{10... | collective-permute-start | bytes 1572872 | tf_op jit(solution)/shard_map/ppermute | solution.py:510
  348.6 13.6 %collective-permute-start.48 = (bf16[384,512]{1,0:T(8,128)(2,1)}, bf16[384,512]{1,0:T(8,128)(2,1)}, u32[]{:S(2)}, u32[]{:S(2)}) collective-permute-start(bf16[384,512]{1,0:T(8,128)(2,1)} %slice.389), channel_id=1, source_target_pairs={{0,4},{4,0},{1,5},{5,1},{2,6},{6,2},{3,7},{7,3},{8,12},{12,8},{9,1... | collective-permute-start | bytes 1179656 | tf_op jit(solution)/shard_map/ppermute | solution.py:38
  371.7 13.8 %collective-permute-start.51 = (bf16[544,512]{1,0:T(8,128)(2,1)S(1)}, bf16[544,512]{1,0:T(8,128)(2,1)S(1)}, u32[]{:S(2)}, u32[]{:S(2)}) collective-permute-start(bf16[544,512]{1,0:T(8,128)(2,1)S(1)} %broadcast_select_fusion), channel_id=1, source_target_pairs={{0,8},{8,0},{16,24},{24,16},{1,9},{9,1},{17,25},{25,17},{2,10},{10... | collective-permute-start | bytes 1671176 | tf_op jit(solution)/shard_map/ppermute | solution.py:510
  372.8 13.0 %collective-permute-start.25 = (bf16[512,512]{1,0:T(8,128)(2,1)S(1)}, bf16[512,512]{1,0:T(8,128)(2,1)S(1)}, u32[]{:S(2)}, u32[]{:S(2)}) collective-permute-start(bf16[512,512]{1,0:T(8,128)(2,1)S(1)} %copy-done.78), channel_id=1, source_target_pairs={{0,1},{1,0},{2,3},{3,2},{4,5},{5,4},{6,7},{7,6},{8,9},{9,8},{10,11... | collective-permute-start | bytes 1572872 | tf_op jit(solution)/shard_map/ppermute | solution.py:29
  373.7 52.8 %collective-permute-start.41 = (bf16[1024,512]{1,0:T(8,128)(2,1)S(1)}, bf16[1024,512]{1,0:T(8,128)(2,1)S(1)}, u32[]{:S(2)}, u32[]{:S(2)}) collective-permute-start(bf16[1024,512]{1,0:T(8,128)(2,1)S(1)} %get-tuple-element.207), channel_id=1, source_target_pairs={{0,1},{1,0},{2,3},{3,2},{4,5},{5,4},{6,7},{7,6},{8,9},{9,8},{10,11... | collective-permute-start | bytes 3145736 | tf_op jit(solution)/shard_map/ppermute | solution.py:29
  376.1 21.8 %collective-permute-start.56 = (bf16[256,512]{1,0:T(8,128)(2,1)S(1)}, bf16[256,512]{1,0:T(8,128)(2,1)S(1)}, u32[]{:S(2)}, u32[]{:S(2)}) collective-permute-start(bf16[256,512]{1,0:T(8,128)(2,1)S(1)} %broadcast_select_fusion.5), channel_id=1, source_target_pairs={{0,16},{8,24},{16,0},{24,8},{1,17},{9,25},{17,1},{25,9},{2,18},{10... | collective-permute-start | bytes 786440 | tf_op jit(solution)/shard_map/ppermute | solution.py:510
  385.8 23.7 %collective-permute-start.52 = (bf16[272,512]{1,0:T(8,128)(2,1)S(1)}, bf16[272,512]{1,0:T(8,128)(2,1)S(1)}, u32[]{:S(2)}, u32[]{:S(2)}) collective-permute-start(bf16[272,512]{1,0:T(8,128)(2,1)S(1)} %broadcast_select_fusion.4), channel_id=1, source_target_pairs={{0,16},{8,24},{16,0},{24,8},{1,17},{9,25},{17,1},{25,9},{2,18},{10... | collective-permute-start | bytes 835592 | tf_op jit(solution)/shard_map/ppermute | solution.py:510
  386.5 41.7 %collective-permute-start.26 = (bf16[1024,256]{1,0:T(8,128)(2,1)S(1)}, bf16[1024,256]{1,0:T(8,128)(2,1)S(1)}, u32[]{:S(2)}, u32[]{:S(2)}) collective-permute-start(bf16[1024,256]{1,0:T(8,128)(2,1)S(1)} %get-tuple-element.159), channel_id=1, source_target_pairs={{0,2},{1,3},{2,0},{3,1},{4,6},{5,7},{6,4},{7,5},{8,10},{9,11},{10,... | collective-permute-start | bytes 1572872 | tf_op jit(solution)/shard_map/ppermute | solution.py:34
  398.0 23.2 %collective-permute-start.57 = (bf16[256,512]{1,0:T(8,128)(2,1)S(1)}, bf16[256,512]{1,0:T(8,128)(2,1)S(1)}, u32[]{:S(2)}, u32[]{:S(2)}) collective-permute-start(bf16[256,512]{1,0:T(8,128)(2,1)S(1)} %add_convert_fusion.21), channel_id=1, source_target_pairs={{0,16},{8,24},{16,0},{24,8},{1,17},{9,25},{17,1},{25,9},{2,18},{10... | collective-permute-start | bytes 786440 | tf_op jit(solution)/shard_map/ppermute | solution.py:512
  409.6 16.6 %collective-permute-start.53 = (bf16[272,512]{1,0:T(8,128)(2,1)S(1)}, bf16[272,512]{1,0:T(8,128)(2,1)S(1)}, u32[]{:S(2)}, u32[]{:S(2)}) collective-permute-start(bf16[272,512]{1,0:T(8,128)(2,1)S(1)} %add_convert_fusion.20), channel_id=1, source_target_pairs={{0,16},{8,24},{16,0},{24,8},{1,17},{9,25},{17,1},{25,9},{2,18},{10... | collective-permute-start | bytes 835592 | tf_op jit(solution)/shard_map/ppermute | solution.py:512
  411.0 24.2 %collective-permute-start.59 = (bf16[512,512]{1,0:T(8,128)(2,1)S(1)}, bf16[512,512]{1,0:T(8,128)(2,1)S(1)}, u32[]{:S(2)}, u32[]{:S(2)}) collective-permute-start(bf16[512,512]{1,0:T(8,128)(2,1)S(1)} %maximum_select_fusion.5), channel_id=1, source_target_pairs={{0,8},{8,0},{16,24},{24,16},{1,9},{9,1},{17,25},{25,17},{2,10},{10... | collective-permute-start | bytes 1572872 | tf_op jit(solution)/shard_map/ppermute | solution.py:512
  421.3 25.0 %collective-permute-start.58 = (bf16[512,512]{1,0:T(8,128)(2,1)S(1)}, bf16[512,512]{1,0:T(8,128)(2,1)S(1)}, u32[]{:S(2)}, u32[]{:S(2)}) collective-permute-start(bf16[512,512]{1,0:T(8,128)(2,1)S(1)} %maximum_select_fusion.4), channel_id=1, source_target_pairs={{0,8},{8,0},{16,24},{24,16},{1,9},{9,1},{17,25},{25,17},{2,10},{10... | collective-permute-start | bytes 1572872 | tf_op jit(solution)/shard_map/ppermute | solution.py:512
  426.4 29.7 %collective-permute-start.54 = (bf16[544,512]{1,0:T(8,128)(2,1)S(1)}, bf16[544,512]{1,0:T(8,128)(2,1)S(1)}, u32[]{:S(2)}, u32[]{:S(2)}) collective-permute-start(bf16[544,512]{1,0:T(8,128)(2,1)S(1)} %maximum_select_fusion.3), channel_id=1, source_target_pairs={{0,8},{8,0},{16,24},{24,16},{1,9},{9,1},{17,25},{25,17},{2,10},{10... | collective-permute-start | bytes 1671176 | tf_op jit(solution)/shard_map/ppermute | solution.py:512
  427.3 23.7 %collective-permute-start.42 = (bf16[1024,256]{1,0:T(8,128)(2,1)S(1)}, bf16[1024,256]{1,0:T(8,128)(2,1)S(1)}, u32[]{:S(2)}, u32[]{:S(2)}) collective-permute-start(bf16[1024,256]{1,0:T(8,128)(2,1)S(1)} %get-tuple-element.209), channel_id=1, source_target_pairs={{0,2},{1,3},{2,0},{3,1},{4,6},{5,7},{6,4},{7,5},{8,10},{9,11},{10,... | collective-permute-start | bytes 1572872 | tf_op jit(solution)/shard_map/ppermute | solution.py:34
  (125 other events, 721.9 us)

commit v3 on v2

--- a/solution.py
+++ b/solution.py
@@ -132,17 +132,18 @@
         out_ref[:, base + 2 * HEAD_DIM : base + 3 * HEAD_DIM] = grad_value.T.astype(bf16)
 
 
-def attend_back(qkv, exponent, mixed, inverse, grad_mixed):
+def attend_back(qkv, exponent, mixed, inverse, grad_mixed, first=0, at=0):
     count, width = qkv.shape
-    pairs = width // (6 * HEAD_DIM)
+    pairs, width = 1, 6 * HEAD_DIM
     return pl.pallas_call(
         functools.partial(attend_back_kernel, min(512, count)),
         grid=(pairs,),
         in_specs=[
-            pl.BlockSpec((count, 6 * HEAD_DIM), lambda p: (0, p)),
-            pl.BlockSpec((2, count, count), lambda p: (p, 0, 0)),
+            pl.BlockSpec((count, 6 * HEAD_DIM), lambda p: (0, p + first)),
+            pl.BlockSpec((2, count, count), lambda p: (p + first, 0, 0)),
         ]
-        + [pl.BlockSpec((count, 2 * HEAD_DIM), lambda p: (0, p))] * 3,
+        + [pl.BlockSpec((count, 2 * HEAD_DIM), lambda p: (0, p + first))] * 2
+        + [pl.BlockSpec((count, 2 * HEAD_DIM), lambda p: (0, p + at))],
         out_specs=pl.BlockSpec((count, 6 * HEAD_DIM), lambda p: (0, p)),
         out_shape=jax.ShapeDtypeStruct((count, width), bf16),
         compiler_params=pltpu.CompilerParams(vmem_limit_bytes=48 * 2**20),
@@ -360,6 +361,32 @@
     )(other, mine, right)
 
 
+def second_kernel(own_a, arrived_a, mine_b, arrived_b, a_other, a_mine, b_own, b_away):
+    size, side = a_mine.shape
+
+    def added(x, y):
+        return (x.astype(f32) + y.astype(f32)).astype(bf16)
+
+    a_other[...] = added(own_a[:size], arrived_a[:size])
+    a_mine[...] = added(own_a[size:], arrived_a[size:])
+    b_own[...] = added(mine_b[:, :side], arrived_b[:, :side])
+    b_away[...] = added(mine_b[:, side:], arrived_b[:, side:])
+
+
+def joined_kernel(a, a_near, b, b_row, out):
+    rows = a.shape[0]
+    out[:rows] = (a[...].astype(f32) + a_near[...].astype(f32)).astype(bf16)
+    out[rows:] = (b[...].astype(f32) + b_row[...].astype(f32)).astype(bf16)
+
+
+def merge_kernel(flags, a, a_near, b, b_row, keep, give):
+    upper = flags[3] == 1
+    low = (a[...].astype(f32) + a_near[...].astype(f32)).astype(bf16)
+    high = (b[...].astype(f32) + b_row[...].astype(f32)).astype(bf16)
+    keep[...] = jnp.where(upper, high, low)
+    give[...] = jnp.where(upper, low, high)
+
+
 def transposed_kernel(left_ref, right_ref, out_ref):
     out_ref[...] = mm(left_ref[...], right_ref[...], TN).astype(bf16)
 
@@ -402,7 +429,7 @@
     return pl.ds(pl.multiple_of(index * size, size), size)
 
 
-def join_wide_kernel(flags, mine_ref, near_ref, core_mine_ref, core_near_ref, out_ref):
+def join_wide_kernel(flags, mine_ref, near_ref, core_mine_ref, core_near_ref, order_ref, out_ref):
     chip, core, place = flags[0], flags[1], flags[2]
     width, half = near_ref.shape[1], near_ref.shape[0] // 2
     own, away = block(core, half), block(1 - core, half)
@@ -485,13 +512,13 @@
 
 
 class PairSum:
-    def __init__(self, values):
-        self.values = values
+    def __init__(self, values, give=None):
+        self.values, self.give = values, give
         self.size = lax.axis_size("dp")
         self.index = lax.axis_index("dp")
         self.undo = []
         self.todo = []
-        rows, bit = values.shape[0], 1
+        rows, bit = values.shape[0] * (1 if give is None else 2), 1
         while self.size & (self.size - 1) == 0 and bit < self.size and rows % 32 == 0:
             self.todo.append(("halve", bit))
             rows, bit = rows // 2, bit * 2
@@ -504,10 +531,11 @@
         pairs = [(i, i ^ bit) for i in range(self.size)]
         upper = (self.index & bit) != 0
         if kind == "halve":
-            rows = self.values.shape[0] // 2
-            low, high = self.values[:rows], self.values[rows:]
-            self.values, give = jnp.where(upper, high, low), jnp.where(upper, low, high)
-            self.arrived = lax.ppermute(give, "dp", pairs)
+            if self.give is None:
+                rows = self.values.shape[0] // 2
+                low, high = self.values[:rows], self.values[rows:]
+                self.values, self.give = jnp.where(upper, high, low), jnp.where(upper, low, high)
+            self.arrived, self.give = lax.ppermute(self.give, "dp", pairs), None
         elif kind == "double":
             self.arrived = lax.ppermute(self.values, "dp", pairs)
         else:
@@ -549,7 +577,9 @@
     chip, core = col // 2, col % 2
     same = row == chip
     first_core = core == 0
-    flags = jnp.stack([chip, core, jnp.where(same, 0, 1)]).astype(jnp.int32)
+    flags = jnp.stack(
+        [chip, core, jnp.where(same, 0, 1), lax.axis_index("dp") % 2]
+    ).astype(jnp.int32)
     seq_count, count, width = tokens.shape
     half = count // 2
     model = width * lax.axis_size("col")
@@ -572,10 +602,6 @@
     qkv_row = to_row(w_qkv)
     core_mine = to_core(pick(tokens, chip))
     core_near = to_core(near)
-    wide = placed(
-        join_wide_kernel, flags, [tokens, near, core_mine, core_near], [shape(count, model)], "join_wide"
-    )[0]
-
     segment = pick(segments, chip).reshape(2, half)
     segment = jnp.concatenate([pick(segment, core), pick(segment, 1 - core)])
     ids = jnp.arange(HEAD_DIM)
@@ -584,21 +610,25 @@
 
     qkv_own = after(w_qkv, near)
     near_a, near_b = to_chip(qkv_own[:, :cut]), to_chip(qkv_own[:, cut:])
+    out_row = to_row(after(w_out, near))
     far_a = to_row(near_a)
-    wide, small_near, qkv_row = hold(wide, small_near, qkv_row)
+    out_near = to_chip(after(w_out, near_a))
+    wide = placed(
+        join_wide_kernel, flags, [tokens, near, core_mine, core_near, near_a[:16, :128]],
+        [shape(count, model)], "join_wide",
+    )[0]
+    wide, small_near, qkv_row, out_row = hold(wide, small_near, qkv_row, out_row)
     far_b = to_chip(qkv_row[:, cut:])
-    out_row = to_row(after(w_out, wide))
+    out_far = to_chip(out_row)
     in_row = to_row(after(w_in, wide))
-    mine = attend(wide, w_qkv, qkv_row, qkv_bias, mask)
+    wide_m, near_b = hold(wide, near_b)
+    mine = attend(wide_m, w_qkv, qkv_row, qkv_bias, mask)
     qkv_bias_near = small_near[6 * width : 6 * width + 2 * cut]
-    wide_a, near_b, far_a, far_b, out_row = hold(after(wide, mine[0]), near_b, far_a, far_b, out_row)
-    out_near = to_chip(after(w_out, out_row))
-    out_far = to_chip(out_row)
-    in_near = to_chip(after(w_in, out_row))
-    down_row = to_row(after(w_down, out_row))
+    wide_a, far_a, far_b, out_near, out_far = hold(after(wide, mine[0]), far_a, far_b, out_near, out_far)
+    in_near = to_chip(after(w_in, wide_a))
+    down_row = to_row(after(w_down, wide_a))
     other_a = attend(wide_a, near_a, far_a, qkv_bias_near[:cut], mask)
-    wide_b, out_near, out_far, in_row = hold(after(wide, other_a[0]), out_near, out_far, in_row)
-    down_near = to_chip(after(w_down, out_near))
+    wide_b, in_row = hold(after(wide, other_a[0]), in_row)
     other_b = attend(wide_b, near_b, far_b, qkv_bias_near[cut:], mask)
     parts = [mine, other_a, other_b]
     lefts = [w_qkv, near_a, near_b]
@@ -623,6 +653,9 @@
     def core_gather(values):
         return jnp.concatenate([values, to_core(values)], axis=0)
 
+    mixed[0], mixed[1], down_row, in_near = hold(*mixed, down_row, in_near)
+    in_far = to_row(in_near)
+    down_near = to_chip(after(w_down, in_near))
     arrived = to_core(sum(mm(m[half:], w) for m, w in zip(mixed, w_outs)).astype(bf16))
     own = sum(mm(m[:half], w) for m, w in zip(mixed, w_outs))
     normed_one, inverse_one, first_out, first_low = by_rows(
@@ -631,16 +664,14 @@
     )
     first_wide = core_gather(first_low)
 
-    first_wide, in_near = hold(first_wide, in_near)
-    in_far = to_row(in_near)
     act_mine, slope_mine = feed(first_wide, w_in, in_row, in_biases[0])
     down_mine = jnp.concatenate([w_down, down_row], axis=1)
-    down_far_a = to_chip(down_row[:mid])
     ffn_mine = [mm(act_mine[half:], down_mine), mm(act_mine[:half], down_mine)]
-    cot_near = to_chip(after(pick(cotangent, 1 - chip), down_row))
-    down_near, *ffn_mine = hold(down_near, *ffn_mine)
+    ffn_mine[0], ffn_mine[1], in_far, down_near = hold(*ffn_mine, in_far, down_near)
+    down_far_a = to_chip(after(down_row[:mid], down_near))
     down_far_b = to_row(down_near[mid:])
-    act_other, slope_other = feed(after(first_wide, down_near), in_near, in_far, in_biases[1])
+    cot_near = to_chip(after(pick(cotangent, 1 - chip), down_near))
+    act_other, slope_other = feed(first_wide, in_near, in_far, in_biases[1])
     down_far = jnp.concatenate([down_far_a, down_far_b], axis=0)
     down_other = jnp.concatenate([down_near, down_far], axis=1)
     arrived = to_core((ffn_mine[0] + mm(act_other[half:], down_other)).astype(bf16))
@@ -658,9 +689,28 @@
     side = model // 2
 
     def second_sends(own_a, arrived_a, mine_b, arrived_b):
-        size = own_a.shape[0] // 2
-        sum_a, sum_b = added(own_a, arrived_a), added(mine_b, arrived_b)
-        return (sum_a[size:], to_chip(sum_a[:size])), (sum_b[:, :side], to_row(sum_b[:, side:]))
+        rows = mine_b.shape[0]
+        a_other, a_mine, b_own, b_away = pl.pallas_call(
+            second_kernel,
+            out_shape=[shape(rows, side)] * 4,
+            compiler_params=pltpu.CompilerParams(vmem_limit_bytes=40 * 2**20),
+            cost_estimate=QUICK,
+            name="second",
+        )(own_a, arrived_a, mine_b, arrived_b)
+        return (a_mine, to_chip(a_other)), (b_own, to_row(b_away))
+
+    def merged(a, a_near, b, b_row):
+        return PairSum(*placed(merge_kernel, flags, [a, a_near, b, b_row], [shape(*a.shape)] * 2, "merge"))
+
+    def joined(a, a_near, b, b_row):
+        rows, cols = a.shape
+        return pl.pallas_call(
+            joined_kernel,
+            out_shape=shape(2 * rows, cols),
+            compiler_params=pltpu.CompilerParams(vmem_limit_bytes=40 * 2**20),
+            cost_estimate=QUICK,
+            name="joined",
+        )(a, a_near, b, b_row)
 
     gw = core_gather(grad_ffn)
     down_away_a, down_own_a, down_other_b, down_mine_b = weight_grads(act_other, act_mine, gw)
@@ -675,7 +725,7 @@
     in_away_a, in_own_a, in_other_b, in_mine_b = weight_grads(hid_other, hid_mine, first_wide)
     own, arrived, *down_first = hold(own, arrived, *down_first)
     (da, da_near), (db, db_row) = second_sends(down_own_a, down_first[0], down_mine_b, down_first[1])
-    in_first = [to_row(after(in_away_a, da)), to_chip(after(in_other_b, db))]
+    own, da, db = hold(own, da, db)
 
     grad_pre_one, grad_attention, sums_one = by_rows(
         norm_back_kernel, flags, wide_vec, [grad_pre_two, own, arrived, normed_one, inverse_one],
@@ -685,24 +735,27 @@
     grad_mixed = [mm(grad_attn_wide, w, NT).astype(bf16) for w in w_outs[::-1]][::-1]
     narrow = grad_mixed[1].shape[1] // 2
     grad_outs = [transposed(m, grad_attn_wide) for m in mixed]
-    grad_outs[0], grad_outs[1], grad_mixed[1], da_near, db_row = hold(*grad_outs, grad_mixed[1], da_near, db_row)
-    sum_down = PairSum(jnp.concatenate([added(da, da_near), added(db, db_row)], axis=0))
-    sum_down.send()
-    go_a = attend_back(*other_a, after(grad_mixed[1][:, :narrow], sum_down.values))
+    grad_mixed[1], da_near, db_row = hold(grad_mixed[1], da_near, db_row)
+    grad_down = joined(da, da_near, db, db_row)
+    in_first = [to_row(after(in_away_a, grad_down)), to_chip(after(in_other_b, grad_down))]
+    grad_down = lax.psum(grad_down, "dp")
+    go_a = attend_back(*other_a, grad_mixed[1])
     wt_oa = transposed(go_a, wide)
-    go_b = attend_back(*other_b, after(grad_mixed[1][:, narrow:], go_a))
-    wt_ob = transposed(go_b, wide)
-    (gm, go_b, wt_oa, wt_ob, *in_first) = sum_down.step(grad_mixed[0], go_b, wt_oa, wt_ob, *in_first)
+    go_b = attend_back(*other_b, after(grad_mixed[1], wt_oa), at=1)
+    gm, go_b, wt_oa, *in_first = hold(grad_mixed[0], go_b, wt_oa, *in_first)
     (ia, ia_near), (ib, ib_row) = second_sends(in_own_a, in_first[0], in_mine_b, in_first[1])
-    qkv_a_other = to_row(after(wt_oa[:, side:], ib))
-    go_m = attend_back(*mine, after(gm, ia, ib))
+    wt_ob = transposed(after(go_b, ia), wide)
+    qkv_a_other = to_row(after(wt_oa[:, side:], ia))
+    gm_a = attend_back(*mine, after(gm, ia, ib, wt_ob))
     out_row_grads = to_row(jnp.concatenate([g[:, side:] for g in grad_outs[::-1]], axis=0))
-    go_m, ia_near, ib_row = sum_down.step(go_m, ia_near, ib_row)
-    grad_mine = go_m
-    sum_in = PairSum(jnp.concatenate([added(ia, ia_near), added(ib, ib_row)], axis=0))
+    gm_a, ia_near, ib_row, grad_down = hold(gm_a, ia_near, ib_row, grad_down)
+    sum_in = merged(ia, ia_near, ib, ib_row)
     sum_in.send()
-    wt_m = transposed(grad_mine, wide)
-    qkv_a_mine = to_row(wt_m[:cut, side:])
+    wt_ma = transposed(gm_a, wide)
+    qkv_a_mine = to_row(wt_ma[:, side:])
+    gm_b = attend_back(*mine, after(gm, wt_ma), first=1, at=1)
+    gm_b, qkv_a_other, out_row_grads, qkv_a_mine = sum_in.step(gm_b, qkv_a_other, out_row_grads, qkv_a_mine)
+    wt_mb = transposed(gm_b, wide)
     rows = grad_outs[0].shape[0]
     out_sums = added(
         jnp.concatenate([g[:, :side] for g in grad_outs[::-1]], axis=0), out_row_grads
@@ -717,7 +770,7 @@
     feature_mine = jnp.where(same, features[:, :width], features[:, width:])
     feature_near = jnp.where(same, features[:, width:], features[:, :width])
     extras = []
-    for g, i, f in zip(((grad_mine,), (go_a, go_b)), grad_in_biases, (feature_mine, feature_near)):
+    for g, i, f in zip(((gm_a, gm_b), (go_a, go_b)), grad_in_biases, (feature_mine, feature_near)):
         sums = jnp.concatenate([jnp.sum(v, axis=0, dtype=f32) for v in g]).reshape(heads, 3, HEAD_DIM)
         sums = jnp.stack([sums[:, 0], sums[:, 2]], axis=1).reshape(-1)
         flat = jnp.concatenate([sums, i, f.reshape(-1)])
@@ -726,27 +779,25 @@
         extras.append(jnp.concatenate([flat, flat], axis=1))
 
     b_near = to_chip(jnp.concatenate([wt_ob, extras[1]], axis=0))
-    sum_mine = added(wt_m[:cut, :side], qkv_a_mine)
+    sum_mine = added(wt_ma[:, :side], qkv_a_mine)
     a_near = to_chip(added(wt_oa[:, :side], qkv_a_other))
-    sum_b = added(jnp.concatenate([wt_m[cut:], extras[0]], axis=0), b_near)
+    sum_b = added(jnp.concatenate([wt_mb, extras[0]], axis=0), b_near)
     b_row = to_row(sum_b[:, side:])
-    grads = [grad_mine, go_a, go_b]
+    grads = [jnp.concatenate([gm_a, after(gm_b, sum_b)], axis=1), go_a, go_b]
     grad_left, grad_right = [sum(mm(g, w, NT) for g, w in zip(grads, ws)) for ws in (lefts, rights)]
-    grad_left, grad_right = sum_down.step(grad_left, grad_right)
-    sum_in.step()
+    grad_left, grad_right, b_row, a_near, out_near_grad = sum_in.step(grad_left, grad_right, b_row, a_near, out_near_grad)
     sum_qkv = PairSum(
         jnp.concatenate(
             [added(sum_mine, a_near), added(sum_b[:, :side], b_row), added(out_sums[rows:], out_near_grad)], axis=0
         )
     )
     sum_qkv.send()
-    sum_down.step()
-    for _ in range(8):
+    for _ in range(3):
+        sum_in.step()
         sum_qkv.step()
-        sum_in.step()
-    grad_w_down = sum_down.finish()
-    grad_w_in = sum_in.finish()
+    grad_in = sum_in.finish()
     summed = sum_qkv.finish().astype(f32)
+    grad_w_down, grad_w_in = grad_down, grad_in
     grad_w_qkv = summed[: 2 * cut].T
     part_b = summed[2 * cut : -rows]
     grad_w_out = summed[-rows:]

time: 468 us -> 438 us (0.936)
  waiting for transfers between devices: 158 us -> 125 us
  other arithmetic: 43.8 us -> 18.3 us
  Pallas kernels: 114 us -> 130 us
  between operations: 3.12 us -> 16.2 us
  matrix products: 37.3 us -> 30.9 us
    ppermute x15, waiting for transfers between devices: 56.8 us -> 20.6 us  [to_row(): return lax.ppermute(values, 'row', [(0, 1), (1, 0)])]
    ppermute x20, waiting for transfers between devices: 35.9 us -> 54 us  [to_chip(): return lax.ppermute(values, 'col', [(i, i ^ 2) for i in range(size)])]
    ppermute x6 -> x4, waiting for transfers between devices: 33 us -> 16.9 us  [send(): self.arrived = lax.ppermute(self.values, 'dp', pairs)]
    convert_element_type x16 -> x10, other arithmetic: 20.5 us -> 7.18 us  [added(): return (own.astype(f32) + arrived.astype(f32)).astype(bf16)]
    pallas_call x0 -> x3, Pallas kernels: none -> 8.2 us  [the longest x2 5.69 us: second_sends(): pl.pallas_call(second_kernel, out_shape=[shape(rows, side)] * 4, compiler...]
    dot_general x20, matrix products: 37.3 us -> 30.9 us  [mm(): return lax.dot_general(left, right, dims, preferred_element_type=f32)]
    unnamed x246 -> x249, local copies, waits for them, and re-layouts: 34.9 us -> 41.2 us
    pallas_call x8 -> x9, Pallas kernels: 7.49 us -> 11.5 us  [placed(): pl.pallas_call(kernel, grid_spec=pltpu.PrefetchScalarGridSpec(num_scalar_...]
  transfers between devices with their start and end apart: 60 -> 57, of which waited for: 24 -> 24; matrix products, arithmetic and copies ran while one was open for 22% -> 17% of each run, Pallas kernels for 22% -> 25%
where the time goes in v3:
time: 438 us; the launch traced here: 431 us
  Pallas kernels  130 us (30%)
  waiting for transfers between devices  125 us (29%)
  local copies, waits for them, and re-layouts  59.5 us (14%)
  starting transfers between devices  50.4 us (12%)
  matrix products  30.9 us (7%)
  other arithmetic  18.3 us (4%)
  between operations  16.2 us (4%)
    ppermute x20, waiting for transfers between devices, to_chip(): return lax.ppermute(values, 'col', [(i, i ^ 2) for i in range(size)])  54 us
    unnamed x249, local copies, waits for them, and re-layouts  41.2 us
    dot_general x20, matrix products, mm(): return lax.dot_general(left, right, dims, preferred_element_type=f32)  30.9 us
    pallas_call x3, Pallas kernels, attend(): pl.pallas_call(functools.partial(attend_kernel, min(512, count)), grid=(p...  30.5 us
    ppermute x4, waiting for transfers between devices, send(): self.arrived, self.give = (lax.ppermute(self.give, 'dp', pairs), None)  29.1 us
    pallas_call x4, Pallas kernels, attend_back(): pl.pallas_call(functools.partial(attend_back_kernel, min(512, count)), gr...  28.8 us
    ppermute x20, starting transfers between devices, to_chip(): return lax.ppermute(values, 'col', [(i, i ^ 2) for i in range(size)])  26.3 us
    ppermute x15, waiting for transfers between devices, to_row(): return lax.ppermute(values, 'row', [(0, 1), (1, 0)])  20.6 us
  transfers between devices with their start and end apart: 57, of which 24 were waited for; matrix products, arithmetic and copies ran while one was open for 17% of the time, Pallas kernels for 25%

profile of v3, /device:TPU:0, one launch (start us, length us, event | category | flops | bytes accessed | tf_op | source)
XLA Modules:
  0.0 430.5 jit_solution(1581886088558191324)
XLA Ops:
  7.4 2.3 dynamic-slice_bitcast_fusion.1
  9.7 3.0 collective-permute-start
  15.5 9.1 %collective-permute-done.near_ref = bf16[1024,256]{1,0:T(8,128)(2,1)S(1)} collective-permute-done((bf16[1024,256]{1,0:T(8,128)(2,1)S(1)}, bf16[1024,256]{1,0:T(8,128)(2,1)S(1)}, u32[]{:S(2)}, u32[]{:S(2)}) %collective-permute-start) | collective-permute-done | bytes 524320 | tf_op jit(solution)/shard_map/ppermute | solution.py:34
  29.4 6.6 %collective-permute-done.3.left_ref = bf16[512,384]{1,0:T(8,128)(2,1)S(1)} collective-permute-done((bf16[512,384]{1,0:T(8,128)(2,1)S(1)}, bf16[512,384]{1,0:T(8,128)(2,1)S(1)}, u32[]{:S(2)}, u32[]{:S(2)}) %collective-permute-start.3) | collective-permute-done | bytes 393248 | tf_op jit(solution)/shard_map/ppermute | solution.py:34
  51.9 14.2 %attend.3 = (bf16[1024,768]{1,0:T(8,128)(2,1)}, bf16[4,1024,1024]{2,1,0:T(8,128)(2,1)}, bf16[1024,256]{1,0:T(8,128)(2,1)S(1)}, f32[1024,256]{1,0:T(8,128)}) custom-call(bf16[1024,1024]{1,0:T(8,128)(2,1)} %copy-done.2, bf16[512,768]{1,0:T(8,128)(2,1)S(1)} %copy-done.32, bf16[512,768]{1,0:T(8,128)(2,1)} %collective-permute-done.5.right_ref, ...), custom_call_target="tpu_custom_call" | custom-call | flops 1024 | bytes 1024 | tf_op jit(solution)/shard_map/attend/pallas_call | solution.py:72
  71.1 8.0 %attend.4 = (bf16[1024,384]{1,0:T(8,128)(2,1)}, bf16[2,1024,1024]{2,1,0:T(8,128)(2,1)}, bf16[1024,128]{1,0:T(8,128)(2,1)S(1)}, f32[1024,128]{1,0:T(8,128)S(1)}) custom-call(bf16[1024,1024]{1,0:T(8,128)(2,1)} %copy-done.2, bf16[512,384]{1,0:T(8,128)(2,1)S(1)} %collective-permute-done.3.left_ref, bf16[512,384]{1,0:T(8,128)(2,1)} %collective-permute-done.9.right_ref, ...), custom_call_target="tpu_custom_call" | custom-call | flops 1024 | bytes 1024 | tf_op jit(solution)/shard_map/attend/pallas_call | solution.py:72
  81.3 8.3 %attend.5 = (bf16[1024,384]{1,0:T(8,128)(2,1)}, bf16[2,1024,1024]{2,1,0:T(8,128)(2,1)}, bf16[1024,128]{1,0:T(8,128)(2,1)S(1)}, f32[1024,128]{1,0:T(8,128)S(1)}) custom-call(bf16[1024,1024]{1,0:T(8,128)(2,1)} %copy-done.2, bf16[512,384]{1,0:T(8,128)(2,1)S(1)} %copy-done.56, bf16[512,384]{1,0:T(8,128)(2,1)} %collective-permute-done.10.right_ref, ...), custom_call_target="tpu_custom_call" | custom-call | flops 1024 | bytes 1024 | tf_op jit(solution)/shard_map/attend/pallas_call | solution.py:72
  89.7 5.6 %collective-permute-done.14.right_ref = bf16[1024,512]{1,0:T(8,128)(2,1)S(1)} collective-permute-done((bf16[1024,512]{1,0:T(8,128)(2,1)}, bf16[1024,512]{1,0:T(8,128)(2,1)S(1)}, u32[]{:S(2)}, u32[]{:S(2)}) %collective-permute-start.14) | collective-permute-done | bytes 1048608 | tf_op jit(solution)/shard_map/ppermute | solution.py:38
  106.1 5.6 %feed.2 = (bf16[1024,1024]{1,0:T(8,128)(2,1)S(1)}, bf16[1024,1024]{1,0:T(8,128)(2,1)S(1)}) custom-call(bf16[1024,1024]{1,0:T(8,128)(2,1)S(1)} %constant_dynamic-update-slice_fusion.8.wide_ref.right_ref, bf16[512,1024]{1,0:T(8,128)(2,1)} %left_ref.4, bf16[512,1024]{1,0:T(8,128)(2,1)} %collective-permute-done.13.right_ref, f32[1,1024]{1,0:T(1,128)S(1)} %bitcast.55), custom_call_target="tpu_custom_call" | custom-call | flops 1024 | bytes 1024 | tf_op jit(solution)/shard_map/feed/pallas_call | solution.py:264
  114.3 15.0 %collective-permute-done.19.left_ref = bf16[1024,512]{1,0:T(8,128)(2,1)S(1)} collective-permute-done((bf16[1024,512]{1,0:T(8,128)(2,1)}, bf16[1024,512]{1,0:T(8,128)(2,1)S(1)}, u32[]{:S(2)}, u32[]{:S(2)}) %collective-permute-start.19) | collective-permute-done | bytes 1048608 | tf_op jit(solution)/shard_map/ppermute | solution.py:34
  132.5 5.5 %feed.3 = (bf16[1024,1024]{1,0:T(8,128)(2,1)S(1)}, bf16[1024,1024]{1,0:T(8,128)(2,1)S(1)}) custom-call(bf16[1024,1024]{1,0:T(8,128)(2,1)S(1)} %constant_dynamic-update-slice_fusion.8.wide_ref.right_ref, bf16[512,1024]{1,0:T(8,128)(2,1)} %collective-permute-done.15.left_ref, bf16[512,1024]{1,0:T(8,128)(2,1)S(1)} %collective-permute-done.18.right_ref, ...), custom_call_target="tpu_custom_call" | custom-call | flops 1024 | bytes 1024 | tf_op jit(solution)/shard_map/feed/pallas_call | solution.py:264
  138.1 6.1 %collective-permute-done.20 = bf16[512,512]{1,0:T(8,128)(2,1)S(1)} collective-permute-done((bf16[512,512]{1,0:T(8,128)(2,1)S(1)}, bf16[512,512]{1,0:T(8,128)(2,1)S(1)}, u32[]{:S(2)}, u32[]{:S(2)}) %collective-permute-start.20) | collective-permute-done | bytes 524320 | tf_op jit(solution)/shard_map/ppermute | solution.py:34
  146.1 7.2 %collective-permute-done.23.near_ref = bf16[1024,256]{1,0:T(8,128)(2,1)S(1)} collective-permute-done((bf16[1024,256]{1,0:T(8,128)(2,1)S(1)}, bf16[1024,256]{1,0:T(8,128)(2,1)S(1)}, u32[]{:S(2)}, u32[]{:S(2)}) %collective-permute-start.23) | collective-permute-done | bytes 524320 | tf_op jit(solution)/shard_map/ppermute | solution.py:34
  156.6 3.1 norm_two.1
  167.8 8.0 %weight_grads.3 = (bf16[1024,512]{1,0:T(8,128)(2,1)}, bf16[1024,512]{1,0:T(8,128)(2,1)S(1)}, bf16[512,1024]{1,0:T(8,128)(2,1)}, bf16[512,1024]{1,0:T(8,128)(2,1)S(1)}) custom-call(bf16[1024,1024]{1,0:T(8,128)(2,1)S(1)} %copy-done.41, bf16[1024,1024]{1,0:T(8,128)(2,1)S(1)} %copy-done.37, ...), custom_call_target="tpu_custom_call" | custom-call | flops 1024 | bytes 1024 | tf_op jit(solution)/shard_map/weight_grads/pallas_call | solution.py:342
  177.9 3.6 feed_back.2
  181.5 5.1 %feed_back.3 = (bf16[1024,1024]{1,0:T(8,128)(2,1)S(1)}, f32[1,1024]{1,0:T(1,128)S(1)}) custom-call(bf16[1024,1024]{1,0:T(8,128)(2,1)S(1)} %constant_dynamic-update-slice_fusion.14.grad_ref.right_ref, bf16[1024,512]{1,0:T(8,128)(2,1)} %left_ref.5, bf16[1024,512]{1,0:T(8,128)(2,1)S(1)} %copy-done.16, bf16[1024,1024]{1,0:T(8,128)(2,1)S(1)} %get-tuple-element.190.slope_ref), custom_call_target="tpu_custom_call" | custom-call | flops 1024 | bytes 1024 | tf_op jit(solution)/shard_map/feed_back/pallas_call | solution.py:290
  188.0 2.3 add_convert_fusion
  190.3 3.3 fusion.6
  195.0 6.4 %collective-permute-done.29.arrived_a = bf16[1024,512]{1,0:T(8,128)(2,1)} collective-permute-done((bf16[1024,512]{1,0:T(8,128)(2,1)}, bf16[1024,512]{1,0:T(8,128)(2,1)}, u32[]{:S(2)}, u32[]{:S(2)}) %collective-permute-start.29) | collective-permute-done | bytes 1048608 | tf_op jit(solution)/shard_map/ppermute | solution.py:38
  202.2 2.8 second.2
  206.7 4.7 %norm_back.1 = (f32[512,1024]{1,0:T(8,128)S(1)}, bf16[512,1024]{1,0:T(8,128)(2,1)}, f32[8,1024]{1,0:T(8,128)S(1)}) custom-call(s32[4]{0:T(128)S(1)} %pad_add_fusion.1.flags, f32[8,1024]{1,0:T(8,128)S(1)} %select_maximum_fusion.vec_ref, f32[512,1024]{1,0:T(8,128)S(1)} %copy-done.53, f32[512,1024]{1,0:T(8,128)S(1)} %convolution_add_fusion.1.own_ref, ...), custom_call_target="tpu_custom_call" | custom-call | flops 1024 | bytes 1024 | tf_op jit(solution)/shard_map/norm_back/pallas_call | solution.py:232
  212.8 8.2 %weight_grads.2 = (bf16[1024,512]{1,0:T(8,128)(2,1)}, bf16[1024,512]{1,0:T(8,128)(2,1)S(1)}, bf16[512,1024]{1,0:T(8,128)(2,1)}, bf16[512,1024]{1,0:T(8,128)(2,1)S(1)}) custom-call(bf16[1024,1024]{1,0:T(8,128)(2,1)S(1)} %copy-done.43, bf16[1024,1024]{1,0:T(8,128)(2,1)S(1)} %copy-done.45, ...), custom_call_target="tpu_custom_call" | custom-call | flops 1024 | bytes 1024 | tf_op jit(solution)/shard_map/weight_grads/pallas_call | solution.py:342
  234.9 4.2 collective-permute-done.32.a_near
  241.3 2.5 joined.1
  247.7 7.2 %attend_back.4.left_ref = bf16[1024,384]{1,0:T(8,128)(2,1)S(1)} custom-call(bf16[1024,384]{1,0:T(8,128)(2,1)S(1)} %copy-done.70, bf16[2,1024,1024]{2,1,0:T(8,128)(2,1)} %get-tuple-element.214.exp_ref, bf16[1024,128]{1,0:T(8,128)(2,1)S(1)} %copy-done.59, f32[1024,128]{1,0:T(8,128)S(1)} %copy-done.73, bf16[1024,256]{1,0:T(8,128)(2,1)S(1)} %copy-done.48), custom_call_target="tpu_custom_call" | custom-call | flops 1024 | bytes 1024 | tf_op jit(solution)/shard_map/attend_back/pallas_call | solution.py:138
  258.1 7.2 %attend_back.5.left_ref = bf16[1024,384]{1,0:T(8,128)(2,1)S(1)} custom-call(bf16[1024,384]{1,0:T(8,128)(2,1)S(1)} %copy-done.71, bf16[2,1024,1024]{2,1,0:T(8,128)(2,1)} %get-tuple-element.209.exp_ref, bf16[1024,128]{1,0:T(8,128)(2,1)S(1)} %copy-done.61, f32[1024,128]{1,0:T(8,128)S(1)} %copy-done.75, bf16[1024,256]{1,0:T(8,128)(2,1)S(1)} %copy-done.49), custom_call_target="tpu_custom_call" | custom-call | flops 1024 | bytes 1024 | tf_op jit(solution)/shard_map/attend_back/pallas_call | solution.py:138
  267.3 3.2 fusion.47
  270.7 3.4 fusion.45
  274.1 3.6 collective-permute-done.34.arrived_a
  277.7 2.8 second.3
  286.5 7.1 %attend_back.6.left_ref = bf16[1024,384]{1,0:T(8,128)(2,1)S(1)} custom-call(bf16[1024,768]{1,0:T(8,128)(2,1)S(1)} %copy-done.17, bf16[4,1024,1024]{2,1,0:T(8,128)(2,1)} %get-tuple-element.229.exp_ref, bf16[1024,256]{1,0:T(8,128)(2,1)S(1)} %get-tuple-element.165.mixed_ref.left_ref, f32[1024,256]{1,0:T(8,128)S(1)} %copy-done.19, bf16[1024,256]{1,0:T(8,128)(2,1)S(1)} %copy-done.46), custom_call_target="tpu_custom_call" | custom-call | flops 1024 | bytes 1024 | tf_op jit(solution)/shard_map/attend_back/pallas_call | solution.py:138
  294.9 2.6 all-reduce.5.cloned.1.call-done
  297.5 2.8 collective-permute-done.37.b_row
  302.4 2.8 merge.1
  314.3 7.2 %attend_back.7.left_ref = bf16[1024,384]{1,0:T(8,128)(2,1)S(1)} custom-call(bf16[1024,768]{1,0:T(8,128)(2,1)S(1)} %copy-done.18, bf16[4,1024,1024]{2,1,0:T(8,128)(2,1)} %get-tuple-element.229.exp_ref, bf16[1024,256]{1,0:T(8,128)(2,1)S(1)} %get-tuple-element.165.mixed_ref.left_ref, f32[1024,256]{1,0:T(8,128)S(1)} %copy-done.20, bf16[1024,256]{1,0:T(8,128)(2,1)S(1)} %copy-done.47), custom_call_target="tpu_custom_call" | custom-call | flops 1024 | bytes 1024 | tf_op jit(solution)/shard_map/attend_back/pallas_call | solution.py:138
  322.7 2.2 constant_dynamic-update-slice_fusion.23
  327.2 4.5 %collective-permute-done.44 = bf16[448,1024]{1,0:T(8,128)(2,1)} collective-permute-done((bf16[448,1024]{1,0:T(8,128)(2,1)}, bf16[448,1024]{1,0:T(8,128)(2,1)}, u32[]{:S(2)}, u32[]{:S(2)}) %collective-permute-start.44) | collective-permute-done | bytes 917536 | tf_op jit(solution)/shard_map/ppermute | solution.py:34
  338.4 2.2 fusion.46
  348.4 4.3 %collective-permute-done.42 = bf16[256,512]{1,0:T(8,128)(2,1)S(1)} collective-permute-done((bf16[256,512]{1,0:T(8,128)(2,1)S(1)}, bf16[256,512]{1,0:T(8,128)(2,1)S(1)}, u32[]{:S(2)}, u32[]{:S(2)}) %collective-permute-start.42) | collective-permute-done | bytes 262176 | tf_op jit(solution)/shard_map/ppermute | solution.py:538
  358.7 6.8 %collective-permute-done.50 = bf16[544,512]{1,0:T(8,128)(2,1)S(1)} collective-permute-done((bf16[544,512]{1,0:T(8,128)(2,1)S(1)}, bf16[544,512]{1,0:T(8,128)(2,1)S(1)}, u32[]{:S(2)}, u32[]{:S(2)}) %collective-permute-start.50) | collective-permute-done | bytes 557088 | tf_op jit(solution)/shard_map/ppermute | solution.py:538
  366.1 2.9 collective-permute-start.54
  369.0 18.0 %collective-permute-done.51 = bf16[272,512]{1,0:T(8,128)(2,1)S(1)} collective-permute-done((bf16[272,512]{1,0:T(8,128)(2,1)S(1)}, bf16[272,512]{1,0:T(8,128)(2,1)S(1)}, u32[]{:S(2)}, u32[]{:S(2)}) %collective-permute-start.51) | collective-permute-done | bytes 278560 | tf_op jit(solution)/shard_map/ppermute | solution.py:538
  389.4 5.2 %collective-permute-done.54 = bf16[256,512]{1,0:T(8,128)(2,1)S(1)} collective-permute-done((bf16[256,512]{1,0:T(8,128)(2,1)S(1)}, bf16[256,512]{1,0:T(8,128)(2,1)S(1)}, u32[]{:S(2)}, u32[]{:S(2)}) %collective-permute-start.54) | collective-permute-done | bytes 262176 | tf_op jit(solution)/shard_map/ppermute | solution.py:540
  394.9 3.7 collective-permute-done.52
  404.5 5.3 %collective-permute-done.55 = bf16[512,512]{1,0:T(8,128)(2,1)S(1)} collective-permute-done((bf16[512,512]{1,0:T(8,128)(2,1)S(1)}, bf16[512,512]{1,0:T(8,128)(2,1)S(1)}, u32[]{:S(2)}, u32[]{:S(2)}) %collective-permute-start.55) | collective-permute-done | bytes 524320 | tf_op jit(solution)/shard_map/ppermute | solution.py:540
  411.6 2.9 copy.32
  416.1 2.7 collective-permute-done.53
  (488 shorter events, 153.0 us)
Async XLA Ops:
  7.3 290.2 %all-reduce.5.cloned.1.call-start = ((), (), s32[]{:S(2)}) async-start(), calls=%async_computation | async-start | bytes 2097152 | tf_op jit(solution)/shard_map/psum | solution.py:741
  9.7 14.9 %collective-permute-start = (bf16[1024,256]{1,0:T(8,128)(2,1)S(1)}, bf16[1024,256]{1,0:T(8,128)(2,1)S(1)}, u32[]{:S(2)}, u32[]{:S(2)}) collective-permute-start(bf16[1024,256]{1,0:T(8,128)(2,1)S(1)} %get-tuple-element.299), channel_id=1, source_target_pairs={{0,2},{1,3},{2,0},{3,1},{4,6},{5,7},{6,4},{7,5},{8,10},{9,11},{10,... | collective-permute-start | bytes 1572872 | tf_op jit(solution)/shard_map/ppermute | solution.py:34
  12.6 16.2 %collective-permute-start.1 = (bf16[1024,256]{1,0:T(8,128)(2,1)}, bf16[1024,256]{1,0:T(8,128)(2,1)}, u32[]{:S(2)}, u32[]{:S(2)}) collective-permute-start(bf16[1024,256]{1,0:T(8,128)(2,1)} %get-tuple-element.298), channel_id=1, source_target_pairs={{0,1},{1,0},{2,3},{3,2},{4,5},{5,4},{6,7},{7,6},{8,9},{9,8},{10,11... | collective-permute-start | bytes 1572872 | tf_op jit(solution)/shard_map/ppermute | solution.py:29
  12.6 30.3 %collective-permute-start.5 = (bf16[512,768]{1,0:T(8,128)(2,1)S(1)}, bf16[512,768]{1,0:T(8,128)(2,1)}, u32[]{:S(2)}, u32[]{:S(2)}) collective-permute-start(bf16[512,768]{1,0:T(8,128)(2,1)S(1)} %copy-done.31), channel_id=1, source_target_pairs={{0,4},{4,0},{1,5},{5,1},{2,6},{6,2},{3,7},{7,3},{8,12},{12,8},{9,1... | collective-permute-start | bytes 2359304 | tf_op jit(solution)/shard_map/ppermute | solution.py:38
  27.2 15.7 %collective-permute-start.6 = (bf16[256,512]{1,0:T(8,128)(2,1)}, bf16[256,512]{1,0:T(8,128)(2,1)}, u32[]{:S(2)}, u32[]{:S(2)}) collective-permute-start(bf16[256,512]{1,0:T(8,128)(2,1)} %param.19), channel_id=1, source_target_pairs={{0,4},{4,0},{1,5},{5,1},{2,6},{6,2},{3,7},{7,3},{8,12},{12,8},{9,1... | collective-permute-start | bytes 786440 | tf_op jit(solution)/shard_map/ppermute | solution.py:38
  28.8 12.7 %collective-permute-start.4 = (f32[3328]{0:T(1024)S(1)}, f32[3328]{0:T(1024)S(1)}, u32[]{:S(2)}, u32[]{:S(2)}) collective-permute-start(f32[3328]{0:T(1024)S(1)} %constant_dynamic-update-slice_fusion.36), channel_id=1, source_target_pairs={{0,2},{1,3},{2,0},{3,1},{4,6},{5,7},{6,4},{7,5},{8,10},{9,11},{10,... | collective-permute-start | bytes 39944 | tf_op jit(solution)/shard_map/ppermute | solution.py:34
  36.0 12.3 %collective-permute-start.7 = (bf16[512,384]{1,0:T(8,128)(2,1)}, bf16[512,384]{1,0:T(8,128)(2,1)S(1)}, u32[]{:S(2)}, u32[]{:S(2)}) collective-permute-start(bf16[512,384]{1,0:T(8,128)(2,1)} %get-tuple-element.300), channel_id=1, source_target_pairs={{0,2},{1,3},{2,0},{3,1},{4,6},{5,7},{6,4},{7,5},{8,10},{9,11},{10,... | collective-permute-start | bytes 1179656 | tf_op jit(solution)/shard_map/ppermute | solution.py:34
  37.5 29.7 %collective-permute-start.11 = (bf16[256,512]{1,0:T(8,128)(2,1)}, bf16[256,512]{1,0:T(8,128)(2,1)}, u32[]{:S(2)}, u32[]{:S(2)}) collective-permute-start(bf16[256,512]{1,0:T(8,128)(2,1)} %param.19), channel_id=1, source_target_pairs={{0,2},{1,3},{2,0},{3,1},{4,6},{5,7},{6,4},{7,5},{8,10},{9,11},{10,... | collective-permute-start | bytes 786440 | tf_op jit(solution)/shard_map/ppermute | solution.py:34
  41.5 25.6 %collective-permute-start.9 = (bf16[512,384]{1,0:T(8,128)(2,1)S(1)}, bf16[512,384]{1,0:T(8,128)(2,1)}, u32[]{:S(2)}, u32[]{:S(2)}) collective-permute-start(bf16[512,384]{1,0:T(8,128)(2,1)S(1)} %collective-permute-done.3.left_ref), channel_id=1, source_target_pairs={{0,4},{4,0},{1,5},{5,1},{2,6},{6,2},{3,7},{7,3},{8,12},{12,8},{9,1... | collective-permute-start | bytes 1179656 | tf_op jit(solution)/shard_map/ppermute | solution.py:38
  44.7 22.5 %collective-permute-start.10 = (bf16[512,384]{1,0:T(8,128)(2,1)}, bf16[512,384]{1,0:T(8,128)(2,1)}, u32[]{:S(2)}, u32[]{:S(2)}) collective-permute-start(bf16[512,384]{1,0:T(8,128)(2,1)} %slice.245), channel_id=1, source_target_pairs={{0,2},{1,3},{2,0},{3,1},{4,6},{5,7},{6,4},{7,5},{8,10},{9,11},{10,... | collective-permute-start | bytes 1179656 | tf_op jit(solution)/shard_map/ppermute | solution.py:34
  46.2 20.9 %collective-permute-start.12 = (bf16[256,512]{1,0:T(8,128)(2,1)}, bf16[256,512]{1,0:T(8,128)(2,1)}, u32[]{:S(2)}, u32[]{:S(2)}) collective-permute-start(bf16[256,512]{1,0:T(8,128)(2,1)} %collective-permute-done.6), channel_id=1, source_target_pairs={{0,2},{1,3},{2,0},{3,1},{4,6},{5,7},{6,4},{7,5},{8,10},{9,11},{10,... | collective-permute-start | bytes 786440 | tf_op jit(solution)/shard_map/ppermute | solution.py:34
  49.0 32.3 %collective-permute-start.13 = (bf16[512,1024]{1,0:T(8,128)(2,1)}, bf16[512,1024]{1,0:T(8,128)(2,1)}, u32[]{:S(2)}, u32[]{:S(2)}) collective-permute-start(bf16[512,1024]{1,0:T(8,128)(2,1)} %left_ref.4), channel_id=1, source_target_pairs={{0,4},{4,0},{1,5},{5,1},{2,6},{6,2},{3,7},{7,3},{8,12},{12,8},{9,1... | collective-permute-start | bytes 3145736 | tf_op jit(solution)/shard_map/ppermute | solution.py:38
  67.2 28.1 %collective-permute-start.14 = (bf16[1024,512]{1,0:T(8,128)(2,1)}, bf16[1024,512]{1,0:T(8,128)(2,1)S(1)}, u32[]{:S(2)}, u32[]{:S(2)}) collective-permute-start(bf16[1024,512]{1,0:T(8,128)(2,1)} %left_ref.5), channel_id=1, source_target_pairs={{0,4},{4,0},{1,5},{5,1},{2,6},{6,2},{3,7},{7,3},{8,12},{12,8},{9,1... | collective-permute-start | bytes 3145736 | tf_op jit(solution)/shard_map/ppermute | solution.py:38
  67.9 27.4 %collective-permute-start.15 = (bf16[512,1024]{1,0:T(8,128)(2,1)}, bf16[512,1024]{1,0:T(8,128)(2,1)}, u32[]{:S(2)}, u32[]{:S(2)}) collective-permute-start(bf16[512,1024]{1,0:T(8,128)(2,1)} %left_ref.4), channel_id=1, source_target_pairs={{0,2},{1,3},{2,0},{3,1},{4,6},{5,7},{6,4},{7,5},{8,10},{9,11},{10,... | collective-permute-start | bytes 3145736 | tf_op jit(solution)/shard_map/ppermute | solution.py:34
  69.3 27.0 %collective-permute-start.8 = (f32[6,512]{1,0:T(8,128)S(1)}, f32[6,512]{1,0:T(8,128)S(1)}, u32[]{:S(2)}, u32[]{:S(2)}) collective-permute-start(f32[6,512]{1,0:T(8,128)S(1)} %constant_dynamic-update-slice_fusion.2), channel_id=1, source_target_pairs={{0,1},{1,0},{2,3},{3,2},{4,5},{5,4},{6,7},{7,6},{8,9},{9,8},{10,11... | collective-permute-start | bytes 36872 | tf_op jit(solution)/shard_map/ppermute | solution.py:29
  103.0 26.3 %collective-permute-start.18 = (bf16[512,1024]{1,0:T(8,128)(2,1)}, bf16[512,1024]{1,0:T(8,128)(2,1)S(1)}, u32[]{:S(2)}, u32[]{:S(2)}) collective-permute-start(bf16[512,1024]{1,0:T(8,128)(2,1)} %collective-permute-done.15.left_ref), channel_id=1, source_target_pairs={{0,4},{4,0},{1,5},{5,1},{2,6},{6,2},{3,7},{7,3},{8,12},{12,8},{9,1... | collective-permute-start | bytes 3145736 | tf_op jit(solution)/shard_map/ppermute | solution.py:38
  104.2 25.1 %collective-permute-start.19 = (bf16[1024,512]{1,0:T(8,128)(2,1)}, bf16[1024,512]{1,0:T(8,128)(2,1)S(1)}, u32[]{:S(2)}, u32[]{:S(2)}) collective-permute-start(bf16[1024,512]{1,0:T(8,128)(2,1)} %left_ref.5), channel_id=1, source_target_pairs={{0,2},{1,3},{2,0},{3,1},{4,6},{5,7},{6,4},{7,5},{8,10},{9,11},{10,... | collective-permute-start | bytes 3145736 | tf_op jit(solution)/shard_map/ppermute | solution.py:34
  129.3 14.9 %collective-permute-start.20 = (bf16[512,512]{1,0:T(8,128)(2,1)S(1)}, bf16[512,512]{1,0:T(8,128)(2,1)S(1)}, u32[]{:S(2)}, u32[]{:S(2)}) collective-permute-start(bf16[512,512]{1,0:T(8,128)(2,1)S(1)} %slice.256), channel_id=1, source_target_pairs={{0,2},{1,3},{2,0},{3,1},{4,6},{5,7},{6,4},{7,5},{8,10},{9,11},{10,... | collective-permute-start | bytes 1572872 | tf_op jit(solution)/shard_map/ppermute | solution.py:34
  130.9 13.3 %collective-permute-start.21 = (bf16[512,512]{1,0:T(8,128)(2,1)S(1)}, bf16[512,512]{1,0:T(8,128)(2,1)S(1)}, u32[]{:S(2)}, u32[]{:S(2)}) collective-permute-start(bf16[512,512]{1,0:T(8,128)(2,1)S(1)} %slice.257), channel_id=1, source_target_pairs={{0,4},{4,0},{1,5},{5,1},{2,6},{6,2},{3,7},{7,3},{8,12},{12,8},{9,1... | collective-permute-start | bytes 1572872 | tf_op jit(solution)/shard_map/ppermute | solution.py:38
  131.5 21.8 %collective-permute-start.23 = (bf16[1024,256]{1,0:T(8,128)(2,1)S(1)}, bf16[1024,256]{1,0:T(8,128)(2,1)S(1)}, u32[]{:S(2)}, u32[]{:S(2)}) collective-permute-start(bf16[1024,256]{1,0:T(8,128)(2,1)S(1)} %dynamic-slice_bitcast_fusion), channel_id=1, source_target_pairs={{0,2},{1,3},{2,0},{3,1},{4,6},{5,7},{6,4},{7,5},{8,10},{9,11},{10,... | collective-permute-start | bytes 1572872 | tf_op jit(solution)/shard_map/ppermute | solution.py:34
  175.8 25.7 %collective-permute-start.29 = (bf16[1024,512]{1,0:T(8,128)(2,1)}, bf16[1024,512]{1,0:T(8,128)(2,1)}, u32[]{:S(2)}, u32[]{:S(2)}) collective-permute-start(bf16[1024,512]{1,0:T(8,128)(2,1)} %get-tuple-element.194), channel_id=1, source_target_pairs={{0,4},{4,0},{1,5},{5,1},{2,6},{6,2},{3,7},{7,3},{8,12},{12,8},{9,1... | collective-permute-start | bytes 3145736 | tf_op jit(solution)/shard_map/ppermute | solution.py:38
  176.8 25.4 %collective-permute-start.30 = (bf16[512,1024]{1,0:T(8,128)(2,1)}, bf16[512,1024]{1,0:T(8,128)(2,1)}, u32[]{:S(2)}, u32[]{:S(2)}) collective-permute-start(bf16[512,1024]{1,0:T(8,128)(2,1)} %get-tuple-element.195), channel_id=1, source_target_pairs={{0,2},{1,3},{2,0},{3,1},{4,6},{5,7},{6,4},{7,5},{8,10},{9,11},{10,... | collective-permute-start | bytes 3145736 | tf_op jit(solution)/shard_map/ppermute | solution.py:34
  190.3 11.9 %collective-permute-start.28 = (bf16[512,1024]{1,0:T(8,128)(2,1)}, bf16[512,1024]{1,0:T(8,128)(2,1)}, u32[]{:S(2)}, u32[]{:S(2)}) collective-permute-start(bf16[512,1024]{1,0:T(8,128)(2,1)} %add_convert_fusion), channel_id=1, source_target_pairs={{0,1},{1,0},{2,3},{3,2},{4,5},{5,4},{6,7},{7,6},{8,9},{9,8},{10,11... | collective-permute-start | bytes 3145736 | tf_op jit(solution)/shard_map/ppermute | solution.py:29
  212.7 14.9 %collective-permute-start.31 = (bf16[512,1024]{1,0:T(8,128)(2,1)}, bf16[512,1024]{1,0:T(8,128)(2,1)}, u32[]{:S(2)}, u32[]{:S(2)}) collective-permute-start(bf16[512,1024]{1,0:T(8,128)(2,1)} %get-tuple-element.207), channel_id=1, source_target_pairs={{0,1},{1,0},{2,3},{3,2},{4,5},{5,4},{6,7},{7,6},{8,9},{9,8},{10,11... | collective-permute-start | bytes 3145736 | tf_op jit(solution)/shard_map/ppermute | solution.py:29
  224.9 14.2 %collective-permute-start.32 = (bf16[512,512]{1,0:T(8,128)(2,1)}, bf16[512,512]{1,0:T(8,128)(2,1)}, u32[]{:S(2)}, u32[]{:S(2)}) collective-permute-start(bf16[512,512]{1,0:T(8,128)(2,1)} %get-tuple-element.211), channel_id=1, source_target_pairs={{0,2},{1,3},{2,0},{3,1},{4,6},{5,7},{6,4},{7,5},{8,10},{9,11},{10,... | collective-permute-start | bytes 1572872 | tf_op jit(solution)/shard_map/ppermute | solution.py:34
  226.1 15.1 %collective-permute-start.33 = (bf16[512,512]{1,0:T(8,128)(2,1)}, bf16[512,512]{1,0:T(8,128)(2,1)}, u32[]{:S(2)}, u32[]{:S(2)}) collective-permute-start(bf16[512,512]{1,0:T(8,128)(2,1)} %get-tuple-element.212), channel_id=1, source_target_pairs={{0,4},{4,0},{1,5},{5,1},{2,6},{6,2},{3,7},{7,3},{8,12},{12,8},{9,1... | collective-permute-start | bytes 1572872 | tf_op jit(solution)/shard_map/ppermute | solution.py:38
  232.8 92.1 %collective-permute-start.40 = (bf16[512,512]{1,0:T(8,128)(2,1)}, bf16[512,512]{1,0:T(8,128)(2,1)}, u32[]{:S(2)}, u32[]{:S(2)}) collective-permute-start(bf16[512,512]{1,0:T(8,128)(2,1)} %pad_maximum_fusion.7), channel_id=1, source_target_pairs={{0,4},{4,0},{1,5},{5,1},{2,6},{6,2},{3,7},{7,3},{8,12},{12,8},{9,1... | collective-permute-start | bytes 1572872 | tf_op jit(solution)/shard_map/ppermute | solution.py:38
  243.8 30.3 %collective-permute-start.35 = (bf16[512,1024]{1,0:T(8,128)(2,1)}, bf16[512,1024]{1,0:T(8,128)(2,1)}, u32[]{:S(2)}, u32[]{:S(2)}) collective-permute-start(bf16[512,1024]{1,0:T(8,128)(2,1)} %get-tuple-element.224), channel_id=1, source_target_pairs={{0,2},{1,3},{2,0},{3,1},{4,6},{5,7},{6,4},{7,5},{8,10},{9,11},{10,... | collective-permute-start | bytes 3145736 | tf_op jit(solution)/shard_map/ppermute | solution.py:34
  255.0 22.7 %collective-permute-start.34 = (bf16[1024,512]{1,0:T(8,128)(2,1)}, bf16[1024,512]{1,0:T(8,128)(2,1)}, u32[]{:S(2)}, u32[]{:S(2)}) collective-permute-start(bf16[1024,512]{1,0:T(8,128)(2,1)} %get-tuple-element.222), channel_id=1, source_target_pairs={{0,4},{4,0},{1,5},{5,1},{2,6},{6,2},{3,7},{7,3},{8,12},{12,8},{9,1... | collective-permute-start | bytes 3145736 | tf_op jit(solution)/shard_map/ppermute | solution.py:38
  281.4 43.5 %collective-permute-start.39 = (bf16[384,512]{1,0:T(8,128)(2,1)}, bf16[384,512]{1,0:T(8,128)(2,1)}, u32[]{:S(2)}, u32[]{:S(2)}) collective-permute-start(bf16[384,512]{1,0:T(8,128)(2,1)} %slice.263), channel_id=1, source_target_pairs={{0,4},{4,0},{1,5},{5,1},{2,6},{6,2},{3,7},{7,3},{8,12},{12,8},{9,1... | collective-permute-start | bytes 1179656 | tf_op jit(solution)/shard_map/ppermute | solution.py:38
  284.5 13.0 %collective-permute-start.36 = (bf16[512,512]{1,0:T(8,128)(2,1)}, bf16[512,512]{1,0:T(8,128)(2,1)}, u32[]{:S(2)}, u32[]{:S(2)}) collective-permute-start(bf16[512,512]{1,0:T(8,128)(2,1)} %get-tuple-element.236), channel_id=1, source_target_pairs={{0,2},{1,3},{2,0},{3,1},{4,6},{5,7},{6,4},{7,5},{8,10},{9,11},{10,... | collective-permute-start | bytes 1572872 | tf_op jit(solution)/shard_map/ppermute | solution.py:34
  285.9 14.4 %collective-permute-start.37 = (bf16[512,512]{1,0:T(8,128)(2,1)}, bf16[512,512]{1,0:T(8,128)(2,1)}, u32[]{:S(2)}, u32[]{:S(2)}) collective-permute-start(bf16[512,512]{1,0:T(8,128)(2,1)} %get-tuple-element.237), channel_id=1, source_target_pairs={{0,4},{4,0},{1,5},{5,1},{2,6},{6,2},{3,7},{7,3},{8,12},{12,8},{9,1... | collective-permute-start | bytes 1572872 | tf_op jit(solution)/shard_map/ppermute | solution.py:38
  306.0 18.8 %collective-permute-start.38 = (bf16[512,512]{1,0:T(8,128)(2,1)}, bf16[512,512]{1,0:T(8,128)(2,1)}, u32[]{:S(2)}, u32[]{:S(2)}) collective-permute-start(bf16[512,512]{1,0:T(8,128)(2,1)} %get-tuple-element.241), channel_id=1, source_target_pairs={{0,8},{8,0},{16,24},{24,16},{1,9},{9,1},{17,25},{25,17},{2,10},{10... | collective-permute-start | bytes 1572872 | tf_op jit(solution)/shard_map/ppermute | solution.py:538
  310.5 14.3 %collective-permute-start.41 = (bf16[384,512]{1,0:T(8,128)(2,1)}, bf16[384,512]{1,0:T(8,128)(2,1)}, u32[]{:S(2)}, u32[]{:S(2)}) collective-permute-start(bf16[384,512]{1,0:T(8,128)(2,1)} %slice.313), channel_id=1, source_target_pairs={{0,4},{4,0},{1,5},{5,1},{2,6},{6,2},{3,7},{7,3},{8,12},{12,8},{9,1... | collective-permute-start | bytes 1179656 | tf_op jit(solution)/shard_map/ppermute | solution.py:38
  313.0 18.8 %collective-permute-start.44 = (bf16[448,1024]{1,0:T(8,128)(2,1)}, bf16[448,1024]{1,0:T(8,128)(2,1)}, u32[]{:S(2)}, u32[]{:S(2)}) collective-permute-start(bf16[448,1024]{1,0:T(8,128)(2,1)} %maximum_maximum_fusion), channel_id=1, source_target_pairs={{0,2},{1,3},{2,0},{3,1},{4,6},{5,7},{6,4},{7,5},{8,10},{9,11},{10,... | collective-permute-start | bytes 2752520 | tf_op jit(solution)/shard_map/ppermute | solution.py:34
  334.9 13.4 %collective-permute-start.47 = (bf16[256,512]{1,0:T(8,128)(2,1)S(1)}, bf16[256,512]{1,0:T(8,128)(2,1)S(1)}, u32[]{:S(2)}, u32[]{:S(2)}) collective-permute-start(bf16[256,512]{1,0:T(8,128)(2,1)S(1)} %slice.329), channel_id=1, source_target_pairs={{0,2},{1,3},{2,0},{3,1},{4,6},{5,7},{6,4},{7,5},{8,10},{9,11},{10,... | collective-permute-start | bytes 786440 | tf_op jit(solution)/shard_map/ppermute | solution.py:34
  337.6 15.1 %collective-permute-start.46 = (bf16[384,512]{1,0:T(8,128)(2,1)S(1)}, bf16[384,512]{1,0:T(8,128)(2,1)S(1)}, u32[]{:S(2)}, u32[]{:S(2)}) collective-permute-start(bf16[384,512]{1,0:T(8,128)(2,1)S(1)} %add_convert_fusion.10), channel_id=1, source_target_pairs={{0,2},{1,3},{2,0},{3,1},{4,6},{5,7},{6,4},{7,5},{8,10},{9,11},{10,... | collective-permute-start | bytes 1179656 | tf_op jit(solution)/shard_map/ppermute | solution.py:34
  340.6 12.1 %collective-permute-start.45 = (bf16[448,512]{1,0:T(8,128)(2,1)S(1)}, bf16[448,512]{1,0:T(8,128)(2,1)S(1)}, u32[]{:S(2)}, u32[]{:S(2)}) collective-permute-start(bf16[448,512]{1,0:T(8,128)(2,1)S(1)} %slice.326), channel_id=1, source_target_pairs={{0,4},{4,0},{1,5},{5,1},{2,6},{6,2},{3,7},{7,3},{8,12},{12,8},{9,1... | collective-permute-start | bytes 1376264 | tf_op jit(solution)/shard_map/ppermute | solution.py:38
  354.3 11.3 %collective-permute-start.50 = (bf16[544,512]{1,0:T(8,128)(2,1)S(1)}, bf16[544,512]{1,0:T(8,128)(2,1)S(1)}, u32[]{:S(2)}, u32[]{:S(2)}) collective-permute-start(bf16[544,512]{1,0:T(8,128)(2,1)S(1)} %broadcast_select_fusion), channel_id=1, source_target_pairs={{0,8},{8,0},{16,24},{24,16},{1,9},{9,1},{17,25},{25,17},{2,10},{10... | collective-permute-start | bytes 1671176 | tf_op jit(solution)/shard_map/ppermute | solution.py:538
  358.7 40.2 %collective-permute-start.48 = (bf16[1024,512]{1,0:T(8,128)(2,1)S(1)}, bf16[1024,512]{1,0:T(8,128)(2,1)S(1)}, u32[]{:S(2)}, u32[]{:S(2)}) collective-permute-start(bf16[1024,512]{1,0:T(8,128)(2,1)S(1)} %get-tuple-element.259), channel_id=1, source_target_pairs={{0,1},{1,0},{2,3},{3,2},{4,5},{5,4},{6,7},{7,6},{8,9},{9,8},{10,11... | collective-permute-start | bytes 3145736 | tf_op jit(solution)/shard_map/ppermute | solution.py:29
  365.8 21.1 %collective-permute-start.51 = (bf16[272,512]{1,0:T(8,128)(2,1)S(1)}, bf16[272,512]{1,0:T(8,128)(2,1)S(1)}, u32[]{:S(2)}, u32[]{:S(2)}) collective-permute-start(bf16[272,512]{1,0:T(8,128)(2,1)S(1)} %broadcast_select_fusion.1), channel_id=1, source_target_pairs={{0,16},{8,24},{16,0},{24,8},{1,17},{9,25},{17,1},{25,9},{2,18},{10... | collective-permute-start | bytes 835592 | tf_op jit(solution)/shard_map/ppermute | solution.py:538
  365.9 21.2 %collective-permute-start.25 = (bf16[512,512]{1,0:T(8,128)(2,1)S(1)}, bf16[512,512]{1,0:T(8,128)(2,1)S(1)}, u32[]{:S(2)}, u32[]{:S(2)}) collective-permute-start(bf16[512,512]{1,0:T(8,128)(2,1)S(1)} %copy-done.90), channel_id=1, source_target_pairs={{0,1},{1,0},{2,3},{3,2},{4,5},{5,4},{6,7},{7,6},{8,9},{9,8},{10,11... | collective-permute-start | bytes 1572872 | tf_op jit(solution)/shard_map/ppermute | solution.py:29
  366.1 28.5 %collective-permute-start.54 = (bf16[256,512]{1,0:T(8,128)(2,1)S(1)}, bf16[256,512]{1,0:T(8,128)(2,1)S(1)}, u32[]{:S(2)}, u32[]{:S(2)}) collective-permute-start(bf16[256,512]{1,0:T(8,128)(2,1)S(1)} %add_convert_fusion.12), channel_id=1, source_target_pairs={{0,16},{8,24},{16,0},{24,8},{1,17},{9,25},{17,1},{25,9},{2,18},{10... | collective-permute-start | bytes 786440 | tf_op jit(solution)/shard_map/ppermute | solution.py:540
  387.1 11.5 %collective-permute-start.52 = (bf16[272,512]{1,0:T(8,128)(2,1)S(1)}, bf16[272,512]{1,0:T(8,128)(2,1)S(1)}, u32[]{:S(2)}, u32[]{:S(2)}) collective-permute-start(bf16[272,512]{1,0:T(8,128)(2,1)S(1)} %add_convert_fusion.11), channel_id=1, source_target_pairs={{0,16},{8,24},{16,0},{24,8},{1,17},{9,25},{17,1},{25,9},{2,18},{10... | collective-permute-start | bytes 835592 | tf_op jit(solution)/shard_map/ppermute | solution.py:540
  387.8 13.6 %collective-permute-start.26 = (bf16[1024,256]{1,0:T(8,128)(2,1)S(1)}, bf16[1024,256]{1,0:T(8,128)(2,1)S(1)}, u32[]{:S(2)}, u32[]{:S(2)}) collective-permute-start(bf16[1024,256]{1,0:T(8,128)(2,1)S(1)} %get-tuple-element.186), channel_id=1, source_target_pairs={{0,2},{1,3},{2,0},{3,1},{4,6},{5,7},{6,4},{7,5},{8,10},{9,11},{10,... | collective-permute-start | bytes 1572872 | tf_op jit(solution)/shard_map/ppermute | solution.py:34
  394.8 15.1 %collective-permute-start.55 = (bf16[512,512]{1,0:T(8,128)(2,1)S(1)}, bf16[512,512]{1,0:T(8,128)(2,1)S(1)}, u32[]{:S(2)}, u32[]{:S(2)}) collective-permute-start(bf16[512,512]{1,0:T(8,128)(2,1)S(1)} %maximum_select_fusion.3), channel_id=1, source_target_pairs={{0,8},{8,0},{16,24},{24,16},{1,9},{9,1},{17,25},{25,17},{2,10},{10... | collective-permute-start | bytes 1572872 | tf_op jit(solution)/shard_map/ppermute | solution.py:540
  398.8 19.9 %collective-permute-start.53 = (bf16[544,512]{1,0:T(8,128)(2,1)S(1)}, bf16[544,512]{1,0:T(8,128)(2,1)S(1)}, u32[]{:S(2)}, u32[]{:S(2)}) collective-permute-start(bf16[544,512]{1,0:T(8,128)(2,1)S(1)} %maximum_select_fusion.2), channel_id=1, source_target_pairs={{0,8},{8,0},{16,24},{24,16},{1,9},{9,1},{17,25},{25,17},{2,10},{10... | collective-permute-start | bytes 1671176 | tf_op jit(solution)/shard_map/ppermute | solution.py:540
  399.7 14.8 %collective-permute-start.49 = (bf16[1024,256]{1,0:T(8,128)(2,1)S(1)}, bf16[1024,256]{1,0:T(8,128)(2,1)S(1)}, u32[]{:S(2)}, u32[]{:S(2)}) collective-permute-start(bf16[1024,256]{1,0:T(8,128)(2,1)S(1)} %get-tuple-element.261), channel_id=1, source_target_pairs={{0,2},{1,3},{2,0},{3,1},{4,6},{5,7},{6,4},{7,5},{8,10},{9,11},{10,... | collective-permute-start | bytes 1572872 | tf_op jit(solution)/shard_map/ppermute | solution.py:34
  (122 other events, 796.9 us)
Sparse Core Ops, SparseCore 0:
  244.8 52.6 all-reduce.4

commit v4 on v3

--- a/solution.py
+++ b/solution.py
@@ -97,7 +97,7 @@
     )(wide, left, right, bias.reshape(1, width), mask)
 
 
-def attend_back_kernel(chunk, qkv_ref, exp_ref, mixed_ref, inv_ref, grad_ref, out_ref):
+def attend_back_kernel(chunk, qkv_ref, exp_ref, mixed_ref, inv_ref, grad_ref, out_ref, sums_ref):
     count = qkv_ref.shape[0]
     lane = lax.broadcasted_iota(jnp.int32, (count, HEAD_DIM), 1)
     minus = jnp.where(lane < 2, -1.0, 0.0).astype(bf16)
@@ -130,6 +130,7 @@
             grad_value = value_part if grad_value is None else grad_value + value_part
         out_ref[:, base + HEAD_DIM : base + 2 * HEAD_DIM] = (grad_key.T * scale).astype(bf16)
         out_ref[:, base + 2 * HEAD_DIM : base + 3 * HEAD_DIM] = grad_value.T.astype(bf16)
+    sums_ref[...] = mm(jnp.ones((8, count), bf16), out_ref[...])
 
 
 def attend_back(qkv, exponent, mixed, inverse, grad_mixed, first=0, at=0):
@@ -144,8 +145,11 @@
         ]
         + [pl.BlockSpec((count, 2 * HEAD_DIM), lambda p: (0, p + first))] * 2
         + [pl.BlockSpec((count, 2 * HEAD_DIM), lambda p: (0, p + at))],
-        out_specs=pl.BlockSpec((count, 6 * HEAD_DIM), lambda p: (0, p)),
-        out_shape=jax.ShapeDtypeStruct((count, width), bf16),
+        out_specs=[
+            pl.BlockSpec((count, 6 * HEAD_DIM), lambda p: (0, p)),
+            pl.BlockSpec((8, 6 * HEAD_DIM), lambda p: (0, p)),
+        ],
+        out_shape=[jax.ShapeDtypeStruct((count, width), bf16), jax.ShapeDtypeStruct((8, width), f32)],
         compiler_params=pltpu.CompilerParams(vmem_limit_bytes=48 * 2**20),
         cost_estimate=QUICK,
         name="attend_back",
@@ -658,6 +662,10 @@
     down_near = to_chip(after(w_down, in_near))
     arrived = to_core(sum(mm(m[half:], w) for m, w in zip(mixed, w_outs)).astype(bf16))
     own = sum(mm(m[:half], w) for m, w in zip(mixed, w_outs))
+    own, in_far, down_near = hold(own, in_far, down_near)
+    cot_near = to_chip(after(pick(cotangent, 1 - chip), down_near))
+    down_far_a = to_chip(after(down_row[: mid // 2], down_near))
+    down_far_b = to_row(down_near[mid // 2 :])
     normed_one, inverse_one, first_out, first_low = by_rows(
         norm_one_kernel, flags, wide_vec, [wide[:half], own, arrived],
         [(model, f32), (128, f32), (model, f32), (model, bf16)], "norm_one",
@@ -666,12 +674,10 @@
 
     act_mine, slope_mine = feed(first_wide, w_in, in_row, in_biases[0])
     down_mine = jnp.concatenate([w_down, down_row], axis=1)
+    act_mine, cot_near = hold(act_mine, cot_near)
     ffn_mine = [mm(act_mine[half:], down_mine), mm(act_mine[:half], down_mine)]
-    ffn_mine[0], ffn_mine[1], in_far, down_near = hold(*ffn_mine, in_far, down_near)
-    down_far_a = to_chip(after(down_row[:mid], down_near))
-    down_far_b = to_row(down_near[mid:])
-    cot_near = to_chip(after(pick(cotangent, 1 - chip), down_near))
     act_other, slope_other = feed(first_wide, in_near, in_far, in_biases[1])
+    act_other, down_far_a, down_far_b = hold(act_other, down_far_a, down_far_b)
     down_far = jnp.concatenate([down_far_a, down_far_b], axis=0)
     down_other = jnp.concatenate([down_near, down_far], axis=1)
     arrived = to_core((ffn_mine[0] + mm(act_other[half:], down_other)).astype(bf16))
@@ -686,6 +692,7 @@
         [(2 * width, bf16), (2 * width, bf16), (model, f32), (model, bf16), (0, f32)], "norm_two",
     )
 
+    out_away = to_core(out_give)
     side = model // 2
 
     def second_sends(own_a, arrived_a, mine_b, arrived_b):
@@ -723,7 +730,10 @@
     arrived = to_core((mm(hid_mine[half:], in_mine, NT) + mm(hid_other[half:], in_other, NT)).astype(bf16))
     own = mm(hid_mine[:half], in_mine, NT) + mm(hid_other[:half], in_other, NT)
     in_away_a, in_own_a, in_other_b, in_mine_b = weight_grads(hid_other, hid_mine, first_wide)
-    own, arrived, *down_first = hold(own, arrived, *down_first)
+    own, arrived, out_away, *down_first = hold(own, arrived, out_away, *down_first)
+    out_keep, out_give = placed(
+        split_chip_kernel, flags, [out_keep, out_away], [shape(count, width)] * 2, "split_chip"
+    )
     (da, da_near), (db, db_row) = second_sends(down_own_a, down_first[0], down_mine_b, down_first[1])
     own, da, db = hold(own, da, db)
 
@@ -739,28 +749,33 @@
     grad_down = joined(da, da_near, db, db_row)
     in_first = [to_row(after(in_away_a, grad_down)), to_chip(after(in_other_b, grad_down))]
     grad_down = lax.psum(grad_down, "dp")
-    go_a = attend_back(*other_a, grad_mixed[1])
+    go_a, sum_oa = attend_back(*other_a, grad_mixed[1])
+    out_near_seq = to_chip(after(out_give, go_a))
     wt_oa = transposed(go_a, wide)
-    go_b = attend_back(*other_b, after(grad_mixed[1], wt_oa), at=1)
-    gm, go_b, wt_oa, *in_first = hold(grad_mixed[0], go_b, wt_oa, *in_first)
+    go_b, sum_ob = attend_back(*other_b, after(grad_mixed[1], wt_oa), at=1)
+    gm, go_b, wt_oa, out_near_seq, *in_first = hold(grad_mixed[0], go_b, wt_oa, out_near_seq, *in_first)
+    output = placed(
+        join_sequences_kernel, flags, [out_keep, out_near_seq], [shape(2, count, width)], "join_sequences"
+    )[0]
     (ia, ia_near), (ib, ib_row) = second_sends(in_own_a, in_first[0], in_mine_b, in_first[1])
     wt_ob = transposed(after(go_b, ia), wide)
     qkv_a_other = to_row(after(wt_oa[:, side:], ia))
-    gm_a = attend_back(*mine, after(gm, ia, ib, wt_ob))
+    gm_a, sum_ma = attend_back(*mine, after(gm, ia, ib, wt_ob))
     out_row_grads = to_row(jnp.concatenate([g[:, side:] for g in grad_outs[::-1]], axis=0))
-    gm_a, ia_near, ib_row, grad_down = hold(gm_a, ia_near, ib_row, grad_down)
+    gm_a, ia_near, ib_row, qkv_a_other, out_row_grads = hold(gm_a, ia_near, ib_row, qkv_a_other, out_row_grads)
+    a_near = to_chip(added(wt_oa[:, :side], qkv_a_other))
+    rows = grad_outs[0].shape[0]
+    out_sums = added(
+        jnp.concatenate([g[:, :side] for g in grad_outs[::-1]], axis=0), out_row_grads
+    )
+    out_near_grad = to_chip(out_sums[:rows])
     sum_in = merged(ia, ia_near, ib, ib_row)
     sum_in.send()
     wt_ma = transposed(gm_a, wide)
     qkv_a_mine = to_row(wt_ma[:, side:])
-    gm_b = attend_back(*mine, after(gm, wt_ma), first=1, at=1)
-    gm_b, qkv_a_other, out_row_grads, qkv_a_mine = sum_in.step(gm_b, qkv_a_other, out_row_grads, qkv_a_mine)
+    gm_b, sum_mb = attend_back(*mine, after(gm, wt_ma), first=1, at=1)
+    gm_b, a_near, qkv_a_mine, grad_down = sum_in.step(gm_b, a_near, qkv_a_mine, grad_down)
     wt_mb = transposed(gm_b, wide)
-    rows = grad_outs[0].shape[0]
-    out_sums = added(
-        jnp.concatenate([g[:, :side] for g in grad_outs[::-1]], axis=0), out_row_grads
-    )
-    out_near_grad = to_chip(out_sums[:rows])
 
     features = jnp.concatenate([sums_one[2:3], sums_one[:2], sums_two[2:3], sums_two[:2]], axis=0)
     f0, f1, f2, f3 = [features[:, i * width : (i + 1) * width] for i in range(4)]
@@ -770,9 +785,12 @@
     feature_mine = jnp.where(same, features[:, :width], features[:, width:])
     feature_near = jnp.where(same, features[:, width:], features[:, :width])
     extras = []
-    for g, i, f in zip(((gm_a, gm_b), (go_a, go_b)), grad_in_biases, (feature_mine, feature_near)):
-        sums = jnp.concatenate([jnp.sum(v, axis=0, dtype=f32) for v in g]).reshape(heads, 3, HEAD_DIM)
-        sums = jnp.stack([sums[:, 0], sums[:, 2]], axis=1).reshape(-1)
+    for g, i, f in zip(((sum_ma, sum_mb), (sum_oa, sum_ob)), grad_in_biases, (feature_mine, feature_near)):
+        sums = jnp.concatenate([v[0] for v in g])
+        three = 3 * HEAD_DIM
+        sums = jnp.concatenate(
+            [sums[three * h + at : three * h + at + HEAD_DIM] for h in range(heads) for at in (0, 2 * HEAD_DIM)]
+        )
         flat = jnp.concatenate([sums, i, f.reshape(-1)])
         lines = -(-flat.shape[0] // (64 * side)) * 64
         flat = jnp.pad(flat, (0, lines * side - flat.shape[0])).reshape(lines, side).astype(bf16)
@@ -780,21 +798,23 @@
 
     b_near = to_chip(jnp.concatenate([wt_ob, extras[1]], axis=0))
     sum_mine = added(wt_ma[:, :side], qkv_a_mine)
-    a_near = to_chip(added(wt_oa[:, :side], qkv_a_other))
     sum_b = added(jnp.concatenate([wt_mb, extras[0]], axis=0), b_near)
     b_row = to_row(sum_b[:, side:])
     grads = [jnp.concatenate([gm_a, after(gm_b, sum_b)], axis=1), go_a, go_b]
     grad_left, grad_right = [sum(mm(g, w, NT) for g, w in zip(grads, ws)) for ws in (lefts, rights)]
-    grad_left, grad_right, b_row, a_near, out_near_grad = sum_in.step(grad_left, grad_right, b_row, a_near, out_near_grad)
+    grad_left, grad_right, b_row, out_near_grad = sum_in.step(grad_left, grad_right, b_row, out_near_grad)
     sum_qkv = PairSum(
         jnp.concatenate(
             [added(sum_mine, a_near), added(sum_b[:, :side], b_row), added(out_sums[rows:], out_near_grad)], axis=0
         )
     )
     sum_qkv.send()
-    for _ in range(3):
-        sum_in.step()
-        sum_qkv.step()
+    while sum_in.todo and sum_qkv.todo:
+        sum_in.arrived, sum_qkv.arrived = hold(sum_in.arrived, sum_qkv.arrived)
+        for one in (sum_qkv, sum_in):
+            one.receive()
+            if one.todo:
+                one.send()
     grad_in = sum_in.finish()
     summed = sum_qkv.finish().astype(f32)
     grad_w_down, grad_w_in = grad_down, grad_in
@@ -811,12 +831,6 @@
     grad_wide = jnp.concatenate([grad_left, grad_right], axis=1)
     grad_wide = jnp.concatenate([grad_wide[:half] + grad_pre_one, grad_wide[half:]], axis=0)
 
-    keep, give = placed(
-        split_chip_kernel, flags, [out_keep, to_core(out_give)], [shape(count, width)] * 2, "split_chip"
-    )
-    output = placed(
-        join_sequences_kernel, flags, [keep, to_chip(give)], [shape(2, count, width)], "join_sequences"
-    )[0]
     keep, give = placed(
         split_core_kernel, flags, [grad_wide],
         [shape(count, 2 * width, dtype=f32), shape(count, 2 * width)], "split_core",

time: 438 us -> 428 us (0.977)
  waiting for transfers between devices: 125 us -> 91.9 us
  local copies, waits for them, and re-layouts: 59.5 us -> 71.3 us
  starting transfers between devices: 50.4 us -> 60.6 us
    ppermute x20, waiting for transfers between devices: 54 us -> 44.4 us  [to_chip(): return lax.ppermute(values, 'col', [(i, i ^ 2) for i in range(size)])]
    ppermute x4, waiting for transfers between devices: 29.1 us -> 19.5 us  [send(): self.arrived, self.give = (lax.ppermute(self.give, 'dp', pairs), None)]
    unnamed x249 -> x263, local copies, waits for them, and re-layouts: 41.2 us -> 50.2 us
    ppermute x4, starting transfers between devices: 3.1 us -> 9.66 us  [send(): self.arrived = lax.ppermute(self.values, 'dp', pairs)]
    ppermute x15, waiting for transfers between devices: 20.6 us -> 14.6 us  [to_row(): return lax.ppermute(values, 'row', [(0, 1), (1, 0)])]
    ppermute x4, starting transfers between devices: 3.11 us -> 7.73 us  [send(): self.arrived, self.give = (lax.ppermute(self.give, 'dp', pairs), None)]
  transfers between devices with their start and end apart: 57 -> 57, of which waited for: 24 -> 19; matrix products, arithmetic and copies ran while one was open for 17% -> 20% of each run, Pallas kernels for 25% -> 27%
where the time goes in v4:
time: 428 us; the launch traced here: 420 us
  Pallas kernels  132 us (31%)
  waiting for transfers between devices  91.9 us (21%)
  local copies, waits for them, and re-layouts  71.3 us (17%)
  starting transfers between devices  60.6 us (14%)
  matrix products  30.6 us (7%)
  other arithmetic  17.4 us (4%)
  between operations  16.1 us (4%)
    unnamed x263, local copies, waits for them, and re-layouts  50.2 us
    ppermute x20, waiting for transfers between devices, to_chip(): return lax.ppermute(values, 'col', [(i, i ^ 2) for i in range(size)])  44.4 us
    pallas_call x4, Pallas kernels, attend_back(): pl.pallas_call(functools.partial(attend_back_kernel, min(512, count)), gr...  31.8 us
    dot_general x20, matrix products, mm(): return lax.dot_general(left, right, dims, preferred_element_type=f32)  30.6 us
    pallas_call x3, Pallas kernels, attend(): pl.pallas_call(functools.partial(attend_kernel, min(512, count)), grid=(p...  30.5 us
    ppermute x20, starting transfers between devices, to_chip(): return lax.ppermute(values, 'col', [(i, i ^ 2) for i in range(size)])  23.9 us
    ppermute x4, waiting for transfers between devices, send(): self.arrived, self.give = (lax.ppermute(self.give, 'dp', pairs), None)  19.5 us
    ppermute x15, starting transfers between devices, to_row(): return lax.ppermute(values, 'row', [(0, 1), (1, 0)])  16.9 us
  transfers between devices with their start and end apart: 57, of which 19 were waited for; matrix products, arithmetic and copies ran while one was open for 20% of the time, Pallas kernels for 27%

profile of v4, /device:TPU:0, one launch (start us, length us, event | category | flops | bytes accessed | tf_op | source)
XLA Modules:
  0.0 420.3 jit_solution(13827112721825817620)
XLA Ops:
  7.4 2.2 dynamic-slice_bitcast_fusion.1
  9.5 3.0 collective-permute-start
  20.3 4.1 collective-permute-done.near_ref
  51.6 14.2 %attend.3 = (bf16[1024,768]{1,0:T(8,128)(2,1)}, bf16[4,1024,1024]{2,1,0:T(8,128)(2,1)}, bf16[1024,256]{1,0:T(8,128)(2,1)S(1)}, f32[1024,256]{1,0:T(8,128)}) custom-call(bf16[1024,1024]{1,0:T(8,128)(2,1)} %copy-done.2, bf16[512,768]{1,0:T(8,128)(2,1)S(1)} %copy-done.24, bf16[512,768]{1,0:T(8,128)(2,1)} %collective-permute-done.5.right_ref, ...), custom_call_target="tpu_custom_call" | custom-call | flops 1024 | bytes 1024 | tf_op jit(solution)/shard_map/attend/pallas_call | solution.py:72
  72.2 8.0 %attend.4 = (bf16[1024,384]{1,0:T(8,128)(2,1)}, bf16[2,1024,1024]{2,1,0:T(8,128)(2,1)}, bf16[1024,128]{1,0:T(8,128)(2,1)S(1)}, f32[1024,128]{1,0:T(8,128)S(1)}) custom-call(bf16[1024,1024]{1,0:T(8,128)(2,1)} %copy-done.2, bf16[512,384]{1,0:T(8,128)(2,1)S(1)} %collective-permute-done.3.left_ref, bf16[512,384]{1,0:T(8,128)(2,1)} %collective-permute-done.9.right_ref, ...), custom_call_target="tpu_custom_call" | custom-call | flops 1024 | bytes 1024 | tf_op jit(solution)/shard_map/attend/pallas_call | solution.py:72
  82.4 8.2 %attend.5 = (bf16[1024,384]{1,0:T(8,128)(2,1)}, bf16[2,1024,1024]{2,1,0:T(8,128)(2,1)}, bf16[1024,128]{1,0:T(8,128)(2,1)S(1)}, f32[1024,128]{1,0:T(8,128)S(1)}) custom-call(bf16[1024,1024]{1,0:T(8,128)(2,1)} %copy-done.2, bf16[512,384]{1,0:T(8,128)(2,1)S(1)} %copy-done.47, bf16[512,384]{1,0:T(8,128)(2,1)} %collective-permute-done.10.right_ref, ...), custom_call_target="tpu_custom_call" | custom-call | flops 1024 | bytes 1024 | tf_op jit(solution)/shard_map/attend/pallas_call | solution.py:72
  90.8 4.4 %collective-permute-done.14.right_ref = bf16[1024,512]{1,0:T(8,128)(2,1)S(1)} collective-permute-done((bf16[1024,512]{1,0:T(8,128)(2,1)}, bf16[1024,512]{1,0:T(8,128)(2,1)S(1)}, u32[]{:S(2)}, u32[]{:S(2)}) %collective-permute-start.14) | collective-permute-done | bytes 1048608 | tf_op jit(solution)/shard_map/ppermute | solution.py:38
  99.9 23.2 %collective-permute-done.17.left_ref = bf16[1024,512]{1,0:T(8,128)(2,1)S(1)} collective-permute-done((bf16[1024,512]{1,0:T(8,128)(2,1)}, bf16[1024,512]{1,0:T(8,128)(2,1)S(1)}, u32[]{:S(2)}, u32[]{:S(2)}) %collective-permute-start.17) | collective-permute-done | bytes 1048608 | tf_op jit(solution)/shard_map/ppermute | solution.py:34
  130.9 5.7 %feed.2 = (bf16[1024,1024]{1,0:T(8,128)(2,1)S(1)}, bf16[1024,1024]{1,0:T(8,128)(2,1)S(1)}) custom-call(bf16[1024,1024]{1,0:T(8,128)(2,1)S(1)} %constant_dynamic-update-slice_fusion.8.wide_ref.right_ref, bf16[512,1024]{1,0:T(8,128)(2,1)} %left_ref.4, bf16[512,1024]{1,0:T(8,128)(2,1)} %collective-permute-done.13.right_ref, f32[1,1024]{1,0:T(1,128)S(1)} %bitcast.87), custom_call_target="tpu_custom_call" | custom-call | flops 1024 | bytes 1024 | tf_op jit(solution)/shard_map/feed/pallas_call | solution.py:268
  136.6 4.8 %feed.3 = (bf16[1024,1024]{1,0:T(8,128)(2,1)S(1)}, bf16[1024,1024]{1,0:T(8,128)(2,1)S(1)}) custom-call(bf16[1024,1024]{1,0:T(8,128)(2,1)S(1)} %constant_dynamic-update-slice_fusion.8.wide_ref.right_ref, bf16[512,1024]{1,0:T(8,128)(2,1)S(1)} %copy-done.13, bf16[512,1024]{1,0:T(8,128)(2,1)S(1)} %collective-permute-done.16.right_ref, f32[1,1024]{1,0:T(1,128)S(1)} %bitcast.88), custom_call_target="tpu_custom_call" | custom-call | flops 1024 | bytes 1024 | tf_op jit(solution)/shard_map/feed/pallas_call | solution.py:268
  141.4 4.6 %collective-permute-done.21 = bf16[256,512]{1,0:T(8,128)(2,1)S(1)} collective-permute-done((bf16[256,512]{1,0:T(8,128)(2,1)S(1)}, bf16[256,512]{1,0:T(8,128)(2,1)S(1)}, u32[]{:S(2)}, u32[]{:S(2)}) %collective-permute-start.21) | collective-permute-done | bytes 262176 | tf_op jit(solution)/shard_map/ppermute | solution.py:34
  151.2 2.6 convolution_add_fusion.2.own_ref
  158.3 3.1 norm_two.1
  161.7 2.1 constant_dynamic-update-slice_fusion.17
  168.3 7.9 %weight_grads.2 = (bf16[1024,512]{1,0:T(8,128)(2,1)}, bf16[1024,512]{1,0:T(8,128)(2,1)S(1)}, bf16[512,1024]{1,0:T(8,128)(2,1)}, bf16[512,1024]{1,0:T(8,128)(2,1)S(1)}) custom-call(bf16[1024,1024]{1,0:T(8,128)(2,1)S(1)} %copy-done.33, bf16[1024,1024]{1,0:T(8,128)(2,1)S(1)} %get-tuple-element.197.mine_ref, ...), custom_call_target="tpu_custom_call" | custom-call | flops 1024 | bytes 1024 | tf_op jit(solution)/shard_map/weight_grads/pallas_call | solution.py:346
  178.8 3.6 feed_back.3
  182.4 5.1 %feed_back.2 = (bf16[1024,1024]{1,0:T(8,128)(2,1)S(1)}, f32[1,1024]{1,0:T(1,128)S(1)}) custom-call(bf16[1024,1024]{1,0:T(8,128)(2,1)S(1)} %constant_dynamic-update-slice_fusion.14.grad_ref.right_ref, bf16[1024,512]{1,0:T(8,128)(2,1)} %left_ref.5, bf16[1024,512]{1,0:T(8,128)(2,1)S(1)} %copy-done.10, bf16[1024,1024]{1,0:T(8,128)(2,1)S(1)} %get-tuple-element.208.slope_ref), custom_call_target="tpu_custom_call" | custom-call | flops 1024 | bytes 1024 | tf_op jit(solution)/shard_map/feed_back/pallas_call | solution.py:294
  189.9 2.3 add_convert_fusion
  192.7 3.5 fusion.6
  198.4 3.5 collective-permute-done.28.arrived_a
  202.7 2.8 second.2
  205.5 5.1 %norm_back.1 = (f32[512,1024]{1,0:T(8,128)S(1)}, bf16[512,1024]{1,0:T(8,128)(2,1)}, f32[8,1024]{1,0:T(8,128)S(1)}) custom-call(s32[4]{0:T(128)S(1)} %pad_add_fusion.1.flags, f32[8,1024]{1,0:T(8,128)S(1)} %select_maximum_fusion.vec_ref, f32[512,1024]{1,0:T(8,128)S(1)} %copy-done.41, f32[512,1024]{1,0:T(8,128)S(1)} %convolution_add_fusion.1.own_ref, ...), custom_call_target="tpu_custom_call" | custom-call | flops 1024 | bytes 1024 | tf_op jit(solution)/shard_map/norm_back/pallas_call | solution.py:236
  212.0 8.2 %weight_grads.3 = (bf16[1024,512]{1,0:T(8,128)(2,1)}, bf16[1024,512]{1,0:T(8,128)(2,1)S(1)}, bf16[512,1024]{1,0:T(8,128)(2,1)}, bf16[512,1024]{1,0:T(8,128)(2,1)S(1)}) custom-call(bf16[1024,1024]{1,0:T(8,128)(2,1)S(1)} %copy-done.29, bf16[1024,1024]{1,0:T(8,128)(2,1)S(1)} %copy-done.31, ...), custom_call_target="tpu_custom_call" | custom-call | flops 1024 | bytes 1024 | tf_op jit(solution)/shard_map/weight_grads/pallas_call | solution.py:346
  238.4 2.4 collective-permute-done.32.b_row
  240.9 2.5 joined.1
  247.1 7.8 %attend_back.4 = (bf16[1024,384]{1,0:T(8,128)(2,1)S(1)}, f32[8,384]{1,0:T(8,128)S(1)}) custom-call(bf16[1024,384]{1,0:T(8,128)(2,1)S(1)} %copy-done.63, bf16[2,1024,1024]{2,1,0:T(8,128)(2,1)} %get-tuple-element.236.exp_ref, bf16[1024,128]{1,0:T(8,128)(2,1)S(1)} %copy-done.52, f32[1024,128]{1,0:T(8,128)S(1)} %copy-done.68, bf16[1024,256]{1,0:T(8,128)(2,1)S(1)} %copy-done.36), custom_call_target="tpu_custom_call" | custom-call | flops 1024 | bytes 1024 | tf_op jit(solution)/shard_map/attend_back/pallas_call | solution.py:139
  257.6 8.2 %attend_back.5 = (bf16[1024,384]{1,0:T(8,128)(2,1)S(1)}, f32[8,384]{1,0:T(8,128)S(1)}) custom-call(bf16[1024,384]{1,0:T(8,128)(2,1)S(1)} %copy-done.64, bf16[2,1024,1024]{2,1,0:T(8,128)(2,1)} %get-tuple-element.231.exp_ref, bf16[1024,128]{1,0:T(8,128)(2,1)S(1)} %copy-done.54, f32[1024,128]{1,0:T(8,128)S(1)} %copy-done.70, bf16[1024,256]{1,0:T(8,128)(2,1)S(1)} %copy-done.37), custom_call_target="tpu_custom_call" | custom-call | flops 1024 | bytes 1024 | tf_op jit(solution)/shard_map/attend_back/pallas_call | solution.py:139
  267.5 3.2 fusion.33
  272.8 4.8 %collective-permute-done.33.near_ref = bf16[1024,256]{1,0:T(8,128)(2,1)S(1)} collective-permute-done((bf16[1024,256]{1,0:T(8,128)(2,1)S(1)}, bf16[1024,256]{1,0:T(8,128)(2,1)S(1)}, u32[]{:S(2)}, u32[]{:S(2)}) %collective-permute-start.33) | collective-permute-done | bytes 524320 | tf_op jit(solution)/shard_map/ppermute | solution.py:34
  278.5 2.5 second.3
  287.3 7.8 %attend_back.6 = (bf16[1024,384]{1,0:T(8,128)(2,1)S(1)}, f32[8,384]{1,0:T(8,128)S(1)}) custom-call(bf16[1024,768]{1,0:T(8,128)(2,1)S(1)} %copy-done.8, bf16[4,1024,1024]{2,1,0:T(8,128)(2,1)} %get-tuple-element.257.exp_ref, bf16[1024,256]{1,0:T(8,128)(2,1)S(1)} %get-tuple-element.184.mixed_ref.left_ref, f32[1024,256]{1,0:T(8,128)S(1)} %copy-done.11, ...), custom_call_target="tpu_custom_call" | custom-call | flops 1024 | bytes 1024 | tf_op jit(solution)/shard_map/attend_back/pallas_call | solution.py:139
  297.8 4.3 %collective-permute-done.37.b_row = bf16[512,512]{1,0:T(8,128)(2,1)} collective-permute-done((bf16[512,512]{1,0:T(8,128)(2,1)}, bf16[512,512]{1,0:T(8,128)(2,1)}, u32[]{:S(2)}, u32[]{:S(2)}) %collective-permute-start.37) | collective-permute-done | bytes 524320 | tf_op jit(solution)/shard_map/ppermute | solution.py:38
  307.4 2.8 merge.1
  313.8 8.0 %attend_back.7 = (bf16[1024,384]{1,0:T(8,128)(2,1)S(1)}, f32[8,384]{1,0:T(8,128)S(1)}) custom-call(bf16[1024,768]{1,0:T(8,128)(2,1)S(1)} %copy-done.8, bf16[4,1024,1024]{2,1,0:T(8,128)(2,1)} %get-tuple-element.257.exp_ref, bf16[1024,256]{1,0:T(8,128)(2,1)S(1)} %get-tuple-element.184.mixed_ref.left_ref, f32[1024,256]{1,0:T(8,128)S(1)} %copy-done.11, ...), custom_call_target="tpu_custom_call" | custom-call | flops 1024 | bytes 1024 | tf_op jit(solution)/shard_map/attend_back/pallas_call | solution.py:139
  324.4 2.1 constant_dynamic-update-slice_fusion.23
  330.5 2.2 fusion.32
  336.2 2.7 collective-permute-start.43
  343.1 5.3 %collective-permute-done.43 = bf16[256,512]{1,0:T(8,128)(2,1)S(1)} collective-permute-done((bf16[256,512]{1,0:T(8,128)(2,1)S(1)}, bf16[256,512]{1,0:T(8,128)(2,1)S(1)}, u32[]{:S(2)}, u32[]{:S(2)}) %collective-permute-start.43) | collective-permute-done | bytes 262176 | tf_op jit(solution)/shard_map/ppermute | solution.py:542
  348.9 3.4 collective-permute-start.50
  356.8 5.4 %collective-permute-done.50 = bf16[256,512]{1,0:T(8,128)(2,1)S(1)} collective-permute-done((bf16[256,512]{1,0:T(8,128)(2,1)S(1)}, bf16[256,512]{1,0:T(8,128)(2,1)S(1)}, u32[]{:S(2)}, u32[]{:S(2)}) %collective-permute-start.50) | collective-permute-done | bytes 262176 | tf_op jit(solution)/shard_map/ppermute | solution.py:544
  362.2 4.9 %collective-permute-done.51 = bf16[544,512]{1,0:T(8,128)(2,1)S(1)} collective-permute-done((bf16[544,512]{1,0:T(8,128)(2,1)S(1)}, bf16[544,512]{1,0:T(8,128)(2,1)S(1)}, u32[]{:S(2)}, u32[]{:S(2)}) %collective-permute-start.51) | collective-permute-done | bytes 557088 | tf_op jit(solution)/shard_map/ppermute | solution.py:542
  367.7 3.4 collective-permute-start.53
  371.1 9.4 %collective-permute-done.53 = bf16[272,512]{1,0:T(8,128)(2,1)S(1)} collective-permute-done((bf16[272,512]{1,0:T(8,128)(2,1)S(1)}, bf16[272,512]{1,0:T(8,128)(2,1)S(1)}, u32[]{:S(2)}, u32[]{:S(2)}) %collective-permute-start.53) | collective-permute-done | bytes 278560 | tf_op jit(solution)/shard_map/ppermute | solution.py:542
  381.5 2.7 collective-permute-start.54
  384.1 7.0 %collective-permute-done.54 = bf16[272,512]{1,0:T(8,128)(2,1)S(1)} collective-permute-done((bf16[272,512]{1,0:T(8,128)(2,1)S(1)}, bf16[272,512]{1,0:T(8,128)(2,1)S(1)}, u32[]{:S(2)}, u32[]{:S(2)}) %collective-permute-start.54) | collective-permute-done | bytes 278560 | tf_op jit(solution)/shard_map/ppermute | solution.py:544
  391.4 3.5 collective-permute-start.55
  400.7 2.9 copy.32
  403.6 3.3 collective-permute-done.49.near_ref
  (494 shorter events, 159.6 us)
Async XLA Ops:
  7.3 319.2 %all-reduce.5.cloned.1.call-start = ((), (), s32[]{:S(2)}) async-start(), calls=%async_computation | async-start | bytes 2097152 | tf_op jit(solution)/shard_map/psum | solution.py:751
  9.5 14.9 %collective-permute-start = (bf16[1024,256]{1,0:T(8,128)(2,1)S(1)}, bf16[1024,256]{1,0:T(8,128)(2,1)S(1)}, u32[]{:S(2)}, u32[]{:S(2)}) collective-permute-start(bf16[1024,256]{1,0:T(8,128)(2,1)S(1)} %get-tuple-element.337), channel_id=1, source_target_pairs={{0,2},{1,3},{2,0},{3,1},{4,6},{5,7},{6,4},{7,5},{8,10},{9,11},{10,... | collective-permute-start | bytes 1572872 | tf_op jit(solution)/shard_map/ppermute | solution.py:34
  12.5 21.3 %collective-permute-start.1 = (bf16[1024,256]{1,0:T(8,128)(2,1)}, bf16[1024,256]{1,0:T(8,128)(2,1)}, u32[]{:S(2)}, u32[]{:S(2)}) collective-permute-start(bf16[1024,256]{1,0:T(8,128)(2,1)} %get-tuple-element.336), channel_id=1, source_target_pairs={{0,1},{1,0},{2,3},{3,2},{4,5},{5,4},{6,7},{7,6},{8,9},{9,8},{10,11... | collective-permute-start | bytes 1572872 | tf_op jit(solution)/shard_map/ppermute | solution.py:29
  12.5 30.1 %collective-permute-start.5 = (bf16[512,768]{1,0:T(8,128)(2,1)S(1)}, bf16[512,768]{1,0:T(8,128)(2,1)}, u32[]{:S(2)}, u32[]{:S(2)}) collective-permute-start(bf16[512,768]{1,0:T(8,128)(2,1)S(1)} %copy-done.23), channel_id=1, source_target_pairs={{0,4},{4,0},{1,5},{5,1},{2,6},{6,2},{3,7},{7,3},{8,12},{12,8},{9,1... | collective-permute-start | bytes 2359304 | tf_op jit(solution)/shard_map/ppermute | solution.py:38
  25.2 10.4 %collective-permute-start.3 = (bf16[512,384]{1,0:T(8,128)(2,1)S(1)}, bf16[512,384]{1,0:T(8,128)(2,1)S(1)}, u32[]{:S(2)}, u32[]{:S(2)}) collective-permute-start(bf16[512,384]{1,0:T(8,128)(2,1)S(1)} %get-tuple-element.339), channel_id=1, source_target_pairs={{0,2},{1,3},{2,0},{3,1},{4,6},{5,7},{6,4},{7,5},{8,10},{9,11},{10,... | collective-permute-start | bytes 1179656 | tf_op jit(solution)/shard_map/ppermute | solution.py:34
  29.7 12.9 %collective-permute-start.6 = (bf16[256,512]{1,0:T(8,128)(2,1)}, bf16[256,512]{1,0:T(8,128)(2,1)}, u32[]{:S(2)}, u32[]{:S(2)}) collective-permute-start(bf16[256,512]{1,0:T(8,128)(2,1)} %param.19), channel_id=1, source_target_pairs={{0,4},{4,0},{1,5},{5,1},{2,6},{6,2},{3,7},{7,3},{8,12},{12,8},{9,1... | collective-permute-start | bytes 786440 | tf_op jit(solution)/shard_map/ppermute | solution.py:38
  35.6 12.3 %collective-permute-start.7 = (bf16[512,384]{1,0:T(8,128)(2,1)}, bf16[512,384]{1,0:T(8,128)(2,1)S(1)}, u32[]{:S(2)}, u32[]{:S(2)}) collective-permute-start(bf16[512,384]{1,0:T(8,128)(2,1)} %get-tuple-element.338), channel_id=1, source_target_pairs={{0,2},{1,3},{2,0},{3,1},{4,6},{5,7},{6,4},{7,5},{8,10},{9,11},{10,... | collective-permute-start | bytes 1179656 | tf_op jit(solution)/shard_map/ppermute | solution.py:34
  37.2 29.7 %collective-permute-start.11 = (bf16[256,512]{1,0:T(8,128)(2,1)}, bf16[256,512]{1,0:T(8,128)(2,1)}, u32[]{:S(2)}, u32[]{:S(2)}) collective-permute-start(bf16[256,512]{1,0:T(8,128)(2,1)} %param.19), channel_id=1, source_target_pairs={{0,2},{1,3},{2,0},{3,1},{4,6},{5,7},{6,4},{7,5},{8,10},{9,11},{10,... | collective-permute-start | bytes 786440 | tf_op jit(solution)/shard_map/ppermute | solution.py:34
  41.2 25.7 %collective-permute-start.9 = (bf16[512,384]{1,0:T(8,128)(2,1)S(1)}, bf16[512,384]{1,0:T(8,128)(2,1)}, u32[]{:S(2)}, u32[]{:S(2)}) collective-permute-start(bf16[512,384]{1,0:T(8,128)(2,1)S(1)} %collective-permute-done.3.left_ref), channel_id=1, source_target_pairs={{0,4},{4,0},{1,5},{5,1},{2,6},{6,2},{3,7},{7,3},{8,12},{12,8},{9,1... | collective-permute-start | bytes 1179656 | tf_op jit(solution)/shard_map/ppermute | solution.py:38
  44.4 22.5 %collective-permute-start.10 = (bf16[512,384]{1,0:T(8,128)(2,1)}, bf16[512,384]{1,0:T(8,128)(2,1)}, u32[]{:S(2)}, u32[]{:S(2)}) collective-permute-start(bf16[512,384]{1,0:T(8,128)(2,1)} %slice.361), channel_id=1, source_target_pairs={{0,2},{1,3},{2,0},{3,1},{4,6},{5,7},{6,4},{7,5},{8,10},{9,11},{10,... | collective-permute-start | bytes 1179656 | tf_op jit(solution)/shard_map/ppermute | solution.py:34
  46.1 20.8 %collective-permute-start.12 = (bf16[256,512]{1,0:T(8,128)(2,1)}, bf16[256,512]{1,0:T(8,128)(2,1)}, u32[]{:S(2)}, u32[]{:S(2)}) collective-permute-start(bf16[256,512]{1,0:T(8,128)(2,1)} %collective-permute-done.6), channel_id=1, source_target_pairs={{0,2},{1,3},{2,0},{3,1},{4,6},{5,7},{6,4},{7,5},{8,10},{9,11},{10,... | collective-permute-start | bytes 786440 | tf_op jit(solution)/shard_map/ppermute | solution.py:34
  48.7 33.8 %collective-permute-start.13 = (bf16[512,1024]{1,0:T(8,128)(2,1)}, bf16[512,1024]{1,0:T(8,128)(2,1)}, u32[]{:S(2)}, u32[]{:S(2)}) collective-permute-start(bf16[512,1024]{1,0:T(8,128)(2,1)} %left_ref.4), channel_id=1, source_target_pairs={{0,4},{4,0},{1,5},{5,1},{2,6},{6,2},{3,7},{7,3},{8,12},{12,8},{9,1... | collective-permute-start | bytes 3145736 | tf_op jit(solution)/shard_map/ppermute | solution.py:38
  66.9 28.3 %collective-permute-start.14 = (bf16[1024,512]{1,0:T(8,128)(2,1)}, bf16[1024,512]{1,0:T(8,128)(2,1)S(1)}, u32[]{:S(2)}, u32[]{:S(2)}) collective-permute-start(bf16[1024,512]{1,0:T(8,128)(2,1)} %left_ref.5), channel_id=1, source_target_pairs={{0,4},{4,0},{1,5},{5,1},{2,6},{6,2},{3,7},{7,3},{8,12},{12,8},{9,1... | collective-permute-start | bytes 3145736 | tf_op jit(solution)/shard_map/ppermute | solution.py:38
  67.6 27.6 %collective-permute-start.15 = (bf16[512,1024]{1,0:T(8,128)(2,1)}, bf16[512,1024]{1,0:T(8,128)(2,1)S(1)}, u32[]{:S(2)}, u32[]{:S(2)}) collective-permute-start(bf16[512,1024]{1,0:T(8,128)(2,1)} %left_ref.4), channel_id=1, source_target_pairs={{0,2},{1,3},{2,0},{3,1},{4,6},{5,7},{6,4},{7,5},{8,10},{9,11},{10,... | collective-permute-start | bytes 3145736 | tf_op jit(solution)/shard_map/ppermute | solution.py:34
  70.5 28.4 %collective-permute-start.8 = (f32[6,512]{1,0:T(8,128)S(1)}, f32[6,512]{1,0:T(8,128)S(1)}, u32[]{:S(2)}, u32[]{:S(2)}) collective-permute-start(f32[6,512]{1,0:T(8,128)S(1)} %constant_dynamic-update-slice_fusion.2), channel_id=1, source_target_pairs={{0,1},{1,0},{2,3},{3,2},{4,5},{5,4},{6,7},{7,6},{8,9},{9,8},{10,11... | collective-permute-start | bytes 36872 | tf_op jit(solution)/shard_map/ppermute | solution.py:29
  95.2 27.9 %collective-permute-start.16 = (bf16[512,1024]{1,0:T(8,128)(2,1)S(1)}, bf16[512,1024]{1,0:T(8,128)(2,1)S(1)}, u32[]{:S(2)}, u32[]{:S(2)}) collective-permute-start(bf16[512,1024]{1,0:T(8,128)(2,1)S(1)} %collective-permute-done.15.left_ref), channel_id=1, source_target_pairs={{0,4},{4,0},{1,5},{5,1},{2,6},{6,2},{3,7},{7,3},{8,12},{12,8},{9,1... | collective-permute-start | bytes 3145736 | tf_op jit(solution)/shard_map/ppermute | solution.py:38
  97.2 25.9 %collective-permute-start.18 = (bf16[512,1024]{1,0:T(8,128)(2,1)S(1)}, bf16[512,1024]{1,0:T(8,128)(2,1)S(1)}, u32[]{:S(2)}, u32[]{:S(2)}) collective-permute-start(bf16[512,1024]{1,0:T(8,128)(2,1)S(1)} %add_convert_fusion.2), channel_id=1, source_target_pairs={{0,1},{1,0},{2,3},{3,2},{4,5},{5,4},{6,7},{7,6},{8,9},{9,8},{10,11... | collective-permute-start | bytes 3145736 | tf_op jit(solution)/shard_map/ppermute | solution.py:29
  97.3 25.8 %collective-permute-start.17 = (bf16[1024,512]{1,0:T(8,128)(2,1)}, bf16[1024,512]{1,0:T(8,128)(2,1)S(1)}, u32[]{:S(2)}, u32[]{:S(2)}) collective-permute-start(bf16[1024,512]{1,0:T(8,128)(2,1)} %left_ref.5), channel_id=1, source_target_pairs={{0,2},{1,3},{2,0},{3,1},{4,6},{5,7},{6,4},{7,5},{8,10},{9,11},{10,... | collective-permute-start | bytes 3145736 | tf_op jit(solution)/shard_map/ppermute | solution.py:34
  125.2 20.8 %collective-permute-start.22 = (bf16[768,512]{1,0:T(8,128)(2,1)S(1)}, bf16[768,512]{1,0:T(8,128)(2,1)S(1)}, u32[]{:S(2)}, u32[]{:S(2)}) collective-permute-start(bf16[768,512]{1,0:T(8,128)(2,1)S(1)} %slice.371), channel_id=1, source_target_pairs={{0,4},{4,0},{1,5},{5,1},{2,6},{6,2},{3,7},{7,3},{8,12},{12,8},{9,1... | collective-permute-start | bytes 2359304 | tf_op jit(solution)/shard_map/ppermute | solution.py:38
  126.3 15.1 %collective-permute-start.20 = (bf16[1024,256]{1,0:T(8,128)(2,1)S(1)}, bf16[1024,256]{1,0:T(8,128)(2,1)S(1)}, u32[]{:S(2)}, u32[]{:S(2)}) collective-permute-start(bf16[1024,256]{1,0:T(8,128)(2,1)S(1)} %dynamic-slice_bitcast_fusion), channel_id=1, source_target_pairs={{0,2},{1,3},{2,0},{3,1},{4,6},{5,7},{6,4},{7,5},{8,10},{9,11},{10,... | collective-permute-start | bytes 1572872 | tf_op jit(solution)/shard_map/ppermute | solution.py:34
  130.2 15.9 %collective-permute-start.21 = (bf16[256,512]{1,0:T(8,128)(2,1)S(1)}, bf16[256,512]{1,0:T(8,128)(2,1)S(1)}, u32[]{:S(2)}, u32[]{:S(2)}) collective-permute-start(bf16[256,512]{1,0:T(8,128)(2,1)S(1)} %slice.370), channel_id=1, source_target_pairs={{0,2},{1,3},{2,0},{3,1},{4,6},{5,7},{6,4},{7,5},{8,10},{9,11},{10,... | collective-permute-start | bytes 786440 | tf_op jit(solution)/shard_map/ppermute | solution.py:34
  176.2 25.6 %collective-permute-start.28 = (bf16[1024,512]{1,0:T(8,128)(2,1)}, bf16[1024,512]{1,0:T(8,128)(2,1)}, u32[]{:S(2)}, u32[]{:S(2)}) collective-permute-start(bf16[1024,512]{1,0:T(8,128)(2,1)} %get-tuple-element.213), channel_id=1, source_target_pairs={{0,4},{4,0},{1,5},{5,1},{2,6},{6,2},{3,7},{7,3},{8,12},{12,8},{9,1... | collective-permute-start | bytes 3145736 | tf_op jit(solution)/shard_map/ppermute | solution.py:38
  177.3 25.3 %collective-permute-start.29 = (bf16[512,1024]{1,0:T(8,128)(2,1)}, bf16[512,1024]{1,0:T(8,128)(2,1)}, u32[]{:S(2)}, u32[]{:S(2)}) collective-permute-start(bf16[512,1024]{1,0:T(8,128)(2,1)} %get-tuple-element.214), channel_id=1, source_target_pairs={{0,2},{1,3},{2,0},{3,1},{4,6},{5,7},{6,4},{7,5},{8,10},{9,11},{10,... | collective-permute-start | bytes 3145736 | tf_op jit(solution)/shard_map/ppermute | solution.py:34
  192.1 10.5 %collective-permute-start.26 = (bf16[512,1024]{1,0:T(8,128)(2,1)}, bf16[512,1024]{1,0:T(8,128)(2,1)}, u32[]{:S(2)}, u32[]{:S(2)}) collective-permute-start(bf16[512,1024]{1,0:T(8,128)(2,1)} %add_convert_fusion), channel_id=1, source_target_pairs={{0,1},{1,0},{2,3},{3,2},{4,5},{5,4},{6,7},{7,6},{8,9},{9,8},{10,11... | collective-permute-start | bytes 3145736 | tf_op jit(solution)/shard_map/ppermute | solution.py:29
  211.9 17.0 %collective-permute-start.30 = (bf16[512,1024]{1,0:T(8,128)(2,1)}, bf16[512,1024]{1,0:T(8,128)(2,1)}, u32[]{:S(2)}, u32[]{:S(2)}) collective-permute-start(bf16[512,1024]{1,0:T(8,128)(2,1)} %get-tuple-element.229), channel_id=1, source_target_pairs={{0,1},{1,0},{2,3},{3,2},{4,5},{5,4},{6,7},{7,6},{8,9},{9,8},{10,11... | collective-permute-start | bytes 3145736 | tf_op jit(solution)/shard_map/ppermute | solution.py:29
  224.1 14.3 %collective-permute-start.31 = (bf16[512,512]{1,0:T(8,128)(2,1)}, bf16[512,512]{1,0:T(8,128)(2,1)}, u32[]{:S(2)}, u32[]{:S(2)}) collective-permute-start(bf16[512,512]{1,0:T(8,128)(2,1)} %get-tuple-element.233), channel_id=1, source_target_pairs={{0,2},{1,3},{2,0},{3,1},{4,6},{5,7},{6,4},{7,5},{8,10},{9,11},{10,... | collective-permute-start | bytes 1572872 | tf_op jit(solution)/shard_map/ppermute | solution.py:34
  225.7 15.1 %collective-permute-start.32 = (bf16[512,512]{1,0:T(8,128)(2,1)}, bf16[512,512]{1,0:T(8,128)(2,1)}, u32[]{:S(2)}, u32[]{:S(2)}) collective-permute-start(bf16[512,512]{1,0:T(8,128)(2,1)} %get-tuple-element.234), channel_id=1, source_target_pairs={{0,4},{4,0},{1,5},{5,1},{2,6},{6,2},{3,7},{7,3},{8,12},{12,8},{9,1... | collective-permute-start | bytes 1572872 | tf_op jit(solution)/shard_map/ppermute | solution.py:38
  234.2 63.6 %collective-permute-start.39 = (bf16[512,512]{1,0:T(8,128)(2,1)}, bf16[512,512]{1,0:T(8,128)(2,1)}, u32[]{:S(2)}, u32[]{:S(2)}) collective-permute-start(bf16[512,512]{1,0:T(8,128)(2,1)} %pad_maximum_fusion.7), channel_id=1, source_target_pairs={{0,4},{4,0},{1,5},{5,1},{2,6},{6,2},{3,7},{7,3},{8,12},{12,8},{9,1... | collective-permute-start | bytes 1572872 | tf_op jit(solution)/shard_map/ppermute | solution.py:38
  243.4 34.3 %collective-permute-start.35 = (bf16[512,1024]{1,0:T(8,128)(2,1)}, bf16[512,1024]{1,0:T(8,128)(2,1)}, u32[]{:S(2)}, u32[]{:S(2)}) collective-permute-start(bf16[512,1024]{1,0:T(8,128)(2,1)} %get-tuple-element.250), channel_id=1, source_target_pairs={{0,2},{1,3},{2,0},{3,1},{4,6},{5,7},{6,4},{7,5},{8,10},{9,11},{10,... | collective-permute-start | bytes 3145736 | tf_op jit(solution)/shard_map/ppermute | solution.py:34
  243.9 33.7 %collective-permute-start.34 = (bf16[1024,512]{1,0:T(8,128)(2,1)}, bf16[1024,512]{1,0:T(8,128)(2,1)S(1)}, u32[]{:S(2)}, u32[]{:S(2)}) collective-permute-start(bf16[1024,512]{1,0:T(8,128)(2,1)} %get-tuple-element.248), channel_id=1, source_target_pairs={{0,4},{4,0},{1,5},{5,1},{2,6},{6,2},{3,7},{7,3},{8,12},{12,8},{9,1... | collective-permute-start | bytes 3145736 | tf_op jit(solution)/shard_map/ppermute | solution.py:38
  256.0 21.6 %collective-permute-start.33 = (bf16[1024,256]{1,0:T(8,128)(2,1)S(1)}, bf16[1024,256]{1,0:T(8,128)(2,1)S(1)}, u32[]{:S(2)}, u32[]{:S(2)}) collective-permute-start(bf16[1024,256]{1,0:T(8,128)(2,1)S(1)} %copy-done.89), channel_id=1, source_target_pairs={{0,2},{1,3},{2,0},{3,1},{4,6},{5,7},{6,4},{7,5},{8,10},{9,11},{10,... | collective-permute-start | bytes 1572872 | tf_op jit(solution)/shard_map/ppermute | solution.py:34
  282.6 15.1 %collective-permute-start.38 = (bf16[384,512]{1,0:T(8,128)(2,1)}, bf16[384,512]{1,0:T(8,128)(2,1)}, u32[]{:S(2)}, u32[]{:S(2)}) collective-permute-start(bf16[384,512]{1,0:T(8,128)(2,1)} %slice.379), channel_id=1, source_target_pairs={{0,4},{4,0},{1,5},{5,1},{2,6},{6,2},{3,7},{7,3},{8,12},{12,8},{9,1... | collective-permute-start | bytes 1179656 | tf_op jit(solution)/shard_map/ppermute | solution.py:38
  283.6 14.1 %collective-permute-start.36 = (bf16[512,512]{1,0:T(8,128)(2,1)}, bf16[512,512]{1,0:T(8,128)(2,1)}, u32[]{:S(2)}, u32[]{:S(2)}) collective-permute-start(bf16[512,512]{1,0:T(8,128)(2,1)} %get-tuple-element.265), channel_id=1, source_target_pairs={{0,2},{1,3},{2,0},{3,1},{4,6},{5,7},{6,4},{7,5},{8,10},{9,11},{10,... | collective-permute-start | bytes 1572872 | tf_op jit(solution)/shard_map/ppermute | solution.py:34
  284.2 17.8 %collective-permute-start.37 = (bf16[512,512]{1,0:T(8,128)(2,1)}, bf16[512,512]{1,0:T(8,128)(2,1)}, u32[]{:S(2)}, u32[]{:S(2)}) collective-permute-start(bf16[512,512]{1,0:T(8,128)(2,1)} %get-tuple-element.266), channel_id=1, source_target_pairs={{0,4},{4,0},{1,5},{5,1},{2,6},{6,2},{3,7},{7,3},{8,12},{12,8},{9,1... | collective-permute-start | bytes 1572872 | tf_op jit(solution)/shard_map/ppermute | solution.py:38
  296.3 32.4 %collective-permute-start.45 = (bf16[448,1024]{1,0:T(8,128)(2,1)}, bf16[448,1024]{1,0:T(8,128)(2,1)}, u32[]{:S(2)}, u32[]{:S(2)}) collective-permute-start(bf16[448,1024]{1,0:T(8,128)(2,1)} %maximum_maximum_fusion), channel_id=1, source_target_pairs={{0,2},{1,3},{2,0},{3,1},{4,6},{5,7},{6,4},{7,5},{8,10},{9,11},{10,... | collective-permute-start | bytes 2752520 | tf_op jit(solution)/shard_map/ppermute | solution.py:34
  303.9 22.6 %collective-permute-start.41 = (bf16[384,512]{1,0:T(8,128)(2,1)}, bf16[384,512]{1,0:T(8,128)(2,1)}, u32[]{:S(2)}, u32[]{:S(2)}) collective-permute-start(bf16[384,512]{1,0:T(8,128)(2,1)} %add_convert_fusion.10), channel_id=1, source_target_pairs={{0,2},{1,3},{2,0},{3,1},{4,6},{5,7},{6,4},{7,5},{8,10},{9,11},{10,... | collective-permute-start | bytes 1179656 | tf_op jit(solution)/shard_map/ppermute | solution.py:34
  306.4 20.1 %collective-permute-start.42 = (bf16[384,512]{1,0:T(8,128)(2,1)}, bf16[384,512]{1,0:T(8,128)(2,1)}, u32[]{:S(2)}, u32[]{:S(2)}) collective-permute-start(bf16[384,512]{1,0:T(8,128)(2,1)} %slice.457), channel_id=1, source_target_pairs={{0,4},{4,0},{1,5},{5,1},{2,6},{6,2},{3,7},{7,3},{8,12},{12,8},{9,1... | collective-permute-start | bytes 1179656 | tf_op jit(solution)/shard_map/ppermute | solution.py:38
  311.0 15.4 %collective-permute-start.40 = (bf16[512,512]{1,0:T(8,128)(2,1)}, bf16[512,512]{1,0:T(8,128)(2,1)}, u32[]{:S(2)}, u32[]{:S(2)}) collective-permute-start(bf16[512,512]{1,0:T(8,128)(2,1)} %get-tuple-element.272), channel_id=1, source_target_pairs={{0,8},{8,0},{16,24},{24,16},{1,9},{9,1},{17,25},{25,17},{2,10},{10... | collective-permute-start | bytes 1572872 | tf_op jit(solution)/shard_map/ppermute | solution.py:542
  322.7 20.3 %collective-permute-start.47 = (bf16[256,512]{1,0:T(8,128)(2,1)S(1)}, bf16[256,512]{1,0:T(8,128)(2,1)S(1)}, u32[]{:S(2)}, u32[]{:S(2)}) collective-permute-start(bf16[256,512]{1,0:T(8,128)(2,1)S(1)} %slice.485), channel_id=1, source_target_pairs={{0,2},{1,3},{2,0},{3,1},{4,6},{5,7},{6,4},{7,5},{8,10},{9,11},{10,... | collective-permute-start | bytes 786440 | tf_op jit(solution)/shard_map/ppermute | solution.py:34
  333.8 14.6 %collective-permute-start.46 = (bf16[448,512]{1,0:T(8,128)(2,1)S(1)}, bf16[448,512]{1,0:T(8,128)(2,1)S(1)}, u32[]{:S(2)}, u32[]{:S(2)}) collective-permute-start(bf16[448,512]{1,0:T(8,128)(2,1)S(1)} %slice.482), channel_id=1, source_target_pairs={{0,4},{4,0},{1,5},{5,1},{2,6},{6,2},{3,7},{7,3},{8,12},{12,8},{9,1... | collective-permute-start | bytes 1376264 | tf_op jit(solution)/shard_map/ppermute | solution.py:38
  336.2 12.2 %collective-permute-start.43 = (bf16[256,512]{1,0:T(8,128)(2,1)S(1)}, bf16[256,512]{1,0:T(8,128)(2,1)S(1)}, u32[]{:S(2)}, u32[]{:S(2)}) collective-permute-start(bf16[256,512]{1,0:T(8,128)(2,1)S(1)} %broadcast_select_fusion.2), channel_id=1, source_target_pairs={{0,16},{8,24},{16,0},{24,8},{1,17},{9,25},{17,1},{25,9},{2,18},{10... | collective-permute-start | bytes 786440 | tf_op jit(solution)/shard_map/ppermute | solution.py:542
  348.7 18.4 %collective-permute-start.51 = (bf16[544,512]{1,0:T(8,128)(2,1)S(1)}, bf16[544,512]{1,0:T(8,128)(2,1)S(1)}, u32[]{:S(2)}, u32[]{:S(2)}) collective-permute-start(bf16[544,512]{1,0:T(8,128)(2,1)S(1)} %broadcast_select_fusion), channel_id=1, source_target_pairs={{0,8},{8,0},{16,24},{24,16},{1,9},{9,1},{17,25},{25,17},{2,10},{10... | collective-permute-start | bytes 1671176 | tf_op jit(solution)/shard_map/ppermute | solution.py:542
  348.9 13.3 %collective-permute-start.50 = (bf16[256,512]{1,0:T(8,128)(2,1)S(1)}, bf16[256,512]{1,0:T(8,128)(2,1)S(1)}, u32[]{:S(2)}, u32[]{:S(2)}) collective-permute-start(bf16[256,512]{1,0:T(8,128)(2,1)S(1)} %add_convert_fusion.12), channel_id=1, source_target_pairs={{0,16},{8,24},{16,0},{24,8},{1,17},{9,25},{17,1},{25,9},{2,18},{10... | collective-permute-start | bytes 786440 | tf_op jit(solution)/shard_map/ppermute | solution.py:544
  356.7 38.2 %collective-permute-start.48 = (bf16[1024,512]{1,0:T(8,128)(2,1)S(1)}, bf16[1024,512]{1,0:T(8,128)(2,1)S(1)}, u32[]{:S(2)}, u32[]{:S(2)}) collective-permute-start(bf16[1024,512]{1,0:T(8,128)(2,1)S(1)} %get-tuple-element.293), channel_id=1, source_target_pairs={{0,1},{1,0},{2,3},{3,2},{4,5},{5,4},{6,7},{7,6},{8,9},{9,8},{10,11... | collective-permute-start | bytes 3145736 | tf_op jit(solution)/shard_map/ppermute | solution.py:29
  367.3 14.0 %collective-permute-start.52 = (bf16[512,512]{1,0:T(8,128)(2,1)S(1)}, bf16[512,512]{1,0:T(8,128)(2,1)S(1)}, u32[]{:S(2)}, u32[]{:S(2)}) collective-permute-start(bf16[512,512]{1,0:T(8,128)(2,1)S(1)} %maximum_select_fusion.3), channel_id=1, source_target_pairs={{0,8},{8,0},{16,24},{24,16},{1,9},{9,1},{17,25},{25,17},{2,10},{10... | collective-permute-start | bytes 1572872 | tf_op jit(solution)/shard_map/ppermute | solution.py:544
  367.7 12.8 %collective-permute-start.53 = (bf16[272,512]{1,0:T(8,128)(2,1)S(1)}, bf16[272,512]{1,0:T(8,128)(2,1)S(1)}, u32[]{:S(2)}, u32[]{:S(2)}) collective-permute-start(bf16[272,512]{1,0:T(8,128)(2,1)S(1)} %broadcast_select_fusion.1), channel_id=1, source_target_pairs={{0,16},{8,24},{16,0},{24,8},{1,17},{9,25},{17,1},{25,9},{2,18},{10... | collective-permute-start | bytes 835592 | tf_op jit(solution)/shard_map/ppermute | solution.py:542
  391.4 17.1 %collective-permute-start.55 = (bf16[544,512]{1,0:T(8,128)(2,1)S(1)}, bf16[544,512]{1,0:T(8,128)(2,1)S(1)}, u32[]{:S(2)}, u32[]{:S(2)}) collective-permute-start(bf16[544,512]{1,0:T(8,128)(2,1)S(1)} %maximum_select_fusion.2), channel_id=1, source_target_pairs={{0,8},{8,0},{16,24},{24,16},{1,9},{9,1},{17,25},{25,17},{2,10},{10... | collective-permute-start | bytes 1671176 | tf_op jit(solution)/shard_map/ppermute | solution.py:544
  395.7 11.2 %collective-permute-start.49 = (bf16[1024,256]{1,0:T(8,128)(2,1)S(1)}, bf16[1024,256]{1,0:T(8,128)(2,1)S(1)}, u32[]{:S(2)}, u32[]{:S(2)}) collective-permute-start(bf16[1024,256]{1,0:T(8,128)(2,1)S(1)} %get-tuple-element.295), channel_id=1, source_target_pairs={{0,2},{1,3},{2,0},{3,1},{4,6},{5,7},{6,4},{7,5},{8,10},{9,11},{10,... | collective-permute-start | bytes 1572872 | tf_op jit(solution)/shard_map/ppermute | solution.py:34
  (129 other events, 887.9 us)
Sparse Core Ops, SparseCore 0:
  244.0 52.5 all-reduce.4
